TPU v7x, 256 devices: a whole 4x4x8 slice. The times are simulated.
256 devices in a mesh: gx: 4 (over y), gy: 16 (over z, x_lo), gz: 4 (over x_hi, core).
Axes of the slice: x: 4 (x_hi: 2, x_lo: 2; x = x_hi * 2 + x_lo), y: 4, z: 8, core: 2. Of those that a mesh axis runs over, the one named last changes fastest.
Arguments:
- source_field: float32 [16, 3, 2, 16, 64, 512], P(None, None, None, 'gx', 'gy', 'gz'), may hold values from -15 to 15
- receiver_tensor: bfloat16 [12, 16, 6, 2, 16, 64, 512], P(None, None, None, None, 'gx', 'gy', 'gz'), may hold values from -6 to 6
- metric_ids: int32 [16, 64, 512], P('gx', 'gy', 'gz'), may hold values from 0 to 7
- metric_table: float32 [8, 3], replicated, may hold values from 0.5 to 2
- observed: float32 [2, 384, 16], P(None, 'gz'), may hold values from -6 to 6
- receiver_index: int32 [384], P('gz'), may hold values from 0 to 11
- bin_ids: int32 [384, 16], P('gz'), may hold values from 0 to 15
- window: int32 [384, 16], P('gz'), may hold values 0 or 1
Outputs:
- model_update: float32 [16, 64, 512], P('gx', 'gy', 'gz')
- direction_field: float32 [16, 64, 512], P('gx', 'gy', 'gz')
- data_vector: float32 [2, 384, 16], P(None, 'gz')
All inputs are finite; a program needn't handle non-finite values. No bound on the sum of `window` on one device may be relied on, other than what follows from the above.
Results may differ from a plain program's by a relative error of at most 0.0003.
Values sent between devices are 32-bit elements; how exact they have to be, the bound alone decides.
No kernel may reach another device: no remote copies, remote signals or barrier semaphores. Data moves between devices by JAX's collectives and lax.ppermute only.
A program may use at most 64 MiB of HBM per device.

v0:
```python
import math

import jax
import jax.numpy as jnp
from jax import lax
from jax.sharding import PartitionSpec as P

ITERS = 2


epsilon = 1e-06


def with_halo(value, sides, width):
    for axis, dim in sides:
        count, length = (lax.axis_size(axis), value.shape[dim])
        up = [(i, (i + 1) % count) for i in range(count - 1)]
        down = [(j, i) for i, j in up]
        last = lax.slice_in_dim(value, length - width, length, axis=dim)
        leading = lax.slice_in_dim(value, 0, width, axis=dim)
        before = lax.ppermute(last, axis, up)
        after = lax.ppermute(leading, axis, down)
        value = jnp.concatenate([before, value, after], axis=dim)
    return value


def derivative(padded, axis_dim):
    length = padded.shape[axis_dim] - 4

    def shifted(start):
        return lax.slice_in_dim(padded, start, start + length, axis=axis_dim)

    return (8.0 * (shifted(3) - shifted(1)) - (shifted(4) - shifted(0))) / 12.0


def metric_scales(metric_ids, metric_table):
    levels = jnp.arange(metric_table.shape[0], dtype=jnp.int32)
    onehot = (metric_ids[None] == levels[:, None, None, None]).astype(jnp.float32)
    return jnp.einsum("mxyz,mp->pxyz", onehot, metric_table, precision=lax.Precision.HIGHEST)


def strain_from(along_x, along_y, along_z, scales):
    grads = [scales[0] * along_x, scales[1] * along_y, scales[2] * along_z]
    comps = [
        grads[0][:, 0],
        grads[1][:, 1],
        grads[2][:, 2],
        0.5 * (grads[1][:, 2] + grads[2][:, 1]),
        0.5 * (grads[0][:, 2] + grads[2][:, 0]),
        0.5 * (grads[0][:, 1] + grads[1][:, 0]),
    ]
    return jnp.stack(comps, axis=1)


def kernel_of(receiver, strain):
    weights = jnp.array([1.0, 1.0, 1.0, 2.0, 2.0, 2.0], jnp.float32)[:, None, None, None]
    rec_re = jnp.take(receiver, 0, axis=-4).astype(jnp.float32)
    rec_im = jnp.take(receiver, 1, axis=-4).astype(jnp.float32)
    src_re = jnp.take(strain, 0, axis=-4)
    src_im = jnp.take(strain, 1, axis=-4)
    real_part = jnp.sum(weights * (rec_re * src_re - rec_im * src_im), axis=-4)
    imag_part = jnp.sum(weights * (rec_re * src_im + rec_im * src_re), axis=-4)
    return jnp.stack([real_part, imag_part], axis=-4)


def select_data(synth, onerec, onebin, window_mask):
    picked = jnp.einsum("ir,rbk->kib", onerec, synth, precision=lax.Precision.HIGHEST)
    return jnp.einsum("kib,ifb->kif", picked, onebin, precision=lax.Precision.HIGHEST) * window_mask


def spread_data(data, onerec, onebin, window_mask):
    summed = jnp.einsum("kif,ifb->kib", data * window_mask, onebin, precision=lax.Precision.HIGHEST)
    return jnp.einsum("kib,ir->rbk", summed, onerec, precision=lax.Precision.HIGHEST)


def norm_of(total):
    return jnp.sqrt(total + epsilon)


def rotation(rho_bar, phi_bar, beta_val, alpha_val):
    rho_new = jnp.sqrt(rho_bar * rho_bar + beta_val * beta_val)
    cosine = rho_bar / rho_new
    sine_val = beta_val / rho_new
    theta_val = sine_val * alpha_val
    return (rho_new, -cosine * alpha_val, cosine * phi_bar, sine_val * phi_bar, theta_val)


def per_device(
    source_field,
    receiver_tensor,
    metric_ids,
    metric_table,
    observed,
    receiver_index,
    bin_ids,
    window,
):
    padded = with_halo(source_field, (("gx", 3), ("gy", 4), ("gz", 5)), 2)
    along_x = derivative(padded[:, :, :, :, 2:-2, 2:-2], 3)
    along_y = derivative(padded[:, :, :, 2:-2, :, 2:-2], 4)
    along_z = derivative(padded[:, :, :, 2:-2, 2:-2, :], 5)
    strain = strain_from(along_x, along_y, along_z, metric_scales(metric_ids, metric_table))
    kernel = kernel_of(receiver_tensor, strain)
    tensors = receiver_tensor.shape[0]
    bins = source_field.shape[0]
    onerec = (receiver_index[:, None] == jnp.arange(tensors, dtype=jnp.int32)[None]).astype(
        jnp.float32
    )
    onebin = (bin_ids[:, :, None] == jnp.arange(bins, dtype=jnp.int32)[None, None]).astype(
        jnp.float32
    )
    window_mask = window.astype(jnp.float32)
    total_cells = (
        source_field.shape[3]
        * source_field.shape[4]
        * source_field.shape[5]
        * lax.axis_size("gx")
        * lax.axis_size("gy")
        * lax.axis_size("gz")
    )
    data_count = 2 * observed.shape[1] * observed.shape[2] * lax.axis_size("gz")

    def local_adjoint(spread):
        return jnp.einsum("rbk,rbkxyz->xyz", spread, kernel, precision=lax.Precision.HIGHEST)

    rhs = observed * window_mask

    def data_norm(data_raw):
        return norm_of(lax.psum(jnp.sum(data_raw * data_raw), "gz"))

    def model_norm(model_raw):
        return norm_of(lax.psum(jnp.sum(model_raw * model_raw), ("gx", "gy", "gz")))

    def adjoint(data_vec):
        spread = lax.psum(spread_data(data_vec, onerec, onebin, window_mask), "gz")
        return local_adjoint(spread)

    beta_val = data_norm(rhs)
    data_vec = rhs / beta_val
    beta_first = beta_val
    model_raw = adjoint(data_vec)
    alpha_val = model_norm(model_raw)
    model_vec = model_raw / alpha_val
    alpha_first = alpha_val
    search = model_vec
    solution = jnp.zeros_like(model_vec)
    phi_bar = beta_val
    rho_bar = alpha_val
    for iteration in range(ITERS):
        synth = lax.psum(
            jnp.einsum("rbkxyz,xyz->rbk", kernel, model_vec, precision=lax.Precision.HIGHEST),
            ("gx", "gy", "gz"),
        )
        data_raw = select_data(synth, onerec, onebin, window_mask) - alpha_val * data_vec
        beta_val = data_norm(data_raw)
        data_vec = data_raw / beta_val
        model_raw = adjoint(data_vec) - beta_val * model_vec
        alpha_val = model_norm(model_raw)
        model_vec = model_raw / alpha_val
        rho_new, rho_bar, phi_val, phi_bar, theta_val = rotation(
            rho_bar, phi_bar, beta_val, alpha_val
        )
        solution = solution + phi_val / rho_new * search
        search = model_vec - theta_val / rho_new * search
    cell_scale = math.sqrt(total_cells)
    model_update = solution * alpha_first * cell_scale / beta_first
    direction_field = model_vec * cell_scale
    data_vector = data_vec * math.sqrt(data_count)
    return (model_update, direction_field, data_vector)


def solution(mesh):
    return jax.shard_map(
        per_device,
        mesh=mesh,
        in_specs=(
            P(None, None, None, "gx", "gy", "gz"),
            P(None, None, None, None, "gx", "gy", "gz"),
            P("gx", "gy", "gz"),
            P(),
            P(None, "gz", None),
            P("gz"),
            P("gz", None),
            P("gz", None),
        ),
        out_specs=(P("gx", "gy", "gz"), P("gx", "gy", "gz"), P(None, "gz", None)),
        check_vma=False,
    )
```

profile of v0, /device:TPU:1, one launch (start us, length us, event | category | flops | bytes accessed | tf_op | source)
XLA Modules:
  0.0 590.1 jit_solution(3377264568492168721)
XLA Ops:
  3.6 4.7 collective-permute-start.1
  9.1 10.3 %psum.77 = f32[]{:T(128)} all-reduce(f32[]{:T(128)} %multiply_reduce_fusion.2), channel_id=1, replica_groups=mesh['gx'=4,'gy'=16,'gz'=4] {'gz'}, use_global_device_ids=true, to_apply=%region_1.2 | all-reduce | flops 1 | bytes 8 | tf_op jit(solution)/shard_map/psum | solution.py:129
  24.9 4.0 collective-permute-start.3
  30.4 40.3 %psum.78 = f32[12,16,2]{1,0,2:T(8,128)} all-reduce(f32[12,16,2]{1,0,2:T(8,128)S(1)} %convolution_bitcast_fusion.8), channel_id=1, replica_groups=mesh['gx'=4,'gy'=16,'gz'=4] {'gz'}, use_global_device_ids=true, to_apply=%region_2.3 | all-reduce | flops 384 | bytes 3072 | tf_op jit(solution)/shard_map/psum | solution.py:135
  73.8 3.8 fusion.63
  77.5 3.8 copy.100
  81.4 3.3 collective-permute-start.4
  84.7 4.5 copy.102
  89.2 4.5 collective-permute-start.5
  98.0 4.8 copy.101
  102.8 4.8 copy.103
  107.6 8.9 %fusion.24 = f32[16,3,2,4,4,128]{5,3,4,2,1,0:T(4,128)S(1)} fusion(f32[16,3,2,8,8,2]{5,3,4,2,1,0:T(8,128)} %copy.103, f32[16,3,2,8,2,128]{5,3,4,2,1,0:T(8,128)S(1)} %collective-permute-done.2, f32[16,3,2,8,2,128]{5,3,4,2,1,0:T(8,128)S(1)} %collective-permute-done.3, f32[16,3,2,2,4,128]{5,3,4,2,1,0:T(2,128)S(1)} %copy.91, ...), kind=kLoop, calls=%fused_computation.47 | loop fusion | flops 4915200 | bytes 4038656 | tf_op jit(solution)/shard_map/mul | solution.py:43
  117.9 14.4 %fusion.2 = (f32[12,16,4,4,128]{4,3,2,1,0:T(4,128)S(1)}, f32[12,16,4,4,128]{4,3,2,1,0:T(4,128)S(1)}) fusion(f32[16,6,4,4,128]{4,3,2,1,0:T(4,128)S(1)} %copy.106, f32[16,6,4,4,128]{4,3,2,1,0:T(4,128)S(1)} %copy.105, f32[6]{0:T(128)S(1)} %copy-done.17, bf16[12,16,6,2,4,4,128]{6,5,4,3,2,1,0:T(4,128)(2,1)} %param.18), kind=kLoop, calls=%fused_computation.6 | loop fusion | flops 27525120 | bytes 14155800 | tf_op jit(solution)/shard_map/reduce_sum | solution.py:61
  136.2 77.6 %psum.79 = f32[]{:T(128)} all-reduce(f32[]{:T(128)} %multiply_reduce_fusion.5), channel_id=1, replica_groups=mesh['gx'=4,'gy'=16,'gz'=4] {'gx','gy','gz'}, use_global_device_ids=true, to_apply=%region_6.11 | all-reduce | flops 1 | bytes 8 | tf_op jit(solution)/shard_map/psum | solution.py:132
  214.5 11.0 %fusion.8 = f32[1,12,16,2,1,1]{2,0,5,4,3,1:T(1,128)S(1)} fusion(f32[4,4,128,1,1,1]{2,3,1,0,5,4:T(1,128)S(1)} %bitcast.106, f32[12,16,2,4,4,128]{5,4,3,1,0,2:T(4,128)S(1)} %pad_maximum_fusion.1), kind=kOutput, calls=%fused_computation.14 | convolution fusion | flops 9437184 | bytes 3155456 | tf_op jit(solution)/shard_map/rbkxyz,xyz->rbk/dot_general | solution.py:151
  225.6 73.5 %psum.80 = f32[12,16,2]{0,1,2:T(8,128)S(1)} all-reduce(f32[12,16,2]{0,1,2:T(8,128)S(1)} %bitcast.101), channel_id=1, replica_groups=mesh['gx'=4,'gy'=16,'gz'=4] {'gx','gy','gz'}, use_global_device_ids=true, to_apply=%region_7.12 | all-reduce | flops 384 | bytes 3072 | tf_op jit(solution)/shard_map/psum | solution.py:150
  300.9 7.8 %psum.81 = f32[]{:T(128)} all-reduce(f32[]{:T(128)} %get-tuple-element.64), channel_id=1, replica_groups=mesh['gx'=4,'gy'=16,'gz'=4] {'gz'}, use_global_device_ids=true, to_apply=%region_9.14 | all-reduce | flops 1 | bytes 8 | tf_op jit(solution)/shard_map/psum | solution.py:129
  310.4 12.8 %psum.82 = f32[12,16,2]{1,0,2:T(8,128)S(1)} all-reduce(f32[12,16,2]{1,0,2:T(8,128)S(1)} %convolution_bitcast_fusion.6), channel_id=1, replica_groups=mesh['gx'=4,'gy'=16,'gz'=4] {'gz'}, use_global_device_ids=true, to_apply=%region_10.15 | all-reduce | flops 384 | bytes 3072 | tf_op jit(solution)/shard_map/psum | solution.py:135
  326.4 74.5 %psum.83 = f32[]{:T(128)} all-reduce(f32[]{:T(128)} %multiply_reduce_fusion.4), channel_id=1, replica_groups=mesh['gx'=4,'gy'=16,'gz'=4] {'gx','gy','gz'}, use_global_device_ids=true, to_apply=%region_12.17 | all-reduce | flops 1 | bytes 8 | tf_op jit(solution)/shard_map/psum | solution.py:132
  401.6 11.0 %fusion.6 = f32[1,12,16,2,1,1]{2,0,5,4,3,1:T(1,128)S(1)} fusion(f32[4,4,128,1,1,1]{2,3,1,0,5,4:T(1,128)S(1)} %bitcast.94, f32[12,16,2,4,4,128]{5,4,3,1,0,2:T(4,128)S(1)} %pad_maximum_fusion.1), kind=kOutput, calls=%fused_computation.12 | convolution fusion | flops 9437184 | bytes 3155456 | tf_op jit(solution)/shard_map/rbkxyz,xyz->rbk/dot_general | solution.py:151
  412.7 73.5 %psum.84 = f32[12,16,2]{0,1,2:T(8,128)S(1)} all-reduce(f32[12,16,2]{0,1,2:T(8,128)S(1)} %bitcast.102), channel_id=1, replica_groups=mesh['gx'=4,'gy'=16,'gz'=4] {'gx','gy','gz'}, use_global_device_ids=true, to_apply=%region_13.18 | all-reduce | flops 384 | bytes 3072 | tf_op jit(solution)/shard_map/psum | solution.py:150
  487.9 7.8 %psum.85 = f32[]{:T(128)} all-reduce(f32[]{:T(128)} %get-tuple-element.62), channel_id=1, replica_groups=mesh['gx'=4,'gy'=16,'gz'=4] {'gz'}, use_global_device_ids=true, to_apply=%region_15.20 | all-reduce | flops 1 | bytes 8 | tf_op jit(solution)/shard_map/psum | solution.py:129
  498.1 13.0 %psum.86 = f32[12,16,2]{1,0,2:T(8,128)S(1)} all-reduce(f32[12,16,2]{1,0,2:T(8,128)S(1)} %convolution_bitcast_fusion.4), channel_id=1, replica_groups=mesh['gx'=4,'gy'=16,'gz'=4] {'gz'}, use_global_device_ids=true, to_apply=%region_16.21 | all-reduce | flops 384 | bytes 3072 | tf_op jit(solution)/shard_map/psum | solution.py:135
  514.3 74.2 %psum.87 = f32[]{:T(128)} all-reduce(f32[]{:T(128)} %multiply_reduce_fusion.3), channel_id=1, replica_groups=mesh['gx'=4,'gy'=16,'gz'=4] {'gx','gy','gz'}, use_global_device_ids=true, to_apply=%region_18.23 | all-reduce | flops 1 | bytes 8 | tf_op jit(solution)/shard_map/psum | solution.py:132
  (106 shorter events, 35.2 us)
Async XLA Ops:
  0.6 19.7 %copy-start = (f32[8,3]{0,1:T(4,128)S(1)}, f32[8,3]{0,1:T(4,128)}, u32[]{:S(2)}) copy-start(f32[8,3]{0,1:T(4,128)} %param.20) | copy-start | bytes 292
  0.6 8.2 %copy-start.1 = (f32[16,3,2,4,4,128]{5,4,3,2,1,0:T(4,128)S(1)}, f32[16,3,2,4,4,128]{5,4,3,2,1,0:T(4,128)}, u32[]{:S(2)}) copy-start(f32[16,3,2,4,4,128]{5,4,3,2,1,0:T(4,128)} %param.17) | copy-start | bytes 2359300
  0.7 7.6 %copy-start.15 = (s32[96,16]{0,1:T(8,128)S(1)}, s32[96,16]{0,1:T(8,128)}, u32[]{:S(2)}) copy-start(s32[96,16]{0,1:T(8,128)} %param.24) | copy-start | bytes 18436
  0.7 7.6 %copy-start.7 = (f32[2,96,16]{1,2,0:T(8,128)S(1)}, f32[2,96,16]{1,2,0:T(8,128)}, u32[]{:S(2)}) copy-start(f32[2,96,16]{1,2,0:T(8,128)} %param.21) | copy-start | bytes 36868
  0.7 19.5 %copy-start.14 = (s32[96,16]{0,1:T(8,128)S(1)}, s32[96,16]{0,1:T(8,128)}, u32[]{:S(2)}) copy-start(s32[96,16]{0,1:T(8,128)} %param.23) | copy-start | bytes 18436
  0.7 19.6 %copy-start.16 = (s32[4,4,128]{2,1,0:T(4,128)S(1)}, s32[4,4,128]{2,1,0:T(4,128)}, u32[]{:S(2)}) copy-start(s32[4,4,128]{2,1,0:T(4,128)} %param.19) | copy-start | bytes 24580
  2.1 19.0 %collective-permute-start = (f32[16,3,2,2,4,128]{5,0,4,3,2,1:T(8,128)S(1)}, f32[16,3,2,2,4,128]{5,0,4,3,2,1:T(8,128)S(1)}, u32[]{:S(2)}, u32[]{:S(2)}) collective-permute-start(f32[16,3,2,2,4,128]{5,0,4,3,2,1:T(8,128)S(1)} %copy.129), channel_id=1, source_target_pairs={{64,0},{128,64},{192,128},{65,1},{129,65},{193,129},{66,2},{130,66... | collective-permute-start | bytes 1179656 | tf_op jit(solution)/shard_map/ppermute | solution.py:22
  3.6 17.9 %collective-permute-start.1 = (f32[16,3,2,2,4,128]{5,0,4,3,2,1:T(8,128)S(1)}, f32[16,3,2,2,4,128]{5,0,4,3,2,1:T(8,128)S(1)}, u32[]{:S(2)}, u32[]{:S(2)}) collective-permute-start(f32[16,3,2,2,4,128]{5,0,4,3,2,1:T(8,128)S(1)} %copy.130), channel_id=1, source_target_pairs={{0,64},{64,128},{128,192},{1,65},{65,129},{129,193},{2,66},{66,130... | collective-permute-start | bytes 1179656 | tf_op jit(solution)/shard_map/ppermute | solution.py:21
  20.3 3.4 copy-start.10
  21.7 8.5 %copy-start.13 = (s32[96]{0:T(128)S(1)}, s32[96]{0:T(128)}, u32[]{:S(2)}) copy-start(s32[96]{0:T(128)} %param.22) | copy-start | bytes 1156
  23.7 49.3 %collective-permute-start.2 = (f32[16,3,2,8,2,128]{5,3,4,2,1,0:T(8,128)}, f32[16,3,2,8,2,128]{5,3,4,2,1,0:T(8,128)S(1)}, u32[]{:S(2)}, u32[]{:S(2)}) collective-permute-start(f32[16,3,2,8,2,128]{5,3,4,2,1,0:T(8,128)} %get-tuple-element.70), channel_id=1, source_target_pairs={{4,0},{8,4},{12,8},{16,12},{20,16},{24,20},{28,24},{32,28},{36,32}... | collective-permute-start | bytes 2359304 | tf_op jit(solution)/shard_map/ppermute | solution.py:22
  24.9 48.1 %collective-permute-start.3 = (f32[16,3,2,8,2,128]{5,3,4,2,1,0:T(8,128)}, f32[16,3,2,8,2,128]{5,3,4,2,1,0:T(8,128)S(1)}, u32[]{:S(2)}, u32[]{:S(2)}) collective-permute-start(f32[16,3,2,8,2,128]{5,3,4,2,1,0:T(8,128)} %get-tuple-element.71), channel_id=1, source_target_pairs={{0,4},{4,8},{8,12},{12,16},{16,20},{20,24},{24,28},{28,32},{32,36}... | collective-permute-start | bytes 2359304 | tf_op jit(solution)/shard_map/ppermute | solution.py:21
  72.1 1.0 copy-start.2
  81.4 16.7 %collective-permute-start.4 = (f32[16,3,2,8,8,2]{0,4,5,3,2,1:T(8,128)S(1)}, f32[16,3,2,8,8,2]{0,4,5,3,2,1:T(8,128)}, u32[]{:S(2)}, u32[]{:S(2)}) collective-permute-start(f32[16,3,2,8,8,2]{0,4,5,3,2,1:T(8,128)S(1)} %copy.100), channel_id=1, source_target_pairs={{1,0},{2,1},{3,2},{5,4},{6,5},{7,6},{9,8},{10,9},{11,10},{13,12},{... | collective-permute-start | bytes 147464 | tf_op jit(solution)/shard_map/ppermute | solution.py:22
  89.2 13.6 %collective-permute-start.5 = (f32[16,3,2,8,8,2]{0,4,5,3,2,1:T(8,128)}, f32[16,3,2,8,8,2]{0,4,5,3,2,1:T(8,128)}, u32[]{:S(2)}, u32[]{:S(2)}) collective-permute-start(f32[16,3,2,8,8,2]{0,4,5,3,2,1:T(8,128)} %copy.102), channel_id=1, source_target_pairs={{0,1},{1,2},{2,3},{4,5},{5,6},{6,7},{8,9},{9,10},{10,11},{12,13},{... | collective-permute-start | bytes 147464 | tf_op jit(solution)/shard_map/ppermute | solution.py:21
  96.3 1.0 copy-start.4
  98.0 9.6 %copy-start.12 = (f32[4,4,128]{2,0,1:T(4,128)S(1)}, f32[4,4,128]{2,0,1:T(4,128)}, u32[]{:S(2)}) copy-start(f32[4,4,128]{2,0,1:T(4,128)} %copy.104) | copy-start | bytes 24580
  107.6 8.9 %copy-start.6 = (f32[16,6,2,4,4,128]{5,3,4,2,1,0:T(4,128)S(1)}, f32[16,6,2,4,4,128]{5,3,4,2,1,0:T(4,128)}, u32[]{:S(2)}) copy-start(f32[16,6,2,4,4,128]{5,3,4,2,1,0:T(4,128)} %slice_dynamic-update-slice_fusion.1) | copy-start | bytes 4718596
  107.6 9.0 %copy-start.5 = (f32[16,3,2,4,4,128]{5,3,4,2,1,0:T(4,128)S(1)}, f32[16,3,2,4,4,128]{5,3,4,2,1,0:T(4,128)}, u32[]{:S(2)}) copy-start(f32[16,3,2,4,4,128]{5,3,4,2,1,0:T(4,128)} %copy-done.4) | copy-start | bytes 2359300
  107.6 9.1 %copy-start.3 = (f32[16,3,2,4,4,128]{5,3,4,2,1,0:T(4,128)S(1)}, f32[16,3,2,4,4,128]{5,3,4,2,1,0:T(4,128)}, u32[]{:S(2)}) copy-start(f32[16,3,2,4,4,128]{5,3,4,2,1,0:T(4,128)} %copy-done.2) | copy-start | bytes 2359300
  117.0 0.9 copy-start.17
  132.2 0.8 copy-start.9
  133.0 166.3 %copy-start.11 = (s32[96,16]{1,0:T(8,128)S(1)}, s32[96,16]{1,0:T(8,128)}, u32[]{:S(2)}) copy-start(s32[96,16]{1,0:T(8,128)} %copy-done.10) | copy-start | bytes 18436
  133.0 167.2 %copy-start.8 = (f32[2,96,16]{1,2,0:T(8,128)S(1)}, f32[2,96,16]{1,2,0:T(8,128)}, u32[]{:S(2)}) copy-start(f32[2,96,16]{1,2,0:T(8,128)} %param.21) | copy-start | bytes 36868
where the time goes:
time: 598 us; the launch traced here: 590 us
  blocking collectives  465 us (78%)
  other arithmetic  34.5 us (6%)
  matrix products  33.8 us (6%)
  local copies, waits for them, and re-layouts  31.2 us (5%)
  starting transfers between devices  19.2 us (3%)
    psum x3, blocking collectives, model_norm(): return norm_of(lax.psum(jnp.sum(model_raw * model_raw), ('gx', 'gy', 'gz')))  226 us
    psum x2, blocking collectives, per_device(): lax.psum(jnp.einsum('rbkxyz,xyz->rbk', kernel, model_vec, precision=lax.P...  147 us
    psum x3, blocking collectives, adjoint(): spread = lax.psum(spread_data(data_vec, onerec, onebin, window_mask), 'gz')  66.2 us
    psum x3, blocking collectives, data_norm(): return norm_of(lax.psum(jnp.sum(data_raw * data_raw), 'gz'))  25.9 us
    dot_general x2, matrix products, per_device(): jnp.einsum('rbkxyz,xyz->rbk', kernel, model_vec, precision=lax.Precision....  22.1 us
    reduce_sum x1, other arithmetic, kernel_of(): real_part = jnp.sum(weights * (rec_re * src_re - rec_im * src_im), axis=-4)  14.4 us
    ppermute x3, starting transfers between devices, with_halo(): before = lax.ppermute(last, axis, up)  13.3 us
    mul x4, other arithmetic, strain_from(): grads = [scales[0] * along_x, scales[1] * along_y, scales[2] * along_z]  12.8 us
  transfers between devices with their start and end apart: 6, of which 0 were waited for; matrix products, arithmetic and copies ran while one was open for 3% of the time, Pallas kernels for 0%

commit v1 on v0

v1 whole, which is shorter than its diff:
```python
import functools
import math

import jax
import jax.numpy as jnp
from jax import lax
from jax.experimental import pallas as pl
from jax.experimental.pallas import tpu as pltpu
from jax.sharding import Mesh, PartitionSpec as P

ITERS = 2
EPSILON = 1e-06
F32 = jnp.float32
BF16 = jnp.bfloat16

AXES = ("y", "z", "xlo", "xhi", "core")
SIZES = {"y": 4, "z": 8, "xlo": 2, "xhi": 2, "core": 2}
GX = ("y",)
GY = ("z", "xlo")
GZ = ("xhi", "core")
PLANE = ("y", "xlo", "xhi")
VMEM_LIMIT = 40 * 1024 * 1024

BINS = 16
TENSORS = 12
FIELDS = 96
PLANES = 16
LANES = 128
ROWS = 384
BLOCKS = ((0, 0), (0, 1), (0, 2), (1, 1), (1, 2), (2, 2))


def vmem():
    return pl.BlockSpec(memory_space=pltpu.VMEM)


def smem():
    return pl.BlockSpec(memory_space=pltpu.SMEM)


def lane_ids(shape):
    return lax.broadcasted_iota(jnp.int32, shape, len(shape) - 1)


def pack_kernel(src, x_lo, x_hi, y_lo, y_hi, z_lo, z_hi):
    x_lo[...] = src[:, 0:8, :]
    x_hi[...] = src[:, 8:16, :]
    lane = lane_ids((FIELDS, LANES))
    low = jnp.zeros((FIELDS, LANES), F32)
    high = jnp.zeros((FIELDS, LANES), F32)
    for plane in range(PLANES):
        value = src[:, plane, :]
        x, y = divmod(plane, 4)
        if y < 2:
            y_lo[x * 2 + y] = value
        else:
            y_hi[x * 2 + y - 2] = value
        turned = pltpu.roll(value, 8 * plane, 1) if plane else value
        place = (lane - 8 * plane) & (LANES - 1)
        low = jnp.where(place < 2, turned, low)
        high = jnp.where(place >= LANES - 2, turned, high)
    z_lo[...] = low
    z_hi[...] = high


def pack(src):
    face = jax.ShapeDtypeStruct((FIELDS, 8, LANES), F32)
    side = jax.ShapeDtypeStruct((8, FIELDS, LANES), F32)
    ends = jax.ShapeDtypeStruct((FIELDS, LANES), F32)
    return pl.pallas_call(
        pack_kernel,
        out_shape=(face, face, side, side, ends, ends),
        in_specs=[vmem()],
        out_specs=(vmem(),) * 6,
        compiler_params=pltpu.CompilerParams(vmem_limit_bytes=VMEM_LIMIT),
        name="pack",
    )(src)


def spread(values, bins, tensor):
    parts = []
    for b in range(BINS):
        here = bins == b
        for k in range(2):
            parts.append(jnp.sum(jnp.where(here, values[k], 0.0), axis=0, keepdims=True))
    table = jnp.concatenate(parts, axis=0)
    return jnp.concatenate(
        [
            jnp.sum(jnp.where(tensor == r, table, 0.0), axis=1, keepdims=True)
            for r in range(TENSORS)
        ],
        axis=0,
    )


def pick(column, bins, tensor):
    table = jnp.zeros((2 * BINS, bins.shape[1]), F32)
    for r in range(TENSORS):
        table = jnp.where(tensor == r, column[r * 32 : (r + 1) * 32, :], table)
    out = [jnp.zeros(bins.shape, F32), jnp.zeros(bins.shape, F32)]
    for b in range(BINS):
        here = bins == b
        for k in range(2):
            out[k] = jnp.where(here, table[2 * b + k : 2 * b + k + 1, :], out[k])
    return out


def data_kernel(observed, tensor_ref, bins_ref, window, stats):
    tensor, bins = tensor_ref[...], bins_ref[...]
    mask = window[...].astype(F32)
    rhs = [observed[k] * mask for k in range(2)]
    total = spread(rhs, bins, tensor)
    count = spread([mask, mask], bins, tensor)
    mean = total / jnp.maximum(count, 1.0)
    near = pick(mean, bins, tensor)
    rest = [rhs[k] - near[k] * mask for k in range(2)]
    square = jnp.sum(rest[0] * rest[0] + rest[1] * rest[1], axis=(0, 1), keepdims=True)
    lane = lane_ids((ROWS, LANES))
    wide = jnp.where(lane == 0, total, jnp.where(lane == 1, count, square))
    for j in range(3):
        stats[:, j * LANES : (j + 1) * LANES] = wide[j * LANES : (j + 1) * LANES, :].T[:8]


def data_sums(observed, tensor, bins, window):
    return pl.pallas_call(
        data_kernel,
        out_shape=jax.ShapeDtypeStruct((8, ROWS), F32),
        in_specs=[vmem()] * 4,
        out_specs=vmem(),
        compiler_params=pltpu.CompilerParams(vmem_limit_bytes=VMEM_LIMIT),
        name="data_sums",
    )(observed, tensor, bins, window)


def merge_sums(one, two):
    total, count = one[0:1] + two[0:1], one[1:2] + two[1:2]
    gap = one[0:1] / jnp.maximum(one[1:2], 1.0) - two[0:1] / jnp.maximum(two[1:2], 1.0)
    apart = jnp.sum(one[1:2] * two[1:2] / jnp.maximum(count, 1.0) * gap * gap)
    rest = one[2:3] + two[2:3] + apart
    return jnp.concatenate([total, count, rest, jnp.zeros((5, ROWS), F32)], axis=0)


def gram_kernel(
    flags, table, src, ids, xb, xa, yb, ya, zb, za, receiver, out, cells, grads, scales
):
    step = pl.program_id(0)

    @pl.when(step == 0)
    def _():
        marks = ids[...]
        for p in range(3):
            scale = jnp.zeros((PLANES, LANES), F32)
            for m in range(8):
                scale = jnp.where(marks == m, table[m, p], scale)
            scales[p] = scale * (1.0 / 12.0)
        lane = lane_ids((FIELDS, LANES))
        halo = zb[...] * flags[4] + za[...] * flags[5]

        def at(x, y):
            if x < 0:
                return xb[:, (x + 2) * 4 + y, :] * flags[0]
            if x > 3:
                return xa[:, (x - 4) * 4 + y, :] * flags[1]
            if y < 0:
                return yb[x * 2 + y + 2] * flags[2]
            if y > 3:
                return ya[x * 2 + y - 4] * flags[3]
            return src[:, x * 4 + y, :]

        for x in range(4):
            for y in range(4):
                plane = x * 4 + y
                grads[0, :, plane, :] = 8.0 * (at(x + 1, y) - at(x - 1, y)) - (
                    at(x + 2, y) - at(x - 2, y)
                )
                grads[1, :, plane, :] = 8.0 * (at(x, y + 1) - at(x, y - 1)) - (
                    at(x, y + 2) - at(x, y - 2)
                )
                mid = at(x, y)
                ends = pltpu.roll(halo, LANES - 8 * plane, 1) if plane else halo
                later = pltpu.roll(jnp.where(lane < 1, ends, mid), LANES - 1, 1)
                sooner = pltpu.roll(jnp.where(lane >= LANES - 1, ends, mid), 1, 1)
                later_two = pltpu.roll(jnp.where(lane < 2, ends, mid), LANES - 2, 1)
                sooner_two = pltpu.roll(jnp.where(lane >= LANES - 2, ends, mid), 2, 1)
                grads[2, :, plane, :] = 8.0 * (later - sooner) - (later_two - sooner_two)

    def grad(p, q, k):
        return scales[p] * grads[p, step * 6 + q * 2 + k]

    def strain(k):
        return (
            grad(0, 0, k),
            grad(1, 1, k),
            grad(2, 2, k),
            grad(1, 2, k) + grad(2, 1, k),
            grad(0, 2, k) + grad(2, 0, k),
            grad(0, 1, k) + grad(1, 0, k),
        )

    real, imag = strain(0), strain(1)
    for r in range(TENSORS):
        re = jnp.zeros((PLANES, LANES), F32)
        im = jnp.zeros((PLANES, LANES), F32)
        for j in range(6):
            rec_re = receiver[r, 0, 2 * j].astype(F32)
            rec_im = receiver[r, 0, 2 * j + 1].astype(F32)
            re = re + (rec_re * real[j] - rec_im * imag[j])
            im = im + (rec_re * imag[j] + rec_im * real[j])
        cells[r * 32 + step * 2] = re
        cells[r * 32 + step * 2 + 1] = im

    @pl.when(step == BINS - 1)
    def _():
        total = jnp.zeros((ROWS, ROWS), F32)
        for plane in range(0, PLANES, 2):
            both = jnp.concatenate([cells[:, plane, :], cells[:, plane + 1, :]], axis=1)
            high = both.astype(BF16)
            low = (both - high.astype(F32)).astype(BF16)
            left = jnp.concatenate([high, high], axis=1)
            right = jnp.concatenate([high * BF16(0.5), low], axis=1)
            total = total + lax.dot_general(
                left, right, (((1,), (1,)), ((), ())), preferred_element_type=F32
            )

        def block(i, j):
            return total[i * LANES : (i + 1) * LANES, j * LANES : (j + 1) * LANES]

        for n, (i, j) in enumerate(BLOCKS):
            out[n * LANES : (n + 1) * LANES, :] = block(i, j) + block(j, i).T


def gram(flags, table, src, ids, halos, receiver):
    whole = lambda *shape: pl.BlockSpec(shape, lambda b: (0,) * len(shape))
    face = whole(FIELDS, 8, LANES)
    side = whole(8, FIELDS, LANES)
    ends = whole(FIELDS, LANES)
    return pl.pallas_call(
        gram_kernel,
        grid=(BINS,),
        out_shape=(
            jax.ShapeDtypeStruct((768, LANES), F32),
            jax.ShapeDtypeStruct((ROWS, PLANES, LANES), F32),
        ),
        in_specs=[
            smem(),
            smem(),
            whole(FIELDS, PLANES, LANES),
            whole(PLANES, LANES),
            face,
            face,
            side,
            side,
            ends,
            ends,
            pl.BlockSpec((TENSORS, 1, 12, PLANES, LANES), lambda b: (0, b, 0, 0, 0)),
        ],
        out_specs=(whole(768, LANES), whole(ROWS, PLANES, LANES)),
        scratch_shapes=[
            pltpu.VMEM((3, FIELDS, PLANES, LANES), F32),
            pltpu.VMEM((3, PLANES, LANES), F32),
        ],
        compiler_params=pltpu.CompilerParams(vmem_limit_bytes=VMEM_LIMIT),
        name="gram",
    )(flags, table, src, ids, *halos, receiver)


def chain_kernel(
    packed, stats, cells, observed, tensor_ref, bins_ref, window, update, direction, data, full, coef
):
    for n, (i, j) in enumerate(BLOCKS):
        tile = packed[n * LANES : (n + 1) * LANES, :]
        full[i * LANES : (i + 1) * LANES, j * LANES : (j + 1) * LANES] = tile
        if i != j:
            full[j * LANES : (j + 1) * LANES, i * LANES : (i + 1) * LANES] = tile.T
    eye = lax.broadcasted_iota(jnp.int32, (LANES, LANES), 0) == lane_ids((LANES, LANES))

    def column(row):
        return jnp.concatenate(
            [
                jnp.sum(
                    jnp.where(eye, row[:, j * LANES : (j + 1) * LANES], 0.0), axis=1, keepdims=True
                )
                for j in range(3)
            ],
            axis=0,
        )

    def product(row):
        return jnp.sum(full[...] * column(row), axis=0, keepdims=True)

    def total(row):
        return jnp.sum(row, axis=1, keepdims=True)

    def norm_of(square):
        return jnp.sqrt(square + EPSILON)

    sums, count, rest = stats[0:1, :], stats[1:2, :], stats[2:3, 0:1]
    mean = sums / jnp.maximum(count, 1.0)

    def data_norm(scale, row):
        inside = scale * mean + row
        return norm_of(scale * scale * rest + total(count * inside * inside))

    one = jnp.ones((1, 1), F32)
    row = jnp.zeros((1, ROWS), F32)
    beta = data_norm(one, row)
    beta_first = beta
    scale = one / beta
    raw = scale * sums
    image = product(raw)
    alpha = norm_of(total(raw * image))
    alpha_first = alpha
    model = raw / alpha
    search = model
    answer = jnp.zeros((1, ROWS), F32)
    phi_bar, rho_bar = beta, alpha
    for _ in range(ITERS):
        scale, row = -alpha * scale, image / alpha - alpha * row
        beta = data_norm(scale, row)
        scale, row = scale / beta, row / beta
        raw = scale * sums + count * row - beta * model
        image = product(raw)
        alpha = norm_of(total(raw * image))
        model = raw / alpha
        rho = jnp.sqrt(rho_bar * rho_bar + beta * beta)
        cosine, sine = rho_bar / rho, beta / rho
        theta = sine * alpha
        rho_bar = -cosine * alpha
        phi = cosine * phi_bar
        phi_bar = sine * phi_bar
        answer = answer + phi / rho * search
        search = model - theta / rho * search
    cell_scale = math.sqrt(PLANES * LANES * math.prod(SIZES.values()))
    coef[0] = jnp.broadcast_to(
        column(answer * (alpha_first * cell_scale / beta_first)), (ROWS, LANES)
    )
    coef[1] = jnp.broadcast_to(column(model * cell_scale), (ROWS, LANES))

    mask = window[...].astype(F32)
    size = math.sqrt(math.prod(observed.shape) * SIZES["xhi"] * SIZES["core"])
    near = pick(column(row * size), bins_ref[...], tensor_ref[...])
    for k in range(2):
        data[k] = (observed[k] * (scale * size) + near[k]) * mask

    def body(n, sums_of):
        tile = cells[n]
        return (
            sums_of[0] + coef[0, pl.ds(n, 1), :] * tile,
            sums_of[1] + coef[1, pl.ds(n, 1), :] * tile,
        )

    start = (jnp.zeros((PLANES, LANES), F32), jnp.zeros((PLANES, LANES), F32))
    first, second = lax.fori_loop(0, ROWS, body, start, unroll=16)
    update[...] = first
    direction[...] = second


def chain(packed, stats, cells, observed, tensor, bins, window):
    field = jax.ShapeDtypeStruct((PLANES, LANES), F32)
    return pl.pallas_call(
        chain_kernel,
        out_shape=(field, field, jax.ShapeDtypeStruct(observed.shape, F32)),
        in_specs=[vmem()] * 7,
        out_specs=(vmem(),) * 3,
        scratch_shapes=[pltpu.VMEM((ROWS, ROWS), F32), pltpu.VMEM((2, ROWS, LANES), F32)],
        compiler_params=pltpu.CompilerParams(vmem_limit_bytes=VMEM_LIMIT),
        name="chain",
    )(packed, stats, cells, observed, tensor, bins, window)


def shift(value, axes, step):
    count = math.prod(SIZES[a] for a in axes)
    return lax.ppermute(value, axes, [(i, (i + step) % count) for i in range(count)])


def swap(value, axis):
    return lax.ppermute(value, axis, [(0, 1), (1, 0)])


def half_scatter(value, axis):
    half = value.shape[0] // 2
    upper = lax.axis_index(axis) == 1
    low, high = value[:half], value[half:]
    return jnp.where(upper, high, low) + swap(jnp.where(upper, low, high), axis)


def half_gather(value, axis):
    upper = lax.axis_index(axis) == 1
    other = swap(value, axis)
    return jnp.where(
        upper, jnp.concatenate([other, value]), jnp.concatenate([value, other])
    )


def exchange(value, axes):
    return lax.all_to_all(value, axes, 0, 0, tiled=True)


def scatter_sum(value, axes):
    count = math.prod(SIZES[a] for a in axes)
    return jnp.sum(exchange(value.reshape(count, -1, LANES), axes), axis=0)


def whole_sum(value, axes):
    count = math.prod(SIZES[a] for a in axes)
    return jnp.sum(exchange(jnp.broadcast_to(value, (count,) + value.shape), axes), axis=0)


def gather(value, axes):
    count = math.prod(SIZES[a] for a in axes)
    return exchange(jnp.broadcast_to(value, (count,) + value.shape), axes).reshape(-1, LANES)


def reduce_all(value):
    value = half_scatter(value, "core")
    value = scatter_sum(value, PLANE)
    value = whole_sum(value, ("z",))
    value = gather(value, PLANE)
    return half_gather(value, "core")


def per_device(
    source_field,
    receiver_tensor,
    metric_ids,
    metric_table,
    observed,
    receiver_index,
    bin_ids,
    window,
):
    src = source_field.reshape(FIELDS, PLANES, LANES)
    receiver = receiver_tensor.reshape(TENSORS, BINS, 12, PLANES, LANES)
    ids = metric_ids.reshape(PLANES, LANES)
    x_lo, x_hi, y_lo, y_hi, z_lo, z_hi = pack(src)
    x_at, y_at, z_at = lax.axis_index(GX), lax.axis_index(GY), lax.axis_index(GZ)
    ends = [math.prod(SIZES[a] for a in axes) - 1 for axes in (GX, GY, GZ)]
    flags = jnp.stack(
        [x_at > 0, x_at < ends[0], y_at > 0, y_at < ends[1], z_at > 0, z_at < ends[2]]
    ).astype(F32)
    yb, ya = shift(y_hi, GY, 1), shift(y_lo, GY, -1)
    xb, xa = shift(x_hi, GX, 1), shift(x_lo, GX, -1)
    zb, za = shift(z_hi, GZ, 1), shift(z_lo, GZ, -1)

    values = observed.transpose(0, 2, 1)
    tensor = receiver_index.reshape(1, -1)
    bins, marks = bin_ids.T, window.T
    stats = data_sums(values, tensor, bins, marks)
    stats = merge_sums(stats, swap(stats, "core"))
    stats = merge_sums(stats, swap(stats, "xhi"))

    packed, cells = gram(
        flags, metric_table, src, ids, (xb, xa, yb, ya, zb, za), receiver
    )
    packed = reduce_all(packed)
    update, direction, data = chain(packed, stats, cells, values, tensor, bins, marks)
    return (
        update.reshape(metric_ids.shape),
        direction.reshape(metric_ids.shape),
        data.transpose(0, 2, 1),
    )


def solution(mesh):
    fine = Mesh(mesh.devices.reshape([SIZES[a] for a in AXES]), AXES)
    return jax.shard_map(
        per_device,
        mesh=fine,
        in_specs=(
            P(None, None, None, GX, GY, GZ),
            P(None, None, None, None, GX, GY, GZ),
            P(GX, GY, GZ),
            P(),
            P(None, GZ, None),
            P(GZ),
            P(GZ, None),
            P(GZ, None),
        ),
        out_specs=(P(GX, GY, GZ), P(GX, GY, GZ), P(None, GZ, None)),
        check_vma=False,
    )
```

time: 598 us -> 116 us (0.19); the launches traced: 590 us -> 115 us
  blocking collectives: 465 us -> 0 us
  matrix products: 33.8 us -> 0 us
  other arithmetic: 34.5 us -> 7.34 us
  Pallas kernels: 0 us -> 25.4 us
  starting transfers between devices: 19.2 us -> 43.4 us
  waiting for transfers between devices: 0.02 us -> 18.5 us
  local copies, waits for them, and re-layouts: 31.2 us -> 19.2 us
    psum x11 -> x0, blocking collectives: 465 us -> none  [the longest x3 226 us: model_norm(): return norm_of(lax.psum(jnp.sum(model_raw * model_raw), ('gx', 'gy', 'gz')))]
    dot_general x16 -> x0, matrix products: 33.8 us -> none  [the longest x2 22.1 us: per_device(): jnp.einsum('rbkxyz,xyz->rbk', kernel, model_vec, precision=lax.Precision....]
    pallas_call x0 -> x4, Pallas kernels: none -> 25.4 us  [the longest x1 21.3 us: gram(): pl.pallas_call(gram_kernel, grid=(BINS,), out_shape=(jax.ShapeDtypeStruct...]
    all_to_all x0 -> x3, starting transfers between devices: none -> 18 us  [exchange(): return lax.all_to_all(value, axes, 0, 0, tiled=True)]
    reduce_sum x7 -> x3, other arithmetic: 18.1 us -> 1.2 us  [the longest x1 1.17 us: merge_sums(): apart = jnp.sum(one[1:2] * two[1:2] / jnp.maximum(count, 1.0) * gap * gap)]
    all_to_all x0 -> x3, waiting for transfers between devices: none -> 16.2 us  [exchange(): return lax.all_to_all(value, axes, 0, 0, tiled=True)]
    slice x5 -> x0, local copies, waits for them, and re-layouts: 14.8 us -> none  [the longest x4 10.3 us: with_halo(): leading = lax.slice_in_dim(value, 0, width, axis=dim)]
    mul x8 -> x0, other arithmetic: 14 us -> none  [the longest x4 12.8 us: strain_from(): grads = [scales[0] * along_x, scales[1] * along_y, scales[2] * along_z]]
  transfers between devices with their start and end apart: 6 -> 13, of which waited for: 0 -> 8; matrix products, arithmetic and copies ran while one was open for 3% -> 8% of each run, Pallas kernels for 0% -> 0%
where the time goes in v1:
time: 116 us; the launch traced here: 115 us
  starting transfers between devices  43.4 us (37%)
  Pallas kernels  25.4 us (22%)
  local copies, waits for them, and re-layouts  19.2 us (17%)
  waiting for transfers between devices  18.5 us (16%)
  other arithmetic  7.34 us (6%)
    pallas_call x1, Pallas kernels, gram(): pl.pallas_call(gram_kernel, grid=(BINS,), out_shape=(jax.ShapeDtypeStruct...  21.3 us
    all_to_all x3, starting transfers between devices, exchange(): return lax.all_to_all(value, axes, 0, 0, tiled=True)  18 us
    unnamed x47, local copies, waits for them, and re-layouts  17.1 us
    ppermute x6, starting transfers between devices, shift(): lax.ppermute(value, axes, [(i, (i + step) % count) for i in range(count)])  16.7 us
    all_to_all x3, waiting for transfers between devices, exchange(): return lax.all_to_all(value, axes, 0, 0, tiled=True)  16.2 us
    ppermute x4, starting transfers between devices, swap(): return lax.ppermute(value, axis, [(0, 1), (1, 0)])  8.72 us
    pallas_call x1, Pallas kernels, chain(): pl.pallas_call(chain_kernel, out_shape=(field, field, jax.ShapeDtypeStruc...  3.07 us
    add x2, other arithmetic, merge_sums(): total, count = (one[0:1] + two[0:1], one[1:2] + two[1:2])  2.67 us
  transfers between devices with their start and end apart: 13, of which 8 were waited for; matrix products, arithmetic and copies ran while one was open for 8% of the time, Pallas kernels for 0%

profile of v1, /device:TPU:1, one launch (start us, length us, event | category | flops | bytes accessed | tf_op | source)
XLA Modules:
  0.0 114.6 jit_solution(6878922549547473813)
XLA Ops:
  0.6 1.1 copy-done
  2.3 2.2 %collective-permute-start = (f32[96,8,128]{2,1,0:T(8,128)S(1)}, f32[96,8,128]{2,1,0:T(8,128)S(1)}, u32[]{:S(2)}, u32[]{:S(2)}) collective-permute-start(f32[96,8,128]{2,1,0:T(8,128)S(1)} %get-tuple-element.14), channel_id=1, source_target_pairs={{0,64},{64,128},{128,192},{192,0},{1,65},{65,129},{129,193},{193,1... | collective-permute-start | bytes 1179656 | tf_op jit(solution)/shard_map/ppermute | solution.py:373
  4.5 1.5 %collective-permute-start.1 = (f32[96,8,128]{2,1,0:T(8,128)S(1)}, f32[96,8,128]{2,1,0:T(8,128)S(1)}, u32[]{:S(2)}, u32[]{:S(2)}) collective-permute-start(f32[96,8,128]{2,1,0:T(8,128)S(1)} %get-tuple-element.15), channel_id=1, source_target_pairs={{0,192},{64,0},{128,64},{192,128},{1,193},{65,1},{129,65},{193,129... | collective-permute-start | bytes 1179656 | tf_op jit(solution)/shard_map/ppermute | solution.py:373
  6.0 1.2 %collective-permute-start.2 = (f32[8,96,128]{2,1,0:T(8,128)S(1)}, f32[8,96,128]{2,1,0:T(8,128)S(1)}, u32[]{:S(2)}, u32[]{:S(2)}) collective-permute-start(f32[8,96,128]{2,1,0:T(8,128)S(1)} %get-tuple-element.16), channel_id=1, source_target_pairs={{0,4},{4,8},{8,12},{12,16},{16,20},{20,24},{24,28},{28,32},{32,36}... | collective-permute-start | bytes 1179656 | tf_op jit(solution)/shard_map/ppermute | solution.py:373
  7.2 5.3 %collective-permute-start.3 = (f32[8,96,128]{2,1,0:T(8,128)S(1)}, f32[8,96,128]{2,1,0:T(8,128)S(1)}, u32[]{:S(2)}, u32[]{:S(2)}) collective-permute-start(f32[8,96,128]{2,1,0:T(8,128)S(1)} %get-tuple-element.17), channel_id=1, source_target_pairs={{0,60},{4,0},{8,4},{12,8},{16,12},{20,16},{24,20},{28,24},{32,28},... | collective-permute-start | bytes 1179656 | tf_op jit(solution)/shard_map/ppermute | solution.py:373
  15.8 1.4 %collective-permute-start.8 = (f32[8,384]{1,0:T(8,128)S(1)}, f32[8,384]{1,0:T(8,128)S(1)}, u32[]{:S(2)}, u32[]{:S(2)}) collective-permute-start(f32[8,384]{1,0:T(8,128)S(1)} %data_sums.1), channel_id=1, source_target_pairs={{0,1},{1,0},{2,3},{3,2},{4,5},{5,4},{6,7},{7,6},{8,9},{9,8},{10,11... | collective-permute-start | bytes 36872 | tf_op jit(solution)/shard_map/ppermute | solution.py:377
  18.1 2.7 %collective-permute-start.4 = (f32[96,128]{1,0:T(8,128)S(1)}, f32[96,128]{1,0:T(8,128)S(1)}, u32[]{:S(2)}, u32[]{:S(2)}) collective-permute-start(f32[96,128]{1,0:T(8,128)S(1)} %get-tuple-element.18), channel_id=1, source_target_pairs={{0,1},{1,2},{2,3},{3,0},{4,5},{5,6},{6,7},{7,4},{8,9},{9,10},{10,1... | collective-permute-start | bytes 147464 | tf_op jit(solution)/shard_map/ppermute | solution.py:373
  21.4 1.3 %copy.12.table = f32[8,3]{1,0:T(8,128)} copy(f32[8,3]{0,1:T(4,128)} %param.11) | data formatting | bytes 192 | tf_op args[3]
  24.4 3.8 %collective-permute-start.5 = (f32[96,128]{1,0:T(8,128)S(1)}, f32[96,128]{1,0:T(8,128)S(1)}, u32[]{:S(2)}, u32[]{:S(2)}) collective-permute-start(f32[96,128]{1,0:T(8,128)S(1)} %get-tuple-element.19), channel_id=1, source_target_pairs={{0,3},{1,0},{2,1},{3,2},{4,7},{5,4},{6,5},{7,6},{8,11},{9,8},{10,9... | collective-permute-start | bytes 147464 | tf_op jit(solution)/shard_map/ppermute | solution.py:373
  28.2 1.2 %fusion.2 = (f32[]{:T(128)}, f32[1,384]{1,0:T(1,128)}) fusion(f32[8,384]{1,0:T(8,128)S(1)} %collective-permute-done.8, f32[8,384]{1,0:T(8,128)S(1)} %data_sums.1), kind=kLoop, calls=%fused_computation.11 | loop fusion | flops 4607 | bytes 7684 | tf_op jit(solution)/shard_map/reduce_sum | solution.py:138
  32.4 1.1 copy-done.1
  33.6 1.0 copy-done.3
  39.4 21.3 %gram.1 = (f32[768,128]{1,0:T(8,128)S(1)}, f32[384,16,128]{2,1,0:T(8,128)S(1)}) custom-call(f32[6]{0:T(128)S(1)} %copy-done.21, f32[8,3]{1,0:T(8,128)S(1)} %copy-done.17, f32[96,16,128]{2,1,0:T(8,128)S(1)} %bitcast.19, s32[16,128]{1,0:T(8,128)S(1)} %bitcast.26, f32[96,8,128]{2,1,0:T(8,128)S(1)} %collective-permute-done.xb, f32[96,8,128]{2,1,0:T(8,128)S(1)} %copy-done.3, ...), custom_call_target="tpu_custom_call" | custom-call | tf_op jit(solution)/shard_map/gram/pallas_call | solution.py:237
  60.8 1.4 %slice_add_fusion.5 = (f32[1,384]{1,0:T(1,128)S(1)}, f32[1,384]{1,0:T(1,128)S(1)}) fusion(f32[8,384]{1,0:T(8,128)} %copy-done.22, f32[8,384]{1,0:T(8,128)} %copy-done.16, f32[]{:T(128)} %get-tuple-element.25), kind=kLoop, calls=%fused_computation.16 | loop fusion | flops 1152 | bytes 9220 | tf_op jit(solution)/shard_map/add | solution.py:136
  62.9 5.9 %all-to-all-start = ((f32[16,24,128]{2,1,0:T(8,128)}), f32[16,24,128]{2,1,0:T(8,128)S(1)}, u32[]{:S(2)}, u32[]{:S(2)}) async-start(f32[16,24,128]{2,1,0:T(8,128)} %bitcast.9), calls=%async_computation | async-start | bytes 393216 | tf_op jit(solution)/shard_map/all_to_all | solution.py:396
  69.6 2.9 %collective-permute-start.9 = (f32[8,384]{1,0:T(8,128)S(1)}, f32[8,384]{1,0:T(8,128)S(1)}, u32[]{:S(2)}, u32[]{:S(2)}) collective-permute-start(f32[8,384]{1,0:T(8,128)S(1)} %maximum_maximum_fusion), channel_id=1, source_target_pairs={{0,2},{2,0},{1,3},{3,1},{4,6},{6,4},{5,7},{7,5},{8,10},{10,8},{9,1... | collective-permute-start | bytes 36872 | tf_op jit(solution)/shard_map/ppermute | solution.py:377
  72.5 3.5 %all-to-all-done = f32[16,24,128]{2,1,0:T(8,128)S(1)} async-done(((f32[16,24,128]{2,1,0:T(8,128)}), f32[16,24,128]{2,1,0:T(8,128)S(1)}, u32[]{:S(2)}, u32[]{:S(2)}) %all-to-all-start) | async-done | bytes 196640 | tf_op jit(solution)/shard_map/all_to_all | solution.py:396
  76.6 8.5 %all-to-all-start.1 = ((f32[8,24,128]{2,1,0:T(8,128)}), f32[8,24,128]{2,1,0:T(8,128)S(1)}, u32[]{:S(2)}, u32[]{:S(2)}) async-start(f32[8,24,128]{2,1,0:T(8,128)} %broadcast_in_dim.6), calls=%async_computation.1 | async-start | bytes 196608 | tf_op jit(solution)/shard_map/all_to_all | solution.py:396
  85.2 1.3 %slice_add_fusion.3 = (f32[1,384]{1,0:T(1,128)S(1)}, f32[]{:T(128)}, f32[1,384]{1,0:T(1,128)S(1)}) fusion(f32[1,384]{1,0:T(1,128)S(1)} %get-tuple-element.27, f32[8,384]{1,0:T(8,128)S(1)} %collective-permute-done.9, f32[1,384]{1,0:T(1,128)} %get-tuple-element.26), kind=kLoop, calls=%fused_computation.14 | loop fusion | flops 4991 | bytes 9220 | tf_op jit(solution)/shard_map/add | solution.py:136
  86.5 6.4 %all-to-all-done.1 = f32[8,24,128]{2,1,0:T(8,128)S(1)} async-done(((f32[8,24,128]{2,1,0:T(8,128)}), f32[8,24,128]{2,1,0:T(8,128)S(1)}, u32[]{:S(2)}, u32[]{:S(2)}) %all-to-all-start.1) | async-done | bytes 98336 | tf_op jit(solution)/shard_map/all_to_all | solution.py:396
  93.5 3.5 %all-to-all-start.2 = ((f32[16,24,128]{2,1,0:T(8,128)}), f32[16,24,128]{2,1,0:T(8,128)S(1)}, u32[]{:S(2)}, u32[]{:S(2)}) async-start(f32[16,24,128]{2,1,0:T(8,128)} %broadcast_in_dim.7), calls=%async_computation.2 | async-start | bytes 393216 | tf_op jit(solution)/shard_map/all_to_all | solution.py:396
  97.7 6.4 %all-to-all-done.2 = f32[16,24,128]{2,1,0:T(8,128)S(1)} async-done(((f32[16,24,128]{2,1,0:T(8,128)}), f32[16,24,128]{2,1,0:T(8,128)S(1)}, u32[]{:S(2)}, u32[]{:S(2)}) %all-to-all-start.2) | async-done | bytes 196640 | tf_op jit(solution)/shard_map/all_to_all | solution.py:396
  104.1 4.3 %collective-permute-start.7 = (f32[384,128]{1,0:T(8,128)S(1)}, f32[384,128]{1,0:T(8,128)S(1)}, u32[]{:S(2)}, u32[]{:S(2)}) collective-permute-start(f32[384,128]{1,0:T(8,128)S(1)} %bitcast.30), channel_id=1, source_target_pairs={{0,1},{1,0},{2,3},{3,2},{4,5},{5,4},{6,7},{7,6},{8,9},{9,8},{10,11... | collective-permute-start | bytes 589832 | tf_op jit(solution)/shard_map/ppermute | solution.py:377
  111.5 3.1 %chain.1 = (f32[16,128]{1,0:T(8,128)}, f32[16,128]{1,0:T(8,128)}, f32[2,16,96]{2,1,0:T(8,128)}) custom-call(f32[768,128]{1,0:T(8,128)S(1)} %maximum_select_fusion.packed, f32[8,384]{1,0:T(8,128)S(1)} %maximum_maximum_fusion.1.stats, f32[384,16,128]{2,1,0:T(8,128)S(1)} %get-tuple-element.21.cells, f32[2,16,96]{2,1,0:T(8,128)S(1)} %bitcast.21, ...), custom_call_target="tpu_custom_call" | custom-call | tf_op jit(solution)/shard_map/chain/pallas_call | solution.py:360
  (70 shorter events, 21.5 us)
Async XLA Ops:
  0.6 1.1 copy-start
  1.8 107.7 %copy-start.9 = (f32[2,96,16]{1,2,0:T(8,128)S(1)}, f32[2,96,16]{1,2,0:T(8,128)}, u32[]{:S(2)}) copy-start(f32[2,96,16]{1,2,0:T(8,128)} %param.12) | copy-start | bytes 36868
  2.3 27.9 %collective-permute-start = (f32[96,8,128]{2,1,0:T(8,128)S(1)}, f32[96,8,128]{2,1,0:T(8,128)S(1)}, u32[]{:S(2)}, u32[]{:S(2)}) collective-permute-start(f32[96,8,128]{2,1,0:T(8,128)S(1)} %get-tuple-element.14), channel_id=1, source_target_pairs={{0,64},{64,128},{128,192},{192,0},{1,65},{65,129},{129,193},{193,1... | collective-permute-start | bytes 1179656 | tf_op jit(solution)/shard_map/ppermute | solution.py:373
  4.5 25.7 %collective-permute-start.1 = (f32[96,8,128]{2,1,0:T(8,128)S(1)}, f32[96,8,128]{2,1,0:T(8,128)S(1)}, u32[]{:S(2)}, u32[]{:S(2)}) collective-permute-start(f32[96,8,128]{2,1,0:T(8,128)S(1)} %get-tuple-element.15), channel_id=1, source_target_pairs={{0,192},{64,0},{128,64},{192,128},{1,193},{65,1},{129,65},{193,129... | collective-permute-start | bytes 1179656 | tf_op jit(solution)/shard_map/ppermute | solution.py:373
  6.0 24.9 %collective-permute-start.2 = (f32[8,96,128]{2,1,0:T(8,128)S(1)}, f32[8,96,128]{2,1,0:T(8,128)S(1)}, u32[]{:S(2)}, u32[]{:S(2)}) collective-permute-start(f32[8,96,128]{2,1,0:T(8,128)S(1)} %get-tuple-element.16), channel_id=1, source_target_pairs={{0,4},{4,8},{8,12},{12,16},{16,20},{20,24},{24,28},{28,32},{32,36}... | collective-permute-start | bytes 1179656 | tf_op jit(solution)/shard_map/ppermute | solution.py:373
  7.2 24.5 %collective-permute-start.3 = (f32[8,96,128]{2,1,0:T(8,128)S(1)}, f32[8,96,128]{2,1,0:T(8,128)S(1)}, u32[]{:S(2)}, u32[]{:S(2)}) collective-permute-start(f32[8,96,128]{2,1,0:T(8,128)S(1)} %get-tuple-element.17), channel_id=1, source_target_pairs={{0,60},{4,0},{8,4},{12,8},{16,12},{20,16},{24,20},{28,24},{32,28},... | collective-permute-start | bytes 1179656 | tf_op jit(solution)/shard_map/ppermute | solution.py:373
  15.8 16.6 %copy-start.16 = (f32[8,384]{1,0:T(8,128)}, f32[8,384]{1,0:T(8,128)S(1)}, u32[]{:S(2)}) copy-start(f32[8,384]{1,0:T(8,128)S(1)} %data_sums.1) | copy-start | bytes 36868
  15.8 2.3 %collective-permute-start.8 = (f32[8,384]{1,0:T(8,128)S(1)}, f32[8,384]{1,0:T(8,128)S(1)}, u32[]{:S(2)}, u32[]{:S(2)}) collective-permute-start(f32[8,384]{1,0:T(8,128)S(1)} %data_sums.1), channel_id=1, source_target_pairs={{0,1},{1,0},{2,3},{3,2},{4,5},{5,4},{6,7},{7,6},{8,9},{9,8},{10,11... | collective-permute-start | bytes 36872 | tf_op jit(solution)/shard_map/ppermute | solution.py:377
  18.1 14.3 %copy-start.22 = (f32[8,384]{1,0:T(8,128)}, f32[8,384]{1,0:T(8,128)S(1)}, u32[]{:S(2)}) copy-start(f32[8,384]{1,0:T(8,128)S(1)} %collective-permute-done.8) | copy-start | bytes 36868
  18.1 5.7 %collective-permute-start.4 = (f32[96,128]{1,0:T(8,128)S(1)}, f32[96,128]{1,0:T(8,128)S(1)}, u32[]{:S(2)}, u32[]{:S(2)}) collective-permute-start(f32[96,128]{1,0:T(8,128)S(1)} %get-tuple-element.18), channel_id=1, source_target_pairs={{0,1},{1,2},{2,3},{3,0},{4,5},{5,6},{6,7},{7,4},{8,9},{9,10},{10,1... | collective-permute-start | bytes 147464 | tf_op jit(solution)/shard_map/ppermute | solution.py:373
  24.4 5.8 %collective-permute-start.5 = (f32[96,128]{1,0:T(8,128)S(1)}, f32[96,128]{1,0:T(8,128)S(1)}, u32[]{:S(2)}, u32[]{:S(2)}) collective-permute-start(f32[96,128]{1,0:T(8,128)S(1)} %get-tuple-element.19), channel_id=1, source_target_pairs={{0,3},{1,0},{2,1},{3,2},{4,7},{5,4},{6,5},{7,6},{8,11},{9,8},{10,9... | collective-permute-start | bytes 147464 | tf_op jit(solution)/shard_map/ppermute | solution.py:373
  30.9 0.8 copy-start.4
  31.7 0.8 copy-start.6
  32.4 1.1 copy-start.1
  33.6 1.0 copy-start.3
  34.6 1.0 copy-start.5
  35.6 1.0 copy-start.7
  36.6 0.8 copy-start.11
  60.7 1.5 %collective-permute-start.6 = (f32[384,128]{1,0:T(8,128)S(1)}, f32[384,128]{1,0:T(8,128)S(1)}, u32[]{:S(2)}, u32[]{:S(2)}) collective-permute-start(f32[384,128]{1,0:T(8,128)S(1)} %slice_select_fusion), channel_id=1, source_target_pairs={{0,1},{1,0},{2,3},{3,2},{4,5},{5,4},{6,7},{7,6},{8,9},{9,8},{10,11... | collective-permute-start | bytes 589832 | tf_op jit(solution)/shard_map/ppermute | solution.py:377
  62.9 13.1 %all-to-all-start = ((f32[16,24,128]{2,1,0:T(8,128)}), f32[16,24,128]{2,1,0:T(8,128)S(1)}, u32[]{:S(2)}, u32[]{:S(2)}) async-start(f32[16,24,128]{2,1,0:T(8,128)} %bitcast.9), calls=%async_computation | async-start | bytes 393216 | tf_op jit(solution)/shard_map/all_to_all | solution.py:396
  69.6 15.6 %collective-permute-start.9 = (f32[8,384]{1,0:T(8,128)S(1)}, f32[8,384]{1,0:T(8,128)S(1)}, u32[]{:S(2)}, u32[]{:S(2)}) collective-permute-start(f32[8,384]{1,0:T(8,128)S(1)} %maximum_maximum_fusion), channel_id=1, source_target_pairs={{0,2},{2,0},{1,3},{3,1},{4,6},{6,4},{5,7},{7,5},{8,10},{10,8},{9,1... | collective-permute-start | bytes 36872 | tf_op jit(solution)/shard_map/ppermute | solution.py:377
  76.6 16.2 %all-to-all-start.1 = ((f32[8,24,128]{2,1,0:T(8,128)}), f32[8,24,128]{2,1,0:T(8,128)S(1)}, u32[]{:S(2)}, u32[]{:S(2)}) async-start(f32[8,24,128]{2,1,0:T(8,128)} %broadcast_in_dim.6), calls=%async_computation.1 | async-start | bytes 196608 | tf_op jit(solution)/shard_map/all_to_all | solution.py:396
  93.5 10.5 %all-to-all-start.2 = ((f32[16,24,128]{2,1,0:T(8,128)}), f32[16,24,128]{2,1,0:T(8,128)S(1)}, u32[]{:S(2)}, u32[]{:S(2)}) async-start(f32[16,24,128]{2,1,0:T(8,128)} %broadcast_in_dim.7), calls=%async_computation.2 | async-start | bytes 393216 | tf_op jit(solution)/shard_map/all_to_all | solution.py:396
  104.1 5.4 %collective-permute-start.7 = (f32[384,128]{1,0:T(8,128)S(1)}, f32[384,128]{1,0:T(8,128)S(1)}, u32[]{:S(2)}, u32[]{:S(2)}) collective-permute-start(f32[384,128]{1,0:T(8,128)S(1)} %bitcast.30), channel_id=1, source_target_pairs={{0,1},{1,0},{2,3},{3,2},{4,5},{5,4},{6,7},{7,6},{8,9},{9,8},{10,11... | collective-permute-start | bytes 589832 | tf_op jit(solution)/shard_map/ppermute | solution.py:377
  (12 other events, 8.2 us)

commit v2 on v1

--- a/solution.py
+++ b/solution.py
@@ -19,7 +19,7 @@
 GY = ("z", "xlo")
 GZ = ("xhi", "core")
 PLANE = ("y", "xlo", "xhi")
-VMEM_LIMIT = 40 * 1024 * 1024
+VMEM_LIMIT = 16 * 1024 * 1024
 
 BINS = 16
 TENSORS = 12
@@ -140,55 +140,79 @@
     return jnp.concatenate([total, count, rest, jnp.zeros((5, ROWS), F32)], axis=0)
 
 
-def gram_kernel(
-    flags, table, src, ids, xb, xa, yb, ya, zb, za, receiver, out, cells, grads, scales
-):
+def ends_of(axes):
+    at = lax.axis_index(axes)
+    last = math.prod(SIZES[a] for a in axes) - 1
+    return jnp.where(at > 0, 1.0, 0.0).astype(F32), jnp.where(at < last, 1.0, 0.0).astype(F32)
+
+
+def scale_of(table, marks, p):
+    scale = jnp.zeros((PLANES, LANES), F32)
+    for m in range(8):
+        scale = jnp.where(marks == m, table[p, m], scale)
+    return scale * (1.0 / 12.0)
+
+
+def tile(ref, at):
+    return ref[pl.ds(pl.multiple_of(at * PLANES, PLANES), PLANES), :]
+
+
+def set_tile(ref, at, value):
+    ref[pl.ds(pl.multiple_of(at * PLANES, PLANES), PLANES), :] = value
+
+
+def rows_of(start, strains, first):
+    re, im = start
+    for rec_re, rec_im, real, imag in strains:
+        rec_re, rec_im = rec_re.astype(F32), rec_im.astype(F32)
+        add_re, add_im = rec_re * real - rec_im * imag, rec_re * imag + rec_im * real
+        re, im = (add_re, add_im) if first else (re + add_re, im + add_im)
+        first = False
+    return re, im
+
+
+def cells_kernel(table, src, ids, xb, xa, zb, za, receiver, cells, grads, scales):
     step = pl.program_id(0)
 
     @pl.when(step == 0)
     def _():
-        marks = ids[...]
         for p in range(3):
-            scale = jnp.zeros((PLANES, LANES), F32)
-            for m in range(8):
-                scale = jnp.where(marks == m, table[m, p], scale)
-            scales[p] = scale * (1.0 / 12.0)
+            scales[p * PLANES : (p + 1) * PLANES, :] = scale_of(table, ids[...], p)
         lane = lane_ids((FIELDS, LANES))
-        halo = zb[...] * flags[4] + za[...] * flags[5]
+        x_before, x_after = ends_of(GX)
+        z_before, z_after = ends_of(GZ)
+        halo = zb[...] * z_before + za[...] * z_after
 
         def at(x, y):
             if x < 0:
-                return xb[:, (x + 2) * 4 + y, :] * flags[0]
+                return xb[pl.ds((x + 2) * 4 + y, FIELDS, stride=8), :] * x_before
             if x > 3:
-                return xa[:, (x - 4) * 4 + y, :] * flags[1]
-            if y < 0:
-                return yb[x * 2 + y + 2] * flags[2]
-            if y > 3:
-                return ya[x * 2 + y - 4] * flags[3]
-            return src[:, x * 4 + y, :]
+                return xa[pl.ds((x - 4) * 4 + y, FIELDS, stride=8), :] * x_after
+            if y < 0 or y > 3:
+                return 0.0
+            return src[pl.ds(x * 4 + y, FIELDS, stride=PLANES), :]
+
+        def put(p, plane, value):
+            grads[pl.ds(p * FIELDS * PLANES + plane, FIELDS, stride=PLANES), :] = value
 
         for x in range(4):
             for y in range(4):
                 plane = x * 4 + y
-                grads[0, :, plane, :] = 8.0 * (at(x + 1, y) - at(x - 1, y)) - (
-                    at(x + 2, y) - at(x - 2, y)
-                )
-                grads[1, :, plane, :] = 8.0 * (at(x, y + 1) - at(x, y - 1)) - (
-                    at(x, y + 2) - at(x, y - 2)
-                )
+                put(0, plane, 8.0 * (at(x + 1, y) - at(x - 1, y)) - (at(x + 2, y) - at(x - 2, y)))
+                put(1, plane, 8.0 * (at(x, y + 1) - at(x, y - 1)) - (at(x, y + 2) - at(x, y - 2)))
                 mid = at(x, y)
                 ends = pltpu.roll(halo, LANES - 8 * plane, 1) if plane else halo
                 later = pltpu.roll(jnp.where(lane < 1, ends, mid), LANES - 1, 1)
                 sooner = pltpu.roll(jnp.where(lane >= LANES - 1, ends, mid), 1, 1)
                 later_two = pltpu.roll(jnp.where(lane < 2, ends, mid), LANES - 2, 1)
                 sooner_two = pltpu.roll(jnp.where(lane >= LANES - 2, ends, mid), 2, 1)
-                grads[2, :, plane, :] = 8.0 * (later - sooner) - (later_two - sooner_two)
+                put(2, plane, 8.0 * (later - sooner) - (later_two - sooner_two))
 
     def grad(p, q, k):
-        return scales[p] * grads[p, step * 6 + q * 2 + k]
-
-    def strain(k):
-        return (
+        return tile(scales, p) * tile(grads, p * FIELDS + step * 6 + q * 2 + k)
+
+    real, imag = [
+        (
             grad(0, 0, k),
             grad(1, 1, k),
             grad(2, 2, k),
@@ -196,24 +220,89 @@
             grad(0, 2, k) + grad(2, 0, k),
             grad(0, 1, k) + grad(1, 0, k),
         )
-
-    real, imag = strain(0), strain(1)
+        for k in range(2)
+    ]
     for r in range(TENSORS):
-        re = jnp.zeros((PLANES, LANES), F32)
-        im = jnp.zeros((PLANES, LANES), F32)
-        for j in range(6):
-            rec_re = receiver[r, 0, 2 * j].astype(F32)
-            rec_im = receiver[r, 0, 2 * j + 1].astype(F32)
-            re = re + (rec_re * real[j] - rec_im * imag[j])
-            im = im + (rec_re * imag[j] + rec_im * real[j])
-        cells[r * 32 + step * 2] = re
-        cells[r * 32 + step * 2 + 1] = im
+        terms = [
+            (receiver[r, 0, 2 * j], receiver[r, 0, 2 * j + 1], real[j], imag[j]) for j in range(6)
+        ]
+        re, im = rows_of((None, None), terms, True)
+        set_tile(cells, r * 32 + step * 2, re)
+        set_tile(cells, r * 32 + step * 2 + 1, im)
+
+
+def whole(*shape):
+    return pl.BlockSpec(shape, lambda b: (0,) * len(shape))
+
+
+def cells_within(table, src, ids, halos, receiver):
+    face = whole(FIELDS * 8, LANES)
+    ends = whole(FIELDS, LANES)
+    return pl.pallas_call(
+        cells_kernel,
+        grid=(BINS,),
+        out_shape=jax.ShapeDtypeStruct((ROWS * PLANES, LANES), F32),
+        in_specs=[
+            smem(),
+            whole(FIELDS * PLANES, LANES),
+            whole(PLANES, LANES),
+            face,
+            face,
+            ends,
+            ends,
+            pl.BlockSpec((TENSORS, 1, 12, PLANES, LANES), lambda b: (0, b, 0, 0, 0)),
+        ],
+        out_specs=whole(ROWS * PLANES, LANES),
+        scratch_shapes=[
+            pltpu.VMEM((3 * FIELDS * PLANES, LANES), F32),
+            pltpu.VMEM((3 * PLANES, LANES), F32),
+        ],
+        compiler_params=pltpu.CompilerParams(vmem_limit_bytes=VMEM_LIMIT),
+        cost_estimate=pl.CostEstimate(
+            flops=20_000_000, bytes_accessed=14_000_000, transcendentals=0
+        ),
+        name="cells_within",
+    )(table, src, ids, *halos, receiver)
+
+
+def gram_kernel(
+    table, ids, yb, ya, within, receiver, s0, s1, s2, s3, keep, send, cells, stats, grads, scales
+):
+    step = pl.program_id(0)
+
+    @pl.when(step == 0)
+    def _():
+        scales[...] = scale_of(table, ids[...], 1)
+        before, after = ends_of(GY)
+        for x in range(4):
+            b_two, b_one = yb[x * 2] * before, yb[x * 2 + 1] * before
+            a_one, a_two = ya[x * 2] * after, ya[x * 2 + 1] * after
+            for y, value in enumerate(
+                (b_two - 8.0 * b_one, b_one, -a_one, 8.0 * a_one - a_two)
+            ):
+                grads[pl.ds(x * 4 + y, FIELDS, stride=PLANES), :] = value
+        stats[...] = merge_sums(merge_sums(s0[...], s1[...]), merge_sums(s2[...], s3[...]))
+
+    def grad(q, k):
+        return scales[...] * tile(grads, step * 6 + q * 2 + k)
+
+    real, imag = [(grad(1, k), grad(2, k), grad(0, k)) for k in range(2)]
+    for r in range(TENSORS):
+        at = r * 32 + step * 2
+        terms = [
+            (receiver[r, 0, j, 0, 0], receiver[r, 0, j, 0, 1], real[j], imag[j]) for j in range(3)
+        ]
+        re, im = rows_of((tile(within, at), tile(within, at + 1)), terms, False)
+        set_tile(cells, at, re)
+        set_tile(cells, at + 1, im)
 
     @pl.when(step == BINS - 1)
     def _():
         total = jnp.zeros((ROWS, ROWS), F32)
         for plane in range(0, PLANES, 2):
-            both = jnp.concatenate([cells[:, plane, :], cells[:, plane + 1, :]], axis=1)
+            both = jnp.concatenate(
+                [cells[pl.ds(plane + i, ROWS, stride=PLANES), :] for i in range(2)], axis=1
+            )
             high = both.astype(BF16)
             low = (both - high.astype(F32)).astype(BF16)
             left = jnp.concatenate([high, high], axis=1)
@@ -225,53 +314,80 @@
         def block(i, j):
             return total[i * LANES : (i + 1) * LANES, j * LANES : (j + 1) * LANES]
 
-        for n, (i, j) in enumerate(BLOCKS):
-            out[n * LANES : (n + 1) * LANES, :] = block(i, j) + block(j, i).T
-
-
-def gram(flags, table, src, ids, halos, receiver):
-    whole = lambda *shape: pl.BlockSpec(shape, lambda b: (0,) * len(shape))
-    face = whole(FIELDS, 8, LANES)
+        full = [block(i, j) + block(j, i).T for i, j in BLOCKS]
+        upper = lax.axis_index("core") == 1
+        for n in range(3):
+            part = slice(n * LANES, (n + 1) * LANES)
+            keep[part, :] = jnp.where(upper, full[n + 3], full[n])
+            send[part, :] = jnp.where(upper, full[n], full[n + 3])
+
+
+def gram(table, ids, halos, within, receiver, sums):
     side = whole(8, FIELDS, LANES)
-    ends = whole(FIELDS, LANES)
+    half = jax.ShapeDtypeStruct((3 * LANES, LANES), F32)
     return pl.pallas_call(
         gram_kernel,
         grid=(BINS,),
         out_shape=(
-            jax.ShapeDtypeStruct((768, LANES), F32),
-            jax.ShapeDtypeStruct((ROWS, PLANES, LANES), F32),
+            half,
+            half,
+            jax.ShapeDtypeStruct((ROWS * PLANES, LANES), F32),
+            jax.ShapeDtypeStruct((8, ROWS), F32),
         ),
         in_specs=[
             smem(),
-            smem(),
-            whole(FIELDS, PLANES, LANES),
             whole(PLANES, LANES),
-            face,
-            face,
             side,
             side,
-            ends,
-            ends,
-            pl.BlockSpec((TENSORS, 1, 12, PLANES, LANES), lambda b: (0, b, 0, 0, 0)),
-        ],
-        out_specs=(whole(768, LANES), whole(ROWS, PLANES, LANES)),
+            whole(ROWS * PLANES, LANES),
+            pl.BlockSpec(
+                (TENSORS, 1, 3, 1, 2, PLANES, LANES), lambda b: (0, b, 0, 1, 0, 0, 0)
+            ),
+        ]
+        + [whole(8, ROWS)] * 4,
+        out_specs=(
+            whole(3 * LANES, LANES),
+            whole(3 * LANES, LANES),
+            whole(ROWS * PLANES, LANES),
+            whole(8, ROWS),
+        ),
         scratch_shapes=[
-            pltpu.VMEM((3, FIELDS, PLANES, LANES), F32),
-            pltpu.VMEM((3, PLANES, LANES), F32),
+            pltpu.VMEM((FIELDS * PLANES, LANES), F32),
+            pltpu.VMEM((PLANES, LANES), F32),
         ],
         compiler_params=pltpu.CompilerParams(vmem_limit_bytes=VMEM_LIMIT),
+        cost_estimate=pl.CostEstimate(
+            flops=1_200_000_000, bytes_accessed=8_000_000, transcendentals=0
+        ),
         name="gram",
-    )(flags, table, src, ids, *halos, receiver)
+    )(table, ids, *halos, within, receiver, *sums)
 
 
 def chain_kernel(
-    packed, stats, cells, observed, tensor_ref, bins_ref, window, update, direction, data, full, coef
+    mine, other, stats, cells, observed_in, tensor_in, bins_in, window_in, update, direction, data,
+    full, coef, observed, tensor_ref, bins_ref, window, sems
 ):
+    copies = [
+        pltpu.make_async_copy(here, there, sems.at[n])
+        for n, (here, there) in enumerate(
+            (
+                (observed_in, observed),
+                (tensor_in, tensor_ref),
+                (bins_in, bins_ref),
+                (window_in, window),
+            )
+        )
+    ]
+    for copy in copies:
+        copy.start()
+    upper = lax.axis_index("core") == 1
     for n, (i, j) in enumerate(BLOCKS):
-        tile = packed[n * LANES : (n + 1) * LANES, :]
-        full[i * LANES : (i + 1) * LANES, j * LANES : (j + 1) * LANES] = tile
+        part = slice(n % 3 * LANES, (n % 3 + 1) * LANES)
+        near, far = mine[part, :], other[part, :]
+        block = jnp.where(upper, far, near) if n < 3 else jnp.where(upper, near, far)
+        full[i * LANES : (i + 1) * LANES, j * LANES : (j + 1) * LANES] = block
         if i != j:
-            full[j * LANES : (j + 1) * LANES, i * LANES : (i + 1) * LANES] = tile.T
+            full[j * LANES : (j + 1) * LANES, i * LANES : (i + 1) * LANES] = block.T
     eye = lax.broadcasted_iota(jnp.int32, (LANES, LANES), 0) == lane_ids((LANES, LANES))
 
     def column(row):
@@ -336,36 +452,41 @@
     )
     coef[1] = jnp.broadcast_to(column(model * cell_scale), (ROWS, LANES))
 
+    def body(n, sums_of):
+        value = tile(cells, n)
+        return (
+            sums_of[0] + coef[0, pl.ds(n, 1), :] * value,
+            sums_of[1] + coef[1, pl.ds(n, 1), :] * value,
+        )
+
+    start = (jnp.zeros((PLANES, LANES), F32), jnp.zeros((PLANES, LANES), F32))
+    first, second = lax.fori_loop(0, ROWS, body, start, unroll=16)
+    update[...] = first
+    direction[...] = second
+
+    for copy in copies:
+        copy.wait()
     mask = window[...].astype(F32)
     size = math.sqrt(math.prod(observed.shape) * SIZES["xhi"] * SIZES["core"])
     near = pick(column(row * size), bins_ref[...], tensor_ref[...])
     for k in range(2):
         data[k] = (observed[k] * (scale * size) + near[k]) * mask
 
-    def body(n, sums_of):
-        tile = cells[n]
-        return (
-            sums_of[0] + coef[0, pl.ds(n, 1), :] * tile,
-            sums_of[1] + coef[1, pl.ds(n, 1), :] * tile,
-        )
-
-    start = (jnp.zeros((PLANES, LANES), F32), jnp.zeros((PLANES, LANES), F32))
-    first, second = lax.fori_loop(0, ROWS, body, start, unroll=16)
-    update[...] = first
-    direction[...] = second
-
-
-def chain(packed, stats, cells, observed, tensor, bins, window):
+
+def chain(mine, other, stats, cells, observed, tensor, bins, window):
     field = jax.ShapeDtypeStruct((PLANES, LANES), F32)
+    given = (observed, tensor, bins, window)
     return pl.pallas_call(
         chain_kernel,
         out_shape=(field, field, jax.ShapeDtypeStruct(observed.shape, F32)),
-        in_specs=[vmem()] * 7,
+        in_specs=[vmem()] * 4 + [pl.BlockSpec(memory_space=pl.ANY)] * 4,
         out_specs=(vmem(),) * 3,
-        scratch_shapes=[pltpu.VMEM((ROWS, ROWS), F32), pltpu.VMEM((2, ROWS, LANES), F32)],
+        scratch_shapes=[pltpu.VMEM((ROWS, ROWS), F32), pltpu.VMEM((2, ROWS, LANES), F32)]
+        + [pltpu.VMEM(x.shape, x.dtype) for x in given]
+        + [pltpu.SemaphoreType.DMA((4,))],
         compiler_params=pltpu.CompilerParams(vmem_limit_bytes=VMEM_LIMIT),
         name="chain",
-    )(packed, stats, cells, observed, tensor, bins, window)
+    )(mine, other, stats, cells, *given)
 
 
 def shift(value, axes, step):
@@ -377,21 +498,6 @@
     return lax.ppermute(value, axis, [(0, 1), (1, 0)])
 
 
-def half_scatter(value, axis):
-    half = value.shape[0] // 2
-    upper = lax.axis_index(axis) == 1
-    low, high = value[:half], value[half:]
-    return jnp.where(upper, high, low) + swap(jnp.where(upper, low, high), axis)
-
-
-def half_gather(value, axis):
-    upper = lax.axis_index(axis) == 1
-    other = swap(value, axis)
-    return jnp.where(
-        upper, jnp.concatenate([other, value]), jnp.concatenate([value, other])
-    )
-
-
 def exchange(value, axes):
     return lax.all_to_all(value, axes, 0, 0, tiled=True)
 
@@ -409,14 +515,6 @@
 def gather(value, axes):
     count = math.prod(SIZES[a] for a in axes)
     return exchange(jnp.broadcast_to(value, (count,) + value.shape), axes).reshape(-1, LANES)
-
-
-def reduce_all(value):
-    value = half_scatter(value, "core")
-    value = scatter_sum(value, PLANE)
-    value = whole_sum(value, ("z",))
-    value = gather(value, PLANE)
-    return half_gather(value, "core")
 
 
 def per_device(
@@ -431,29 +529,36 @@
 ):
     src = source_field.reshape(FIELDS, PLANES, LANES)
     receiver = receiver_tensor.reshape(TENSORS, BINS, 12, PLANES, LANES)
+    by_pairs = receiver_tensor.reshape(TENSORS, BINS, 3, 2, 2, PLANES, LANES)
     ids = metric_ids.reshape(PLANES, LANES)
+    table = metric_table.T
     x_lo, x_hi, y_lo, y_hi, z_lo, z_hi = pack(src)
-    x_at, y_at, z_at = lax.axis_index(GX), lax.axis_index(GY), lax.axis_index(GZ)
-    ends = [math.prod(SIZES[a] for a in axes) - 1 for axes in (GX, GY, GZ)]
-    flags = jnp.stack(
-        [x_at > 0, x_at < ends[0], y_at > 0, y_at < ends[1], z_at > 0, z_at < ends[2]]
-    ).astype(F32)
+    zb, za = shift(z_hi, GZ, 1), shift(z_lo, GZ, -1)
+    xb, xa = shift(x_hi, GX, 1), shift(x_lo, GX, -1)
     yb, ya = shift(y_hi, GY, 1), shift(y_lo, GY, -1)
-    xb, xa = shift(x_hi, GX, 1), shift(x_lo, GX, -1)
-    zb, za = shift(z_hi, GZ, 1), shift(z_lo, GZ, -1)
 
     values = observed.transpose(0, 2, 1)
     tensor = receiver_index.reshape(1, -1)
     bins, marks = bin_ids.T, window.T
     stats = data_sums(values, tensor, bins, marks)
-    stats = merge_sums(stats, swap(stats, "core"))
-    stats = merge_sums(stats, swap(stats, "xhi"))
-
-    packed, cells = gram(
-        flags, metric_table, src, ids, (xb, xa, yb, ya, zb, za), receiver
+    near = swap(stats, "core")
+    sums = (stats, near, swap(stats, "xhi"), swap(near, "xhi"))
+
+    flat = (FIELDS * 8, LANES)
+    within = cells_within(
+        table,
+        src.reshape(FIELDS * PLANES, LANES),
+        ids,
+        (xb.reshape(flat), xa.reshape(flat), zb, za),
+        receiver,
     )
-    packed = reduce_all(packed)
-    update, direction, data = chain(packed, stats, cells, values, tensor, bins, marks)
+    keep, send, cells, stats = gram(table, ids, (yb, ya), within, by_pairs, sums)
+    packed = keep + swap(send, "core")
+    packed = scatter_sum(packed, PLANE)
+    packed = whole_sum(packed, ("z",))
+    packed = gather(packed, PLANE)
+    other = swap(packed, "core")
+    update, direction, data = chain(packed, other, stats, cells, values, tensor, bins, marks)
     return (
         update.reshape(metric_ids.shape),
         direction.reshape(metric_ids.shape),

time: 116 us -> 104 us (0.90)
  blocking collectives: 0 us -> 39.1 us
  starting transfers between devices: 43.4 us -> 25.9 us
  waiting for transfers between devices: 18.5 us -> 7.9 us
  local copies, waits for them, and re-layouts: 19.2 us -> 10.1 us
  other arithmetic: 7.34 us -> 0.05 us
  Pallas kernels: 25.4 us -> 19.6 us
    all_to_all x0 -> x3, blocking collectives: none -> 39.1 us  [exchange(): return lax.all_to_all(value, axes, 0, 0, tiled=True)]
    all_to_all x3 -> x0, starting transfers between devices: 18 us -> none  [exchange(): return lax.all_to_all(value, axes, 0, 0, tiled=True)]
    all_to_all x3 -> x0, waiting for transfers between devices: 16.2 us -> none  [exchange(): return lax.all_to_all(value, axes, 0, 0, tiled=True)]
    unnamed x47 -> x28, local copies, waits for them, and re-layouts: 17.1 us -> 10.1 us
    pallas_call x1 -> x2, Pallas kernels: 21.3 us -> 15.2 us  [the longest x1 9.22 us: cells_within(): pl.pallas_call(cells_kernel, grid=(BINS,), out_shape=jax.ShapeDtypeStruct...]
    add x4 -> x1, other arithmetic: 4.03 us -> 0.02 us  [per_device(): packed = keep + swap(send, 'core')]
    ppermute x6, waiting for transfers between devices: 1.09 us -> 4.92 us  [shift(): lax.ppermute(value, axes, [(i, (i + step) % count) for i in range(count)])]
    ppermute x4 -> x5, waiting for transfers between devices: 1.21 us -> 2.98 us  [swap(): return lax.ppermute(value, axis, [(0, 1), (1, 0)])]
  transfers between devices with their start and end apart: 13 -> 11, of which waited for: 8 -> 5; matrix products, arithmetic and copies ran while one was open for 8% -> 0% of each run, Pallas kernels for 0% -> 9%
where the time goes in v2:
time: 104 us
  blocking collectives  39.1 us (38%)
  starting transfers between devices  25.9 us (25%)
  Pallas kernels  19.6 us (19%)
  local copies, waits for them, and re-layouts  10.1 us (10%)
  waiting for transfers between devices  7.9 us (8%)
    all_to_all x3, blocking collectives, exchange(): return lax.all_to_all(value, axes, 0, 0, tiled=True)  39.1 us
    ppermute x6, starting transfers between devices, shift(): lax.ppermute(value, axes, [(i, (i + step) % count) for i in range(count)])  16.7 us
    unnamed x28, local copies, waits for them, and re-layouts  10.1 us
    pallas_call x1, Pallas kernels, cells_within(): pl.pallas_call(cells_kernel, grid=(BINS,), out_shape=jax.ShapeDtypeStruct...  9.22 us
    ppermute x5, starting transfers between devices, swap(): return lax.ppermute(value, axis, [(0, 1), (1, 0)])  9.15 us
    pallas_call x1, Pallas kernels, gram(): pl.pallas_call(gram_kernel, grid=(BINS,), out_shape=(half, half, jax.Shap...  6.02 us
    ppermute x6, waiting for transfers between devices, shift(): lax.ppermute(value, axes, [(i, (i + step) % count) for i in range(count)])  4.92 us
    pallas_call x1, Pallas kernels, chain(): pl.pallas_call(chain_kernel, out_shape=(field, field, jax.ShapeDtypeStruc...  3.32 us
  transfers between devices with their start and end apart: 11, of which 5 were waited for; matrix products, arithmetic and copies ran while one was open for 0% of the time, Pallas kernels for 9%

profile of v2, /device:TPU:1, one launch (start us, length us, event | category | flops | bytes accessed | tf_op | source)
XLA Modules:
  0.0 103.6 jit_solution(18282039202878046419)
XLA Ops:
  0.6 1.1 %copy-done.2 = f32[16,3,2,4,4,128]{5,4,3,2,1,0:T(4,128)S(1)} copy-done((f32[16,3,2,4,4,128]{5,4,3,2,1,0:T(4,128)S(1)}, f32[16,3,2,4,4,128]{5,4,3,2,1,0:T(4,128)}, u32[]{:S(2)}) %copy-start.2) | copy-done | bytes 786456
  2.3 2.2 %collective-permute-start.2 = (f32[96,8,128]{2,1,0:T(8,128)S(1)}, f32[96,8,128]{2,1,0:T(8,128)S(1)}, u32[]{:S(2)}, u32[]{:S(2)}) collective-permute-start(f32[96,8,128]{2,1,0:T(8,128)S(1)} %get-tuple-element.18), channel_id=1, source_target_pairs={{0,64},{64,128},{128,192},{192,0},{1,65},{65,129},{129,193},{193,1... | collective-permute-start | bytes 1179656 | tf_op jit(solution)/shard_map/ppermute | solution.py:494
  4.5 1.5 %collective-permute-start.3 = (f32[96,8,128]{2,1,0:T(8,128)S(1)}, f32[96,8,128]{2,1,0:T(8,128)S(1)}, u32[]{:S(2)}, u32[]{:S(2)}) collective-permute-start(f32[96,8,128]{2,1,0:T(8,128)S(1)} %get-tuple-element.19), channel_id=1, source_target_pairs={{0,192},{64,0},{128,64},{192,128},{1,193},{65,1},{129,65},{193,129... | collective-permute-start | bytes 1179656 | tf_op jit(solution)/shard_map/ppermute | solution.py:494
  6.0 1.2 %collective-permute-start = (f32[8,96,128]{2,1,0:T(8,128)S(1)}, f32[8,96,128]{2,1,0:T(8,128)S(1)}, u32[]{:S(2)}, u32[]{:S(2)}) collective-permute-start(f32[8,96,128]{2,1,0:T(8,128)S(1)} %get-tuple-element.16), channel_id=1, source_target_pairs={{0,4},{4,8},{8,12},{12,16},{16,20},{20,24},{24,28},{28,32},{32,36}... | collective-permute-start | bytes 1179656 | tf_op jit(solution)/shard_map/ppermute | solution.py:494
  7.2 5.3 %collective-permute-start.1 = (f32[8,96,128]{2,1,0:T(8,128)S(1)}, f32[8,96,128]{2,1,0:T(8,128)S(1)}, u32[]{:S(2)}, u32[]{:S(2)}) collective-permute-start(f32[8,96,128]{2,1,0:T(8,128)S(1)} %get-tuple-element.17), channel_id=1, source_target_pairs={{0,60},{4,0},{8,4},{12,8},{16,12},{20,16},{24,20},{28,24},{32,28},... | collective-permute-start | bytes 1179656 | tf_op jit(solution)/shard_map/ppermute | solution.py:494
  12.5 0.7 copy-done.4
  15.8 1.4 %collective-permute-start.6 = (f32[8,384]{1,0:T(8,128)S(1)}, f32[8,384]{1,0:T(8,128)S(1)}, u32[]{:S(2)}, u32[]{:S(2)}) collective-permute-start(f32[8,384]{1,0:T(8,128)S(1)} %data_sums.1.s0), channel_id=1, source_target_pairs={{0,1},{1,0},{2,3},{3,2},{4,5},{5,4},{6,7},{7,6},{8,9},{9,8},{10,11... | collective-permute-start | bytes 36872 | tf_op jit(solution)/shard_map/ppermute | solution.py:498
  17.3 0.8 collective-permute-done.6.s1
  18.1 2.7 %collective-permute-start.4 = (f32[96,128]{1,0:T(8,128)S(1)}, f32[96,128]{1,0:T(8,128)S(1)}, u32[]{:S(2)}, u32[]{:S(2)}) collective-permute-start(f32[96,128]{1,0:T(8,128)S(1)} %get-tuple-element.20), channel_id=1, source_target_pairs={{0,1},{1,2},{2,3},{3,0},{4,5},{5,6},{6,7},{7,4},{8,9},{9,10},{10,1... | collective-permute-start | bytes 147464 | tf_op jit(solution)/shard_map/ppermute | solution.py:494
  20.8 3.0 %collective-permute-done.4.zb = f32[96,128]{1,0:T(8,128)S(1)} collective-permute-done((f32[96,128]{1,0:T(8,128)S(1)}, f32[96,128]{1,0:T(8,128)S(1)}, u32[]{:S(2)}, u32[]{:S(2)}) %collective-permute-start.4) | collective-permute-done | bytes 49184 | tf_op jit(solution)/shard_map/ppermute | solution.py:494
  23.8 3.8 %collective-permute-start.5 = (f32[96,128]{1,0:T(8,128)S(1)}, f32[96,128]{1,0:T(8,128)S(1)}, u32[]{:S(2)}, u32[]{:S(2)}) collective-permute-start(f32[96,128]{1,0:T(8,128)S(1)} %get-tuple-element.21), channel_id=1, source_target_pairs={{0,3},{1,0},{2,1},{3,2},{4,7},{5,4},{6,5},{7,6},{8,11},{9,8},{10,9... | collective-permute-start | bytes 147464 | tf_op jit(solution)/shard_map/ppermute | solution.py:494
  27.6 1.9 %collective-permute-done.5.za = f32[96,128]{1,0:T(8,128)S(1)} collective-permute-done((f32[96,128]{1,0:T(8,128)S(1)}, f32[96,128]{1,0:T(8,128)S(1)}, u32[]{:S(2)}, u32[]{:S(2)}) %collective-permute-start.5) | collective-permute-done | bytes 49184 | tf_op jit(solution)/shard_map/ppermute | solution.py:494
  29.5 2.7 %collective-permute-start.7 = (f32[8,384]{1,0:T(8,128)S(1)}, f32[8,384]{1,0:T(8,128)S(1)}, u32[]{:S(2)}, u32[]{:S(2)}) collective-permute-start(f32[8,384]{1,0:T(8,128)S(1)} %data_sums.1.s0), channel_id=1, source_target_pairs={{0,2},{2,0},{1,3},{3,1},{4,6},{6,4},{5,7},{7,5},{8,10},{10,8},{9,1... | collective-permute-start | bytes 36872 | tf_op jit(solution)/shard_map/ppermute | solution.py:498
  32.5 3.7 %copy-done = bf16[12,16,6,2,4,4,128]{6,5,4,3,2,1,0:T(4,128)(2,1)S(1)} copy-done((bf16[12,16,6,2,4,4,128]{6,5,4,3,2,1,0:T(4,128)(2,1)S(1)}, bf16[12,16,6,2,4,4,128]{6,5,4,3,2,1,0:T(4,128)(2,1)}, u32[]{:S(2)}) %copy-start) | copy-done | bytes 9437208
  36.2 1.1 %copy-done.3 = f32[16,3,2,4,4,128]{5,4,3,2,1,0:T(4,128)S(1)} copy-done((f32[16,3,2,4,4,128]{5,4,3,2,1,0:T(4,128)S(1)}, f32[16,3,2,4,4,128]{5,4,3,2,1,0:T(4,128)}, u32[]{:S(2)}) %copy-start.3) | copy-done | bytes 786456
  38.7 9.2 %cells_within.1.within = f32[6144,128]{1,0:T(8,128)S(1)} custom-call(f32[3,8]{1,0:T(4,128)S(1)} %bitcast.33, f32[1536,128]{1,0:T(8,128)S(1)} %bitcast.20, s32[16,128]{1,0:T(8,128)S(1)} %bitcast.27, f32[768,128]{1,0:T(8,128)S(1)} %bitcast.23, f32[768,128]{1,0:T(8,128)S(1)} %bitcast.24, f32[96,128]{1,0:T(8,128)S(1)} %collective-permute-done.4.zb, ...), custom_call_target="tpu_custom_call" | custom-call | flops 20000000 | bytes 14000000 | tf_op jit(solution)/shard_map/cells_within/pallas_call | solution.py:241
  48.1 6.0 %gram.1 = (f32[384,128]{1,0:T(8,128)S(1)}, f32[384,128]{1,0:T(8,128)S(1)}, f32[6144,128]{1,0:T(8,128)S(1)}, f32[8,384]{1,0:T(8,128)S(1)}) custom-call(f32[3,8]{1,0:T(4,128)S(1)} %bitcast.34, s32[16,128]{1,0:T(8,128)S(1)} %bitcast.28, f32[8,96,128]{2,1,0:T(8,128)S(1)} %collective-permute-done.yb, f32[8,96,128]{2,1,0:T(8,128)S(1)} %collective-permute-done.1.ya, ...), custom_call_target="tpu_custom_call" | custom-call | flops 1200000000 | bytes 8000000 | tf_op jit(solution)/shard_map/gram/pallas_call | solution.py:328
  54.5 1.1 %collective-permute-done.9 = f32[384,128]{1,0:T(8,128)S(1)} collective-permute-done((f32[384,128]{1,0:T(8,128)S(1)}, f32[384,128]{1,0:T(8,128)S(1)}, u32[]{:S(2)}, u32[]{:S(2)}) %collective-permute-start.9) | collective-permute-done | bytes 196640 | tf_op jit(solution)/shard_map/ppermute | solution.py:498
  55.6 12.9 %all_to_all.15 = f32[16,24,128]{2,1,0:T(8,128)S(1)} all-to-all(f32[16,24,128]{2,1,0:T(8,128)S(1)} %bitcast.37), channel_id=1, replica_groups=mesh['y'=4,'z'=8,'xlo'=2,'xhi'=2,'core'=2] {'y','xlo','xhi'}, dimensions={0} | all-to-all | bytes 393216 | tf_op jit(solution)/shard_map/all_to_all | solution.py:502
  68.6 16.0 %all_to_all.16 = f32[8,24,128]{2,1,0:T(8,128)S(1)} all-to-all(f32[8,24,128]{2,1,0:T(8,128)S(1)} %broadcast_in_dim.6), channel_id=1, replica_groups=mesh['y'=4,'z'=8,'xlo'=2,'xhi'=2,'core'=2] {'z'}, dimensions={0} | all-to-all | bytes 196608 | tf_op jit(solution)/shard_map/all_to_all | solution.py:502
  84.7 10.1 %all_to_all.17 = f32[16,24,128]{2,1,0:T(8,128)S(1)} all-to-all(f32[16,24,128]{2,1,0:T(8,128)S(1)} %broadcast_in_dim.7), channel_id=1, replica_groups=mesh['y'=4,'z'=8,'xlo'=2,'xhi'=2,'core'=2] {'y','xlo','xhi'}, dimensions={0} | all-to-all | bytes 393216 | tf_op jit(solution)/shard_map/all_to_all | solution.py:502
  94.8 4.3 %collective-permute-start.10 = (f32[384,128]{1,0:T(8,128)S(1)}, f32[384,128]{1,0:T(8,128)S(1)}, u32[]{:S(2)}, u32[]{:S(2)}) collective-permute-start(f32[384,128]{1,0:T(8,128)S(1)} %bitcast.21), channel_id=1, source_target_pairs={{0,1},{1,0},{2,3},{3,2},{4,5},{5,4},{6,7},{7,6},{8,9},{9,8},{10,11... | collective-permute-start | bytes 589832 | tf_op jit(solution)/shard_map/ppermute | solution.py:498
  99.0 1.1 %collective-permute-done.10.other = f32[384,128]{1,0:T(8,128)S(1)} collective-permute-done((f32[384,128]{1,0:T(8,128)S(1)}, f32[384,128]{1,0:T(8,128)S(1)}, u32[]{:S(2)}, u32[]{:S(2)}) %collective-permute-start.10) | collective-permute-done | bytes 196640 | tf_op jit(solution)/shard_map/ppermute | solution.py:498
  100.1 3.3 %chain.1 = (f32[16,128]{1,0:T(8,128)}, f32[16,128]{1,0:T(8,128)}, f32[2,16,96]{2,1,0:T(8,128)}) custom-call(f32[384,128]{1,0:T(8,128)S(1)} %bitcast.22, f32[384,128]{1,0:T(8,128)S(1)} %collective-permute-done.10.other, f32[8,384]{1,0:T(8,128)S(1)} %get-tuple-element.24.stats, f32[6144,128]{1,0:T(8,128)S(1)} %get-tuple-element.25.cells, ...), custom_call_target="tpu_custom_call" | custom-call | tf_op jit(solution)/shard_map/chain/pallas_call | solution.py:479
  (39 shorter events, 5.4 us)
Async XLA Ops:
  0.6 1.1 %copy-start.2 = (f32[16,3,2,4,4,128]{5,4,3,2,1,0:T(4,128)S(1)}, f32[16,3,2,4,4,128]{5,4,3,2,1,0:T(4,128)}, u32[]{:S(2)}) copy-start(f32[16,3,2,4,4,128]{5,4,3,2,1,0:T(4,128)} %param.8) | copy-start | bytes 2359300
  2.3 30.0 %collective-permute-start.2 = (f32[96,8,128]{2,1,0:T(8,128)S(1)}, f32[96,8,128]{2,1,0:T(8,128)S(1)}, u32[]{:S(2)}, u32[]{:S(2)}) collective-permute-start(f32[96,8,128]{2,1,0:T(8,128)S(1)} %get-tuple-element.18), channel_id=1, source_target_pairs={{0,64},{64,128},{128,192},{192,0},{1,65},{65,129},{129,193},{193,1... | collective-permute-start | bytes 1179656 | tf_op jit(solution)/shard_map/ppermute | solution.py:494
  4.5 28.1 %collective-permute-start.3 = (f32[96,8,128]{2,1,0:T(8,128)S(1)}, f32[96,8,128]{2,1,0:T(8,128)S(1)}, u32[]{:S(2)}, u32[]{:S(2)}) collective-permute-start(f32[96,8,128]{2,1,0:T(8,128)S(1)} %get-tuple-element.19), channel_id=1, source_target_pairs={{0,192},{64,0},{128,64},{192,128},{1,193},{65,1},{129,65},{193,129... | collective-permute-start | bytes 1179656 | tf_op jit(solution)/shard_map/ppermute | solution.py:494
  6.0 42.0 %collective-permute-start = (f32[8,96,128]{2,1,0:T(8,128)S(1)}, f32[8,96,128]{2,1,0:T(8,128)S(1)}, u32[]{:S(2)}, u32[]{:S(2)}) collective-permute-start(f32[8,96,128]{2,1,0:T(8,128)S(1)} %get-tuple-element.16), channel_id=1, source_target_pairs={{0,4},{4,8},{8,12},{12,16},{16,20},{20,24},{24,28},{28,32},{32,36}... | collective-permute-start | bytes 1179656 | tf_op jit(solution)/shard_map/ppermute | solution.py:494
  7.2 40.8 %collective-permute-start.1 = (f32[8,96,128]{2,1,0:T(8,128)S(1)}, f32[8,96,128]{2,1,0:T(8,128)S(1)}, u32[]{:S(2)}, u32[]{:S(2)}) collective-permute-start(f32[8,96,128]{2,1,0:T(8,128)S(1)} %get-tuple-element.17), channel_id=1, source_target_pairs={{0,60},{4,0},{8,4},{12,8},{16,12},{20,16},{24,20},{28,24},{32,28},... | collective-permute-start | bytes 1179656 | tf_op jit(solution)/shard_map/ppermute | solution.py:494
  12.5 0.7 copy-start.4
  13.2 0.7 copy-start.7
  13.9 0.7 copy-start.9
  15.8 2.3 %collective-permute-start.6 = (f32[8,384]{1,0:T(8,128)S(1)}, f32[8,384]{1,0:T(8,128)S(1)}, u32[]{:S(2)}, u32[]{:S(2)}) collective-permute-start(f32[8,384]{1,0:T(8,128)S(1)} %data_sums.1.s0), channel_id=1, source_target_pairs={{0,1},{1,0},{2,3},{3,2},{4,5},{5,4},{6,7},{7,6},{8,9},{9,8},{10,11... | collective-permute-start | bytes 36872 | tf_op jit(solution)/shard_map/ppermute | solution.py:498
  18.1 5.7 %collective-permute-start.4 = (f32[96,128]{1,0:T(8,128)S(1)}, f32[96,128]{1,0:T(8,128)S(1)}, u32[]{:S(2)}, u32[]{:S(2)}) collective-permute-start(f32[96,128]{1,0:T(8,128)S(1)} %get-tuple-element.20), channel_id=1, source_target_pairs={{0,1},{1,2},{2,3},{3,0},{4,5},{5,6},{6,7},{7,4},{8,9},{9,10},{10,1... | collective-permute-start | bytes 147464 | tf_op jit(solution)/shard_map/ppermute | solution.py:494
  23.8 5.8 %collective-permute-start.5 = (f32[96,128]{1,0:T(8,128)S(1)}, f32[96,128]{1,0:T(8,128)S(1)}, u32[]{:S(2)}, u32[]{:S(2)}) collective-permute-start(f32[96,128]{1,0:T(8,128)S(1)} %get-tuple-element.21), channel_id=1, source_target_pairs={{0,3},{1,0},{2,1},{3,2},{4,7},{5,4},{6,5},{7,6},{8,11},{9,8},{10,9... | collective-permute-start | bytes 147464 | tf_op jit(solution)/shard_map/ppermute | solution.py:494
  29.5 18.4 %collective-permute-start.7 = (f32[8,384]{1,0:T(8,128)S(1)}, f32[8,384]{1,0:T(8,128)S(1)}, u32[]{:S(2)}, u32[]{:S(2)}) collective-permute-start(f32[8,384]{1,0:T(8,128)S(1)} %data_sums.1.s0), channel_id=1, source_target_pairs={{0,2},{2,0},{1,3},{3,1},{4,6},{6,4},{5,7},{7,5},{8,10},{10,8},{9,1... | collective-permute-start | bytes 36872 | tf_op jit(solution)/shard_map/ppermute | solution.py:498
  32.2 15.7 %collective-permute-start.8 = (f32[8,384]{1,0:T(8,128)S(1)}, f32[8,384]{1,0:T(8,128)S(1)}, u32[]{:S(2)}, u32[]{:S(2)}) collective-permute-start(f32[8,384]{1,0:T(8,128)S(1)} %collective-permute-done.6.s1), channel_id=1, source_target_pairs={{0,2},{2,0},{1,3},{3,1},{4,6},{6,4},{5,7},{7,5},{8,10},{10,8},{9,1... | collective-permute-start | bytes 36872 | tf_op jit(solution)/shard_map/ppermute | solution.py:498
  32.5 3.7 %copy-start = (bf16[12,16,6,2,4,4,128]{6,5,4,3,2,1,0:T(4,128)(2,1)S(1)}, bf16[12,16,6,2,4,4,128]{6,5,4,3,2,1,0:T(4,128)(2,1)}, u32[]{:S(2)}) copy-start(bf16[12,16,6,2,4,4,128]{6,5,4,3,2,1,0:T(4,128)(2,1)} %param.9) | copy-start | bytes 28311556
  36.2 1.1 %copy-start.3 = (f32[16,3,2,4,4,128]{5,4,3,2,1,0:T(4,128)S(1)}, f32[16,3,2,4,4,128]{5,4,3,2,1,0:T(4,128)}, u32[]{:S(2)}) copy-start(f32[16,3,2,4,4,128]{5,4,3,2,1,0:T(4,128)} %param.8) | copy-start | bytes 2359300
  37.3 0.7 copy-start.6
  38.0 0.7 copy-start.11
  38.7 9.3 %copy-start.1 = (bf16[12,16,6,2,4,4,128]{6,5,4,3,2,1,0:T(4,128)(2,1)S(1)}, bf16[12,16,6,2,4,4,128]{6,5,4,3,2,1,0:T(4,128)(2,1)}, u32[]{:S(2)}) copy-start(bf16[12,16,6,2,4,4,128]{6,5,4,3,2,1,0:T(4,128)(2,1)} %param.9) | copy-start | bytes 28311556
  48.0 52.1 %copy-start.5 = (f32[2,96,16]{1,2,0:T(8,128)S(1)}, f32[2,96,16]{1,2,0:T(8,128)}, u32[]{:S(2)}) copy-start(f32[2,96,16]{1,2,0:T(8,128)} %param.12) | copy-start | bytes 36868
  48.0 52.1 %copy-start.8 = (s32[96,16]{0,1:T(8,128)S(1)}, s32[96,16]{0,1:T(8,128)}, u32[]{:S(2)}) copy-start(s32[96,16]{0,1:T(8,128)} %param.14) | copy-start | bytes 18436
  48.0 52.1 %copy-start.10 = (s32[96,16]{0,1:T(8,128)S(1)}, s32[96,16]{0,1:T(8,128)}, u32[]{:S(2)}) copy-start(s32[96,16]{0,1:T(8,128)} %param.15) | copy-start | bytes 18436
  48.0 52.1 %copy-start.13 = (s32[96]{0:T(128)S(1)}, s32[96]{0:T(128)}, u32[]{:S(2)}) copy-start(s32[96]{0:T(128)} %param.13) | copy-start | bytes 1156
  54.1 1.5 %collective-permute-start.9 = (f32[384,128]{1,0:T(8,128)S(1)}, f32[384,128]{1,0:T(8,128)S(1)}, u32[]{:S(2)}, u32[]{:S(2)}) collective-permute-start(f32[384,128]{1,0:T(8,128)S(1)} %get-tuple-element.23), channel_id=1, source_target_pairs={{0,1},{1,0},{2,3},{3,2},{4,5},{5,4},{6,7},{7,6},{8,9},{9,8},{10,11... | collective-permute-start | bytes 589832 | tf_op jit(solution)/shard_map/ppermute | solution.py:498
  94.8 5.3 %collective-permute-start.10 = (f32[384,128]{1,0:T(8,128)S(1)}, f32[384,128]{1,0:T(8,128)S(1)}, u32[]{:S(2)}, u32[]{:S(2)}) collective-permute-start(f32[384,128]{1,0:T(8,128)S(1)} %bitcast.21), channel_id=1, source_target_pairs={{0,1},{1,0},{2,3},{3,2},{4,5},{5,4},{6,7},{7,6},{8,9},{9,8},{10,11... | collective-permute-start | bytes 589832 | tf_op jit(solution)/shard_map/ppermute | solution.py:498
  (1 other events, 0.7 us)

commit v3 on v2

--- a/solution.py
+++ b/solution.py
@@ -34,15 +34,100 @@
     return pl.BlockSpec(memory_space=pltpu.VMEM)
 
 
-def smem():
-    return pl.BlockSpec(memory_space=pltpu.SMEM)
+def hbm():
+    return pl.BlockSpec(memory_space=pltpu.HBM)
 
 
 def lane_ids(shape):
     return lax.broadcasted_iota(jnp.int32, shape, len(shape) - 1)
 
 
-def pack_kernel(src, x_lo, x_hi, y_lo, y_hi, z_lo, z_hi):
+def spread(values, bins, tensor):
+    parts = []
+    for b in range(BINS):
+        here = bins == b
+        for k in range(2):
+            parts.append(jnp.sum(jnp.where(here, values[k], 0.0), axis=0, keepdims=True))
+    table = jnp.concatenate(parts, axis=0)
+    return jnp.concatenate(
+        [
+            jnp.sum(jnp.where(tensor == r, table, 0.0), axis=1, keepdims=True)
+            for r in range(TENSORS)
+        ],
+        axis=0,
+    )
+
+
+def pick(column, bins, tensor):
+    table = jnp.zeros((2 * BINS, bins.shape[1]), F32)
+    for r in range(TENSORS):
+        table = jnp.where(tensor == r, column[r * 32 : (r + 1) * 32, :], table)
+    out = [jnp.zeros(bins.shape, F32), jnp.zeros(bins.shape, F32)]
+    for b in range(BINS):
+        here = bins == b
+        for k in range(2):
+            out[k] = jnp.where(here, table[2 * b + k : 2 * b + k + 1, :], out[k])
+    return out
+
+
+def data_sums(observed, tensor, bins, window):
+    mask = window.astype(F32)
+    rhs = [observed[k] * mask for k in range(2)]
+    total = spread(rhs, bins, tensor)
+    count = spread([mask, mask], bins, tensor)
+    mean = total / jnp.maximum(count, 1.0)
+    near = pick(mean, bins, tensor)
+    rest = [rhs[k] - near[k] * mask for k in range(2)]
+    square = jnp.sum(rest[0] * rest[0] + rest[1] * rest[1], axis=(0, 1), keepdims=True)
+    lane = lane_ids((ROWS, LANES))
+    wide = jnp.where(lane == 0, total, jnp.where(lane == 1, count, square))
+    return jnp.concatenate([wide[j * LANES : (j + 1) * LANES, :].T[:8] for j in range(3)], axis=0)
+
+
+def merge_sums(one, two):
+    total, count = one[0:1] + two[0:1], one[1:2] + two[1:2]
+    gap = one[0:1] / jnp.maximum(one[1:2], 1.0) - two[0:1] / jnp.maximum(two[1:2], 1.0)
+    apart = jnp.sum(
+        one[1:2] * two[1:2] / jnp.maximum(count, 1.0) * gap * gap, axis=1, keepdims=True
+    )
+    rest = one[2:3] + two[2:3] + apart
+    return jnp.concatenate([total, count, rest, jnp.zeros((5, ROWS), F32)], axis=0)
+
+
+def pack_kernel(
+    src_in, ids_in, table_in, observed_in, tensor_in, bins_in, window_in,
+    src, x_lo, x_hi, y_lo, y_hi, to_core, to_cross, stats, scales,
+    ids, table, observed, tensor, bins, window, sems,
+):
+    copies = [
+        pltpu.make_async_copy(here, there, sems.at[n])
+        for n, (here, there) in enumerate(
+            (
+                (src_in, src),
+                (ids_in, ids),
+                (table_in, table),
+                (observed_in, observed),
+                (tensor_in, tensor),
+                (bins_in, bins),
+                (window_in, window),
+            )
+        )
+    ]
+    for copy in copies:
+        copy.start()
+    for copy in copies[1:]:
+        copy.wait()
+    for p in range(3):
+        scale = jnp.zeros((PLANES, LANES), F32)
+        for m in range(8):
+            scale = jnp.where(ids[...] == m, table[p, m], scale)
+        scales[p * PLANES : (p + 1) * PLANES, :] = scale * (1.0 / 12.0)
+    sums = data_sums(observed, tensor[...], bins[...], window[...])
+    stats[...] = sums
+    to_core[FIELDS:, :] = sums
+    to_cross[FIELDS:, :] = sums
+
+    copies[0].wait()
     x_lo[...] = src[:, 0:8, :]
     x_hi[...] = src[:, 8:16, :]
     lane = lane_ids((FIELDS, LANES))
@@ -59,98 +144,43 @@
         place = (lane - 8 * plane) & (LANES - 1)
         low = jnp.where(place < 2, turned, low)
         high = jnp.where(place >= LANES - 2, turned, high)
-    z_lo[...] = low
-    z_hi[...] = high
-
-
-def pack(src):
+    upper = lax.axis_index("core") == 1
+    to_core[:FIELDS, :] = jnp.where(upper, low, high)
+    to_cross[:FIELDS, :] = jnp.where(upper, high, low)
+
+
+def pack(src, ids, table, observed, tensor, bins, window):
     face = jax.ShapeDtypeStruct((FIELDS, 8, LANES), F32)
     side = jax.ShapeDtypeStruct((8, FIELDS, LANES), F32)
-    ends = jax.ShapeDtypeStruct((FIELDS, LANES), F32)
+    ends = jax.ShapeDtypeStruct((FIELDS + 24, LANES), F32)
+    given = (src, ids, table, observed, tensor, bins, window)
     return pl.pallas_call(
         pack_kernel,
-        out_shape=(face, face, side, side, ends, ends),
-        in_specs=[vmem()],
-        out_specs=(vmem(),) * 6,
+        out_shape=(
+            jax.ShapeDtypeStruct(src.shape, F32),
+            face,
+            face,
+            side,
+            side,
+            ends,
+            ends,
+            jax.ShapeDtypeStruct((24, LANES), F32),
+            jax.ShapeDtypeStruct((3 * PLANES, LANES), F32),
+        ),
+        in_specs=[hbm()] * 7,
+        out_specs=(vmem(),) * 9,
+        scratch_shapes=[pltpu.VMEM(ids.shape, ids.dtype), pltpu.SMEM(table.shape, table.dtype)]
+        + [pltpu.VMEM(x.shape, x.dtype) for x in given[3:]]
+        + [pltpu.SemaphoreType.DMA((7,))],
         compiler_params=pltpu.CompilerParams(vmem_limit_bytes=VMEM_LIMIT),
         name="pack",
-    )(src)
-
-
-def spread(values, bins, tensor):
-    parts = []
-    for b in range(BINS):
-        here = bins == b
-        for k in range(2):
-            parts.append(jnp.sum(jnp.where(here, values[k], 0.0), axis=0, keepdims=True))
-    table = jnp.concatenate(parts, axis=0)
-    return jnp.concatenate(
-        [
-            jnp.sum(jnp.where(tensor == r, table, 0.0), axis=1, keepdims=True)
-            for r in range(TENSORS)
-        ],
-        axis=0,
-    )
-
-
-def pick(column, bins, tensor):
-    table = jnp.zeros((2 * BINS, bins.shape[1]), F32)
-    for r in range(TENSORS):
-        table = jnp.where(tensor == r, column[r * 32 : (r + 1) * 32, :], table)
-    out = [jnp.zeros(bins.shape, F32), jnp.zeros(bins.shape, F32)]
-    for b in range(BINS):
-        here = bins == b
-        for k in range(2):
-            out[k] = jnp.where(here, table[2 * b + k : 2 * b + k + 1, :], out[k])
-    return out
-
-
-def data_kernel(observed, tensor_ref, bins_ref, window, stats):
-    tensor, bins = tensor_ref[...], bins_ref[...]
-    mask = window[...].astype(F32)
-    rhs = [observed[k] * mask for k in range(2)]
-    total = spread(rhs, bins, tensor)
-    count = spread([mask, mask], bins, tensor)
-    mean = total / jnp.maximum(count, 1.0)
-    near = pick(mean, bins, tensor)
-    rest = [rhs[k] - near[k] * mask for k in range(2)]
-    square = jnp.sum(rest[0] * rest[0] + rest[1] * rest[1], axis=(0, 1), keepdims=True)
-    lane = lane_ids((ROWS, LANES))
-    wide = jnp.where(lane == 0, total, jnp.where(lane == 1, count, square))
-    for j in range(3):
-        stats[:, j * LANES : (j + 1) * LANES] = wide[j * LANES : (j + 1) * LANES, :].T[:8]
-
-
-def data_sums(observed, tensor, bins, window):
-    return pl.pallas_call(
-        data_kernel,
-        out_shape=jax.ShapeDtypeStruct((8, ROWS), F32),
-        in_specs=[vmem()] * 4,
-        out_specs=vmem(),
-        compiler_params=pltpu.CompilerParams(vmem_limit_bytes=VMEM_LIMIT),
-        name="data_sums",
-    )(observed, tensor, bins, window)
-
-
-def merge_sums(one, two):
-    total, count = one[0:1] + two[0:1], one[1:2] + two[1:2]
-    gap = one[0:1] / jnp.maximum(one[1:2], 1.0) - two[0:1] / jnp.maximum(two[1:2], 1.0)
-    apart = jnp.sum(one[1:2] * two[1:2] / jnp.maximum(count, 1.0) * gap * gap)
-    rest = one[2:3] + two[2:3] + apart
-    return jnp.concatenate([total, count, rest, jnp.zeros((5, ROWS), F32)], axis=0)
+    )(*given)
 
 
 def ends_of(axes):
     at = lax.axis_index(axes)
     last = math.prod(SIZES[a] for a in axes) - 1
     return jnp.where(at > 0, 1.0, 0.0).astype(F32), jnp.where(at < last, 1.0, 0.0).astype(F32)
-
-
-def scale_of(table, marks, p):
-    scale = jnp.zeros((PLANES, LANES), F32)
-    for m in range(8):
-        scale = jnp.where(marks == m, table[p, m], scale)
-    return scale * (1.0 / 12.0)
 
 
 def tile(ref, at):
@@ -171,108 +201,106 @@
     return re, im
 
 
-def cells_kernel(table, src, ids, xb, xa, zb, za, receiver, cells, grads, scales):
-    step = pl.program_id(0)
-
-    @pl.when(step == 0)
-    def _():
-        for p in range(3):
-            scales[p * PLANES : (p + 1) * PLANES, :] = scale_of(table, ids[...], p)
-        lane = lane_ids((FIELDS, LANES))
-        x_before, x_after = ends_of(GX)
-        z_before, z_after = ends_of(GZ)
-        halo = zb[...] * z_before + za[...] * z_after
-
-        def at(x, y):
-            if x < 0:
-                return xb[pl.ds((x + 2) * 4 + y, FIELDS, stride=8), :] * x_before
-            if x > 3:
-                return xa[pl.ds((x - 4) * 4 + y, FIELDS, stride=8), :] * x_after
-            if y < 0 or y > 3:
-                return 0.0
-            return src[pl.ds(x * 4 + y, FIELDS, stride=PLANES), :]
-
-        def put(p, plane, value):
-            grads[pl.ds(p * FIELDS * PLANES + plane, FIELDS, stride=PLANES), :] = value
-
-        for x in range(4):
-            for y in range(4):
-                plane = x * 4 + y
-                put(0, plane, 8.0 * (at(x + 1, y) - at(x - 1, y)) - (at(x + 2, y) - at(x - 2, y)))
-                put(1, plane, 8.0 * (at(x, y + 1) - at(x, y - 1)) - (at(x, y + 2) - at(x, y - 2)))
-                mid = at(x, y)
-                ends = pltpu.roll(halo, LANES - 8 * plane, 1) if plane else halo
-                later = pltpu.roll(jnp.where(lane < 1, ends, mid), LANES - 1, 1)
-                sooner = pltpu.roll(jnp.where(lane >= LANES - 1, ends, mid), 1, 1)
-                later_two = pltpu.roll(jnp.where(lane < 2, ends, mid), LANES - 2, 1)
-                sooner_two = pltpu.roll(jnp.where(lane >= LANES - 2, ends, mid), 2, 1)
-                put(2, plane, 8.0 * (later - sooner) - (later_two - sooner_two))
-
-    def grad(p, q, k):
-        return tile(scales, p) * tile(grads, p * FIELDS + step * 6 + q * 2 + k)
-
-    real, imag = [
-        (
-            grad(0, 0, k),
-            grad(1, 1, k),
-            grad(2, 2, k),
-            grad(1, 2, k) + grad(2, 1, k),
-            grad(0, 2, k) + grad(2, 0, k),
-            grad(0, 1, k) + grad(1, 0, k),
-        )
-        for k in range(2)
-    ]
-    for r in range(TENSORS):
-        terms = [
-            (receiver[r, 0, 2 * j], receiver[r, 0, 2 * j + 1], real[j], imag[j]) for j in range(6)
+def cells_kernel(scales, src, xb, xa, from_core, from_cross, receiver, cells, grads, slots, sems):
+    def fetch(b, slot):
+        return pltpu.make_async_copy(receiver.at[:, b], slots.at[slot], sems.at[slot])
+
+    fetch(0, 0).start()
+    lane = lane_ids((FIELDS, LANES))
+    x_before, x_after = ends_of(GX)
+    crossing = jnp.where(lax.axis_index("xhi") != lax.axis_index("core"), 1.0, 0.0).astype(F32)
+    halo = from_core[:FIELDS, :] + from_cross[:FIELDS, :] * crossing
+
+    def at(x, y):
+        if x < 0:
+            return xb[pl.ds((x + 2) * 4 + y, FIELDS, stride=8), :] * x_before
+        if x > 3:
+            return xa[pl.ds((x - 4) * 4 + y, FIELDS, stride=8), :] * x_after
+        if y < 0 or y > 3:
+            return 0.0
+        return src[pl.ds(x * 4 + y, FIELDS, stride=PLANES), :]
+
+    def put(p, plane, value):
+        grads[pl.ds(p * FIELDS * PLANES + plane, FIELDS, stride=PLANES), :] = value
+
+    for x in range(4):
+        for y in range(4):
+            plane = x * 4 + y
+            put(0, plane, 8.0 * (at(x + 1, y) - at(x - 1, y)) - (at(x + 2, y) - at(x - 2, y)))
+            put(1, plane, 8.0 * (at(x, y + 1) - at(x, y - 1)) - (at(x, y + 2) - at(x, y - 2)))
+            mid = at(x, y)
+            ends = pltpu.roll(halo, LANES - 8 * plane, 1) if plane else halo
+            later = pltpu.roll(jnp.where(lane < 1, ends, mid), LANES - 1, 1)
+            sooner = pltpu.roll(jnp.where(lane >= LANES - 1, ends, mid), 1, 1)
+            later_two = pltpu.roll(jnp.where(lane < 2, ends, mid), LANES - 2, 1)
+            sooner_two = pltpu.roll(jnp.where(lane >= LANES - 2, ends, mid), 2, 1)
+            put(2, plane, 8.0 * (later - sooner) - (later_two - sooner_two))
+
+    def body(b, carry):
+        slot = b & 1
+
+        @pl.when(b + 1 < BINS)
+        def _():
+            fetch(b + 1, 1 - slot).start()
+
+        def grad(p, q, k):
+            return tile(scales, p) * tile(grads, p * FIELDS + b * 6 + q * 2 + k)
+
+        real, imag = [
+            (
+                grad(0, 0, k),
+                grad(1, 1, k),
+                grad(2, 2, k),
+                grad(1, 2, k) + grad(2, 1, k),
+                grad(0, 2, k) + grad(2, 0, k),
+                grad(0, 1, k) + grad(1, 0, k),
+            )
+            for k in range(2)
         ]
-        re, im = rows_of((None, None), terms, True)
-        set_tile(cells, r * 32 + step * 2, re)
-        set_tile(cells, r * 32 + step * 2 + 1, im)
+        fetch(b, slot).wait()
+        for r in range(TENSORS):
+            terms = [
+                (slots[slot, r, 2 * j], slots[slot, r, 2 * j + 1], real[j], imag[j])
+                for j in range(6)
+            ]
+            re, im = rows_of((None, None), terms, True)
+            set_tile(cells, r * 32 + b * 2, re)
+            set_tile(cells, r * 32 + b * 2 + 1, im)
+        return carry
+
+    lax.fori_loop(0, BINS, body, 0)
 
 
 def whole(*shape):
     return pl.BlockSpec(shape, lambda b: (0,) * len(shape))
 
 
-def cells_within(table, src, ids, halos, receiver):
-    face = whole(FIELDS * 8, LANES)
-    ends = whole(FIELDS, LANES)
+def cells_within(scales, src, halos, receiver):
     return pl.pallas_call(
         cells_kernel,
-        grid=(BINS,),
         out_shape=jax.ShapeDtypeStruct((ROWS * PLANES, LANES), F32),
-        in_specs=[
-            smem(),
-            whole(FIELDS * PLANES, LANES),
-            whole(PLANES, LANES),
-            face,
-            face,
-            ends,
-            ends,
-            pl.BlockSpec((TENSORS, 1, 12, PLANES, LANES), lambda b: (0, b, 0, 0, 0)),
-        ],
-        out_specs=whole(ROWS * PLANES, LANES),
+        in_specs=[vmem()] * 6 + [hbm()],
+        out_specs=vmem(),
         scratch_shapes=[
             pltpu.VMEM((3 * FIELDS * PLANES, LANES), F32),
-            pltpu.VMEM((3 * PLANES, LANES), F32),
+            pltpu.VMEM((2, TENSORS, 12, PLANES, LANES), BF16),
+            pltpu.SemaphoreType.DMA((2,)),
         ],
         compiler_params=pltpu.CompilerParams(vmem_limit_bytes=VMEM_LIMIT),
         cost_estimate=pl.CostEstimate(
             flops=20_000_000, bytes_accessed=14_000_000, transcendentals=0
         ),
         name="cells_within",
-    )(table, src, ids, *halos, receiver)
+    )(scales, src, *halos, receiver)
 
 
 def gram_kernel(
-    table, ids, yb, ya, within, receiver, s0, s1, s2, s3, keep, send, cells, stats, grads, scales
+    scales, yb, ya, within, receiver, own, from_core, from_cross, from_xhi, keep, send, cells, stats, grads
 ):
     step = pl.program_id(0)
 
     @pl.when(step == 0)
     def _():
-        scales[...] = scale_of(table, ids[...], 1)
         before, after = ends_of(GY)
         for x in range(4):
             b_two, b_one = yb[x * 2] * before, yb[x * 2 + 1] * before
@@ -281,10 +309,17 @@
                 (b_two - 8.0 * b_one, b_one, -a_one, 8.0 * a_one - a_two)
             ):
                 grads[pl.ds(x * 4 + y, FIELDS, stride=PLANES), :] = value
-        stats[...] = merge_sums(merge_sums(s0[...], s1[...]), merge_sums(s2[...], s3[...]))
+
+        def sums_of(value):
+            return jnp.concatenate([value[8 * j : 8 * j + 8, :] for j in range(3)], axis=1)
+
+        stats[...] = merge_sums(
+            merge_sums(sums_of(own[...]), sums_of(from_core[FIELDS:, :])),
+            merge_sums(sums_of(from_cross[FIELDS:, :]), sums_of(from_xhi[...])),
+        )
 
     def grad(q, k):
-        return scales[...] * tile(grads, step * 6 + q * 2 + k)
+        return tile(scales, 1) * tile(grads, step * 6 + q * 2 + k)
 
     real, imag = [(grad(1, k), grad(2, k), grad(0, k)) for k in range(2)]
     for r in range(TENSORS):
@@ -322,7 +357,7 @@
             send[part, :] = jnp.where(upper, full[n], full[n + 3])
 
 
-def gram(table, ids, halos, within, receiver, sums):
+def gram(scales, halos, within, receiver, sums):
     side = whole(8, FIELDS, LANES)
     half = jax.ShapeDtypeStruct((3 * LANES, LANES), F32)
     return pl.pallas_call(
@@ -335,8 +370,7 @@
             jax.ShapeDtypeStruct((8, ROWS), F32),
         ),
         in_specs=[
-            smem(),
-            whole(PLANES, LANES),
+            whole(3 * PLANES, LANES),
             side,
             side,
             whole(ROWS * PLANES, LANES),
@@ -344,23 +378,20 @@
                 (TENSORS, 1, 3, 1, 2, PLANES, LANES), lambda b: (0, b, 0, 1, 0, 0, 0)
             ),
         ]
-        + [whole(8, ROWS)] * 4,
+        + [whole(24, LANES), whole(120, LANES), whole(120, LANES), whole(24, LANES)],
         out_specs=(
             whole(3 * LANES, LANES),
             whole(3 * LANES, LANES),
             whole(ROWS * PLANES, LANES),
             whole(8, ROWS),
         ),
-        scratch_shapes=[
-            pltpu.VMEM((FIELDS * PLANES, LANES), F32),
-            pltpu.VMEM((PLANES, LANES), F32),
-        ],
+        scratch_shapes=[pltpu.VMEM((FIELDS * PLANES, LANES), F32)],
         compiler_params=pltpu.CompilerParams(vmem_limit_bytes=VMEM_LIMIT),
         cost_estimate=pl.CostEstimate(
             flops=1_200_000_000, bytes_accessed=8_000_000, transcendentals=0
         ),
         name="gram",
-    )(table, ids, *halos, within, receiver, *sums)
+    )(scales, *halos, within, receiver, *sums)
 
 
 def chain_kernel(
@@ -532,27 +563,27 @@
     by_pairs = receiver_tensor.reshape(TENSORS, BINS, 3, 2, 2, PLANES, LANES)
     ids = metric_ids.reshape(PLANES, LANES)
     table = metric_table.T
-    x_lo, x_hi, y_lo, y_hi, z_lo, z_hi = pack(src)
-    zb, za = shift(z_hi, GZ, 1), shift(z_lo, GZ, -1)
-    xb, xa = shift(x_hi, GX, 1), shift(x_lo, GX, -1)
-    yb, ya = shift(y_hi, GY, 1), shift(y_lo, GY, -1)
-
     values = observed.transpose(0, 2, 1)
     tensor = receiver_index.reshape(1, -1)
     bins, marks = bin_ids.T, window.T
-    stats = data_sums(values, tensor, bins, marks)
-    near = swap(stats, "core")
-    sums = (stats, near, swap(stats, "xhi"), swap(near, "xhi"))
+    src, x_lo, x_hi, y_lo, y_hi, to_core, to_cross, stats, scales = pack(
+        src, ids, table, values, tensor, bins, marks
+    )
+    from_core = swap(to_core, "core")
+    from_cross = lax.ppermute(to_cross, GZ, [(i, 3 - i) for i in range(4)])
+    from_xhi = swap(stats, "xhi")
+    xb, xa = shift(x_hi, GX, 1), shift(x_lo, GX, -1)
+    yb, ya = shift(y_hi, GY, 1), shift(y_lo, GY, -1)
 
     flat = (FIELDS * 8, LANES)
     within = cells_within(
-        table,
+        scales,
         src.reshape(FIELDS * PLANES, LANES),
-        ids,
-        (xb.reshape(flat), xa.reshape(flat), zb, za),
+        (xb.reshape(flat), xa.reshape(flat), from_core, from_cross),
         receiver,
     )
-    keep, send, cells, stats = gram(table, ids, (yb, ya), within, by_pairs, sums)
+    sums = (stats, from_core, from_cross, from_xhi)
+    keep, send, cells, stats = gram(scales, (yb, ya), within, by_pairs, sums)
     packed = keep + swap(send, "core")
     packed = scatter_sum(packed, PLANE)
     packed = whole_sum(packed, ("z",))

time: 104 us -> 102 us (0.981)
  waiting for transfers between devices: 7.9 us -> 14.7 us
  starting transfers between devices: 25.9 us -> 19.2 us
  local copies, waits for them, and re-layouts: 10.1 us -> 9 us
    ppermute x0 -> x1, waiting for transfers between devices: none -> 11.3 us  [per_device(): from_cross = lax.ppermute(to_cross, GZ, [(i, 3 - i) for i in range(4)])]
    ppermute x6 -> x4, starting transfers between devices: 16.7 us -> 10.2 us  [shift(): lax.ppermute(value, axes, [(i, (i + step) % count) for i in range(count)])]
    ppermute x6 -> x4, waiting for transfers between devices: 4.92 us -> 0.01 us  [shift(): lax.ppermute(value, axes, [(i, (i + step) % count) for i in range(count)])]
    ppermute x5 -> x4, starting transfers between devices: 9.15 us -> 6.29 us  [swap(): return lax.ppermute(value, axis, [(0, 1), (1, 0)])]
    ppermute x0 -> x1, starting transfers between devices: none -> 2.69 us  [per_device(): from_cross = lax.ppermute(to_cross, GZ, [(i, 3 - i) for i in range(4)])]
    unnamed x28 -> x26, local copies, waits for them, and re-layouts: 10.1 us -> 8.98 us
    ppermute x5 -> x4, waiting for transfers between devices: 2.98 us -> 3.4 us  [swap(): return lax.ppermute(value, axis, [(0, 1), (1, 0)])]
    pallas_call x3 -> x2, Pallas kernels: 10.3 us -> 10.4 us  [the longest x1 8.55 us: cells_within(): pl.pallas_call(cells_kernel, out_shape=jax.ShapeDtypeStruct((ROWS * PLANE...]
  transfers between devices with their start and end apart: 11 -> 9, of which waited for: 5 -> 4; matrix products, arithmetic and copies ran while one was open for 0% -> 0% of each run, Pallas kernels for 9% -> 8%
where the time goes in v3:
time: 102 us; the launch traced here: 101 us
  blocking collectives  38.3 us (38%)
  starting transfers between devices  19.2 us (19%)
  Pallas kernels  18.9 us (19%)
  waiting for transfers between devices  14.7 us (14%)
  local copies, waits for them, and re-layouts  9 us (9%)
    all_to_all x3, blocking collectives, exchange(): return lax.all_to_all(value, axes, 0, 0, tiled=True)  38.3 us
    ppermute x1, waiting for transfers between devices, per_device(): from_cross = lax.ppermute(to_cross, GZ, [(i, 3 - i) for i in range(4)])  11.3 us
    ppermute x4, starting transfers between devices, shift(): lax.ppermute(value, axes, [(i, (i + step) % count) for i in range(count)])  10.2 us
    unnamed x26, local copies, waits for them, and re-layouts  8.98 us
    pallas_call x1, Pallas kernels, cells_within(): pl.pallas_call(cells_kernel, out_shape=jax.ShapeDtypeStruct((ROWS * PLANE...  8.55 us
    ppermute x4, starting transfers between devices, swap(): return lax.ppermute(value, axis, [(0, 1), (1, 0)])  6.29 us
    pallas_call x1, Pallas kernels, gram(): pl.pallas_call(gram_kernel, grid=(BINS,), out_shape=(half, half, jax.Shap...  5.23 us
    ppermute x4, waiting for transfers between devices, swap(): return lax.ppermute(value, axis, [(0, 1), (1, 0)])  3.4 us
  transfers between devices with their start and end apart: 9, of which 4 were waited for; matrix products, arithmetic and copies ran while one was open for 0% of the time, Pallas kernels for 8%

profile of v3, /device:TPU:1, one launch (start us, length us, event | category | flops | bytes accessed | tf_op | source)
XLA Modules:
  0.0 101.2 jit_solution(12132549334175241287)
XLA Ops:
  0.6 1.1 %copy-done.2 = f32[16,3,2,4,4,128]{5,4,3,2,1,0:T(4,128)S(1)} copy-done((f32[16,3,2,4,4,128]{5,4,3,2,1,0:T(4,128)S(1)}, f32[16,3,2,4,4,128]{5,4,3,2,1,0:T(4,128)}, u32[]{:S(2)}) %copy-start.2) | copy-done | bytes 786456
  1.8 0.7 copy-done.3
  2.5 0.7 copy-done.5
  3.2 0.7 copy-done.7
  3.9 0.7 copy-done.9
  5.9 1.8 %pack.1 = (f32[96,16,128]{2,1,0:T(8,128)S(1)}, f32[96,8,128]{2,1,0:T(8,128)S(1)}, f32[96,8,128]{2,1,0:T(8,128)S(1)}, f32[8,96,128]{2,1,0:T(8,128)S(1)}, f32[8,96...) custom-call(f32[96,16,128]{2,1,0:T(8,128)S(1)} %bitcast.21, ...), custom_call_target="tpu_custom_call" | custom-call | tf_op jit(solution)/shard_map/pack/pallas_call | solution.py:157
  7.8 2.2 %collective-permute-start.2 = (f32[96,8,128]{2,1,0:T(8,128)S(1)}, f32[96,8,128]{2,1,0:T(8,128)S(1)}, u32[]{:S(2)}, u32[]{:S(2)}) collective-permute-start(f32[96,8,128]{2,1,0:T(8,128)S(1)} %get-tuple-element.23), channel_id=1, source_target_pairs={{0,64},{64,128},{128,192},{192,0},{1,65},{65,129},{129,193},{193,1... | collective-permute-start | bytes 1179656 | tf_op jit(solution)/shard_map/ppermute | solution.py:525
  10.0 1.5 %collective-permute-start.3 = (f32[96,8,128]{2,1,0:T(8,128)S(1)}, f32[96,8,128]{2,1,0:T(8,128)S(1)}, u32[]{:S(2)}, u32[]{:S(2)}) collective-permute-start(f32[96,8,128]{2,1,0:T(8,128)S(1)} %get-tuple-element.24), channel_id=1, source_target_pairs={{0,192},{64,0},{128,64},{192,128},{1,193},{65,1},{129,65},{193,129... | collective-permute-start | bytes 1179656 | tf_op jit(solution)/shard_map/ppermute | solution.py:525
  11.5 1.2 %collective-permute-start = (f32[8,96,128]{2,1,0:T(8,128)S(1)}, f32[8,96,128]{2,1,0:T(8,128)S(1)}, u32[]{:S(2)}, u32[]{:S(2)}) collective-permute-start(f32[8,96,128]{2,1,0:T(8,128)S(1)} %get-tuple-element.20), channel_id=1, source_target_pairs={{0,4},{4,8},{8,12},{12,16},{16,20},{20,24},{24,28},{28,32},{32,36}... | collective-permute-start | bytes 1179656 | tf_op jit(solution)/shard_map/ppermute | solution.py:525
  12.7 5.3 %collective-permute-start.1 = (f32[8,96,128]{2,1,0:T(8,128)S(1)}, f32[8,96,128]{2,1,0:T(8,128)S(1)}, u32[]{:S(2)}, u32[]{:S(2)}) collective-permute-start(f32[8,96,128]{2,1,0:T(8,128)S(1)} %get-tuple-element.21), channel_id=1, source_target_pairs={{0,60},{4,0},{8,4},{12,8},{16,12},{20,16},{24,20},{28,24},{32,28},... | collective-permute-start | bytes 1179656 | tf_op jit(solution)/shard_map/ppermute | solution.py:525
  18.0 1.4 %collective-permute-start.4 = (f32[120,128]{1,0:T(8,128)S(1)}, f32[120,128]{1,0:T(8,128)S(1)}, u32[]{:S(2)}, u32[]{:S(2)}) collective-permute-start(f32[120,128]{1,0:T(8,128)S(1)} %get-tuple-element.25), channel_id=1, source_target_pairs={{0,1},{1,0},{2,3},{3,2},{4,5},{5,4},{6,7},{7,6},{8,9},{9,8},{10,11... | collective-permute-start | bytes 184328 | tf_op jit(solution)/shard_map/ppermute | solution.py:529
  19.4 0.9 collective-permute-done.4.from_core
  20.3 2.7 %collective-permute-start.5 = (f32[120,128]{1,0:T(8,128)S(1)}, f32[120,128]{1,0:T(8,128)S(1)}, u32[]{:S(2)}, u32[]{:S(2)}) collective-permute-start(f32[120,128]{1,0:T(8,128)S(1)} %get-tuple-element.26), channel_id=1, source_target_pairs={{0,3},{1,2},{2,1},{3,0},{4,7},{5,6},{6,5},{7,4},{8,11},{9,10},{10,... | collective-permute-start | bytes 184328 | tf_op jit(solution)/shard_map/ppermute | solution.py:573
  22.9 11.3 %collective-permute-done.5.from_cross = f32[120,128]{1,0:T(8,128)S(1)} collective-permute-done((f32[120,128]{1,0:T(8,128)S(1)}, f32[120,128]{1,0:T(8,128)S(1)}, u32[]{:S(2)}, u32[]{:S(2)}) %collective-permute-start.5) | collective-permute-done | bytes 61472 | tf_op jit(solution)/shard_map/ppermute | solution.py:573
  34.8 3.7 %copy-done = bf16[12,16,6,2,4,4,128]{6,5,4,3,2,1,0:T(4,128)(2,1)S(1)} copy-done((bf16[12,16,6,2,4,4,128]{6,5,4,3,2,1,0:T(4,128)(2,1)S(1)}, bf16[12,16,6,2,4,4,128]{6,5,4,3,2,1,0:T(4,128)(2,1)}, u32[]{:S(2)}) %copy-start) | copy-done | bytes 9437208
  38.5 8.5 %cells_within.1.within = f32[6144,128]{1,0:T(8,128)S(1)} custom-call(f32[48,128]{1,0:T(8,128)S(1)} %get-tuple-element.19.scales, f32[1536,128]{1,0:T(8,128)S(1)} %bitcast.22, f32[768,128]{1,0:T(8,128)S(1)} %bitcast.23, f32[768,128]{1,0:T(8,128)S(1)} %bitcast.24, f32[120,128]{1,0:T(8,128)S(1)} %collective-permute-done.4.from_core, ...), custom_call_target="tpu_custom_call" | custom-call | flops 20000000 | bytes 14000000 | tf_op jit(solution)/shard_map/cells_within/pallas_call | solution.py:279
  47.1 5.2 %gram.1 = (f32[384,128]{1,0:T(8,128)S(1)}, f32[384,128]{1,0:T(8,128)S(1)}, f32[6144,128]{1,0:T(8,128)S(1)}, f32[8,384]{1,0:T(8,128)S(1)}) custom-call(f32[48,128]{1,0:T(8,128)S(1)} %get-tuple-element.19.scales, f32[8,96,128]{2,1,0:T(8,128)S(1)} %collective-permute-done.yb, f32[8,96,128]{2,1,0:T(8,128)S(1)} %collective-permute-done.1.ya, ...), custom_call_target="tpu_custom_call" | custom-call | flops 1200000000 | bytes 8000000 | tf_op jit(solution)/shard_map/gram/pallas_call | solution.py:363
  52.5 1.4 %collective-permute-done.7 = f32[384,128]{1,0:T(8,128)S(1)} collective-permute-done((f32[384,128]{1,0:T(8,128)S(1)}, f32[384,128]{1,0:T(8,128)S(1)}, u32[]{:S(2)}, u32[]{:S(2)}) %collective-permute-start.7) | collective-permute-done | bytes 196640 | tf_op jit(solution)/shard_map/ppermute | solution.py:529
  53.9 12.9 %all_to_all.15 = f32[16,24,128]{2,1,0:T(8,128)S(1)} all-to-all(f32[16,24,128]{2,1,0:T(8,128)S(1)} %bitcast.35), channel_id=1, replica_groups=mesh['y'=4,'z'=8,'xlo'=2,'xhi'=2,'core'=2] {'y','xlo','xhi'}, dimensions={0} | all-to-all | bytes 393216 | tf_op jit(solution)/shard_map/all_to_all | solution.py:533
  66.8 15.2 %all_to_all.16 = f32[8,24,128]{2,1,0:T(8,128)S(1)} all-to-all(f32[8,24,128]{2,1,0:T(8,128)S(1)} %broadcast_in_dim.6), channel_id=1, replica_groups=mesh['y'=4,'z'=8,'xlo'=2,'xhi'=2,'core'=2] {'z'}, dimensions={0} | all-to-all | bytes 196608 | tf_op jit(solution)/shard_map/all_to_all | solution.py:533
  82.1 10.1 %all_to_all.17 = f32[16,24,128]{2,1,0:T(8,128)S(1)} all-to-all(f32[16,24,128]{2,1,0:T(8,128)S(1)} %broadcast_in_dim.7), channel_id=1, replica_groups=mesh['y'=4,'z'=8,'xlo'=2,'xhi'=2,'core'=2] {'y','xlo','xhi'}, dimensions={0} | all-to-all | bytes 393216 | tf_op jit(solution)/shard_map/all_to_all | solution.py:533
  92.3 4.3 %collective-permute-start.8 = (f32[384,128]{1,0:T(8,128)S(1)}, f32[384,128]{1,0:T(8,128)S(1)}, u32[]{:S(2)}, u32[]{:S(2)}) collective-permute-start(f32[384,128]{1,0:T(8,128)S(1)} %bitcast.19), channel_id=1, source_target_pairs={{0,1},{1,0},{2,3},{3,2},{4,5},{5,4},{6,7},{7,6},{8,9},{9,8},{10,11... | collective-permute-start | bytes 589832 | tf_op jit(solution)/shard_map/ppermute | solution.py:529
  96.6 1.1 %collective-permute-done.8.other = f32[384,128]{1,0:T(8,128)S(1)} collective-permute-done((f32[384,128]{1,0:T(8,128)S(1)}, f32[384,128]{1,0:T(8,128)S(1)}, u32[]{:S(2)}, u32[]{:S(2)}) %collective-permute-start.8) | collective-permute-done | bytes 196640 | tf_op jit(solution)/shard_map/ppermute | solution.py:529
  97.7 3.3 %chain.1 = (f32[16,128]{1,0:T(8,128)}, f32[16,128]{1,0:T(8,128)}, f32[2,16,96]{2,1,0:T(8,128)}) custom-call(f32[384,128]{1,0:T(8,128)S(1)} %bitcast.20, f32[384,128]{1,0:T(8,128)S(1)} %collective-permute-done.8.other, f32[8,384]{1,0:T(8,128)S(1)} %get-tuple-element.30.stats, f32[6144,128]{1,0:T(8,128)S(1)} %get-tuple-element.31.cells, ...), custom_call_target="tpu_custom_call" | custom-call | tf_op jit(solution)/shard_map/chain/pallas_call | solution.py:510
  (32 shorter events, 2.1 us)
Async XLA Ops:
  0.6 1.1 %copy-start.2 = (f32[16,3,2,4,4,128]{5,4,3,2,1,0:T(4,128)S(1)}, f32[16,3,2,4,4,128]{5,4,3,2,1,0:T(4,128)}, u32[]{:S(2)}) copy-start(f32[16,3,2,4,4,128]{5,4,3,2,1,0:T(4,128)} %param.8) | copy-start | bytes 2359300
  1.8 0.7 copy-start.3
  2.5 0.7 copy-start.5
  3.2 0.7 copy-start.7
  3.9 0.7 copy-start.9
  4.6 0.7 copy-start.10
  5.3 0.7 copy-start.11
  7.8 27.0 %collective-permute-start.2 = (f32[96,8,128]{2,1,0:T(8,128)S(1)}, f32[96,8,128]{2,1,0:T(8,128)S(1)}, u32[]{:S(2)}, u32[]{:S(2)}) collective-permute-start(f32[96,8,128]{2,1,0:T(8,128)S(1)} %get-tuple-element.23), channel_id=1, source_target_pairs={{0,64},{64,128},{128,192},{192,0},{1,65},{65,129},{129,193},{193,1... | collective-permute-start | bytes 1179656 | tf_op jit(solution)/shard_map/ppermute | solution.py:525
  10.0 24.8 %collective-permute-start.3 = (f32[96,8,128]{2,1,0:T(8,128)S(1)}, f32[96,8,128]{2,1,0:T(8,128)S(1)}, u32[]{:S(2)}, u32[]{:S(2)}) collective-permute-start(f32[96,8,128]{2,1,0:T(8,128)S(1)} %get-tuple-element.24), channel_id=1, source_target_pairs={{0,192},{64,0},{128,64},{192,128},{1,193},{65,1},{129,65},{193,129... | collective-permute-start | bytes 1179656 | tf_op jit(solution)/shard_map/ppermute | solution.py:525
  11.5 35.6 %collective-permute-start = (f32[8,96,128]{2,1,0:T(8,128)S(1)}, f32[8,96,128]{2,1,0:T(8,128)S(1)}, u32[]{:S(2)}, u32[]{:S(2)}) collective-permute-start(f32[8,96,128]{2,1,0:T(8,128)S(1)} %get-tuple-element.20), channel_id=1, source_target_pairs={{0,4},{4,8},{8,12},{12,16},{16,20},{20,24},{24,28},{28,32},{32,36}... | collective-permute-start | bytes 1179656 | tf_op jit(solution)/shard_map/ppermute | solution.py:525
  12.7 34.4 %collective-permute-start.1 = (f32[8,96,128]{2,1,0:T(8,128)S(1)}, f32[8,96,128]{2,1,0:T(8,128)S(1)}, u32[]{:S(2)}, u32[]{:S(2)}) collective-permute-start(f32[8,96,128]{2,1,0:T(8,128)S(1)} %get-tuple-element.21), channel_id=1, source_target_pairs={{0,60},{4,0},{8,4},{12,8},{16,12},{20,16},{24,20},{28,24},{32,28},... | collective-permute-start | bytes 1179656 | tf_op jit(solution)/shard_map/ppermute | solution.py:525
  18.0 2.3 %collective-permute-start.4 = (f32[120,128]{1,0:T(8,128)S(1)}, f32[120,128]{1,0:T(8,128)S(1)}, u32[]{:S(2)}, u32[]{:S(2)}) collective-permute-start(f32[120,128]{1,0:T(8,128)S(1)} %get-tuple-element.25), channel_id=1, source_target_pairs={{0,1},{1,0},{2,3},{3,2},{4,5},{5,4},{6,7},{7,6},{8,9},{9,8},{10,11... | collective-permute-start | bytes 184328 | tf_op jit(solution)/shard_map/ppermute | solution.py:529
  20.3 14.0 %collective-permute-start.5 = (f32[120,128]{1,0:T(8,128)S(1)}, f32[120,128]{1,0:T(8,128)S(1)}, u32[]{:S(2)}, u32[]{:S(2)}) collective-permute-start(f32[120,128]{1,0:T(8,128)S(1)} %get-tuple-element.26), channel_id=1, source_target_pairs={{0,3},{1,2},{2,1},{3,0},{4,7},{5,6},{6,5},{7,4},{8,11},{9,10},{10,... | collective-permute-start | bytes 184328 | tf_op jit(solution)/shard_map/ppermute | solution.py:573
  34.3 12.8 %collective-permute-start.6 = (f32[24,128]{1,0:T(8,128)S(1)}, f32[24,128]{1,0:T(8,128)S(1)}, u32[]{:S(2)}, u32[]{:S(2)}) collective-permute-start(f32[24,128]{1,0:T(8,128)S(1)} %get-tuple-element.27.own), channel_id=1, source_target_pairs={{0,2},{2,0},{1,3},{3,1},{4,6},{6,4},{5,7},{7,5},{8,10},{10,8},{9,1... | collective-permute-start | bytes 36872 | tf_op jit(solution)/shard_map/ppermute | solution.py:529
  34.8 3.7 %copy-start = (bf16[12,16,6,2,4,4,128]{6,5,4,3,2,1,0:T(4,128)(2,1)S(1)}, bf16[12,16,6,2,4,4,128]{6,5,4,3,2,1,0:T(4,128)(2,1)}, u32[]{:S(2)}) copy-start(bf16[12,16,6,2,4,4,128]{6,5,4,3,2,1,0:T(4,128)(2,1)} %param.9) | copy-start | bytes 28311556
  38.5 8.6 %copy-start.1 = (bf16[12,16,6,2,4,4,128]{6,5,4,3,2,1,0:T(4,128)(2,1)S(1)}, bf16[12,16,6,2,4,4,128]{6,5,4,3,2,1,0:T(4,128)(2,1)}, u32[]{:S(2)}) copy-start(bf16[12,16,6,2,4,4,128]{6,5,4,3,2,1,0:T(4,128)(2,1)} %param.9) | copy-start | bytes 28311556
  47.1 50.6 %copy-start.4 = (f32[2,96,16]{1,2,0:T(8,128)S(1)}, f32[2,96,16]{1,2,0:T(8,128)}, u32[]{:S(2)}) copy-start(f32[2,96,16]{1,2,0:T(8,128)} %param.12) | copy-start | bytes 36868
  47.1 50.6 %copy-start.6 = (s32[96,16]{0,1:T(8,128)S(1)}, s32[96,16]{0,1:T(8,128)}, u32[]{:S(2)}) copy-start(s32[96,16]{0,1:T(8,128)} %param.14) | copy-start | bytes 18436
  47.1 50.6 %copy-start.8 = (s32[96,16]{0,1:T(8,128)S(1)}, s32[96,16]{0,1:T(8,128)}, u32[]{:S(2)}) copy-start(s32[96,16]{0,1:T(8,128)} %param.15) | copy-start | bytes 18436
  47.1 50.5 %copy-start.12 = (s32[96]{0:T(128)S(1)}, s32[96]{0:T(128)}, u32[]{:S(2)}) copy-start(s32[96]{0:T(128)} %param.13) | copy-start | bytes 1156
  52.4 1.5 %collective-permute-start.7 = (f32[384,128]{1,0:T(8,128)S(1)}, f32[384,128]{1,0:T(8,128)S(1)}, u32[]{:S(2)}, u32[]{:S(2)}) collective-permute-start(f32[384,128]{1,0:T(8,128)S(1)} %get-tuple-element.29), channel_id=1, source_target_pairs={{0,1},{1,0},{2,3},{3,2},{4,5},{5,4},{6,7},{7,6},{8,9},{9,8},{10,11... | collective-permute-start | bytes 589832 | tf_op jit(solution)/shard_map/ppermute | solution.py:529
  92.3 5.4 %collective-permute-start.8 = (f32[384,128]{1,0:T(8,128)S(1)}, f32[384,128]{1,0:T(8,128)S(1)}, u32[]{:S(2)}, u32[]{:S(2)}) collective-permute-start(f32[384,128]{1,0:T(8,128)S(1)} %bitcast.19), channel_id=1, source_target_pairs={{0,1},{1,0},{2,3},{3,2},{4,5},{5,4},{6,7},{7,6},{8,9},{9,8},{10,11... | collective-permute-start | bytes 589832 | tf_op jit(solution)/shard_map/ppermute | solution.py:529

commit v4 on v3

--- a/solution.py
+++ b/solution.py
@@ -32,6 +32,10 @@
 
 def vmem():
     return pl.BlockSpec(memory_space=pltpu.VMEM)
+
+
+def in_hbm(value):
+    return pltpu.with_memory_space_constraint(value, pltpu.HBM)
 
 
 def hbm():
@@ -174,7 +178,7 @@
         + [pltpu.SemaphoreType.DMA((7,))],
         compiler_params=pltpu.CompilerParams(vmem_limit_bytes=VMEM_LIMIT),
         name="pack",
-    )(*given)
+    )(*(in_hbm(x) for x in given))
 
 
 def ends_of(axes):
@@ -291,7 +295,7 @@
             flops=20_000_000, bytes_accessed=14_000_000, transcendentals=0
         ),
         name="cells_within",
-    )(scales, src, *halos, receiver)
+    )(scales, src, *halos, in_hbm(receiver))
 
 
 def gram_kernel(

time: 102 us -> 98.8 us (0.969)
  local copies, waits for them, and re-layouts: 9 us -> 0.05 us
  Pallas kernels: 18.9 us -> 25.3 us
    unnamed x26 -> x10, local copies, waits for them, and re-layouts: 8.98 us -> 0.03 us
    pallas_call x1, Pallas kernels: 8.55 us -> 14.6 us  [cells_within(): pl.pallas_call(cells_kernel, out_shape=jax.ShapeDtypeStruct((ROWS * PLANE...]
  transfers between devices with their start and end apart: 9 -> 9, of which waited for: 4 -> 4; matrix products, arithmetic and copies ran while one was open for 0% -> 0% of each run, Pallas kernels for 8% -> 15%
where the time goes in v4:
time: 98.8 us; the launch traced here: 98.4 us
  blocking collectives  38.3 us (39%)
  Pallas kernels  25.3 us (26%)
  starting transfers between devices  19.2 us (19%)
  waiting for transfers between devices  14.7 us (15%)
    all_to_all x3, blocking collectives, exchange(): return lax.all_to_all(value, axes, 0, 0, tiled=True)  38.3 us
    pallas_call x1, Pallas kernels, cells_within(): pl.pallas_call(cells_kernel, out_shape=jax.ShapeDtypeStruct((ROWS * PLANE...  14.6 us
    ppermute x1, waiting for transfers between devices, per_device(): from_cross = lax.ppermute(to_cross, GZ, [(i, 3 - i) for i in range(4)])  11.3 us
    ppermute x4, starting transfers between devices, shift(): lax.ppermute(value, axes, [(i, (i + step) % count) for i in range(count)])  10.2 us
    ppermute x4, starting transfers between devices, swap(): return lax.ppermute(value, axis, [(0, 1), (1, 0)])  6.29 us
    pallas_call x1, Pallas kernels, gram(): pl.pallas_call(gram_kernel, grid=(BINS,), out_shape=(half, half, jax.Shap...  5.23 us
    ppermute x4, waiting for transfers between devices, swap(): return lax.ppermute(value, axis, [(0, 1), (1, 0)])  3.4 us
    pallas_call x1, Pallas kernels, chain(): pl.pallas_call(chain_kernel, out_shape=(field, field, jax.ShapeDtypeStruc...  3.32 us
  transfers between devices with their start and end apart: 9, of which 4 were waited for; matrix products, arithmetic and copies ran while one was open for 0% of the time, Pallas kernels for 15%

profile of v4, /device:TPU:1, one launch (start us, length us, event | category | flops | bytes accessed | tf_op | source)
XLA Modules:
  0.0 98.4 jit_solution(11142703493606429429)
XLA Ops:
  0.6 2.2 %pack.1 = (f32[96,16,128]{2,1,0:T(8,128)S(1)}, f32[96,8,128]{2,1,0:T(8,128)S(1)}, f32[96,8,128]{2,1,0:T(8,128)S(1)}, f32[8,96,128]{2,1,0:T(8,128)S(1)}, f32[8,96...) custom-call(f32[96,16,128]{2,1,0:T(8,128)} %bitcast.32, ...), custom_call_target="tpu_custom_call" | custom-call | tf_op jit(solution)/shard_map/pack/pallas_call | solution.py:161
  2.9 2.2 %collective-permute-start.2 = (f32[96,8,128]{2,1,0:T(8,128)S(1)}, f32[96,8,128]{2,1,0:T(8,128)S(1)}, u32[]{:S(2)}, u32[]{:S(2)}) collective-permute-start(f32[96,8,128]{2,1,0:T(8,128)S(1)} %get-tuple-element.23), channel_id=1, source_target_pairs={{0,64},{64,128},{128,192},{192,0},{1,65},{65,129},{129,193},{193,1... | collective-permute-start | bytes 1179656 | tf_op jit(solution)/shard_map/ppermute | solution.py:529
  5.1 1.5 %collective-permute-start.3 = (f32[96,8,128]{2,1,0:T(8,128)S(1)}, f32[96,8,128]{2,1,0:T(8,128)S(1)}, u32[]{:S(2)}, u32[]{:S(2)}) collective-permute-start(f32[96,8,128]{2,1,0:T(8,128)S(1)} %get-tuple-element.24), channel_id=1, source_target_pairs={{0,192},{64,0},{128,64},{192,128},{1,193},{65,1},{129,65},{193,129... | collective-permute-start | bytes 1179656 | tf_op jit(solution)/shard_map/ppermute | solution.py:529
  6.6 1.2 %collective-permute-start = (f32[8,96,128]{2,1,0:T(8,128)S(1)}, f32[8,96,128]{2,1,0:T(8,128)S(1)}, u32[]{:S(2)}, u32[]{:S(2)}) collective-permute-start(f32[8,96,128]{2,1,0:T(8,128)S(1)} %get-tuple-element.20), channel_id=1, source_target_pairs={{0,4},{4,8},{8,12},{12,16},{16,20},{20,24},{24,28},{28,32},{32,36}... | collective-permute-start | bytes 1179656 | tf_op jit(solution)/shard_map/ppermute | solution.py:529
  7.8 5.3 %collective-permute-start.1 = (f32[8,96,128]{2,1,0:T(8,128)S(1)}, f32[8,96,128]{2,1,0:T(8,128)S(1)}, u32[]{:S(2)}, u32[]{:S(2)}) collective-permute-start(f32[8,96,128]{2,1,0:T(8,128)S(1)} %get-tuple-element.21), channel_id=1, source_target_pairs={{0,60},{4,0},{8,4},{12,8},{16,12},{20,16},{24,20},{28,24},{32,28},... | collective-permute-start | bytes 1179656 | tf_op jit(solution)/shard_map/ppermute | solution.py:529
  13.1 1.4 %collective-permute-start.4 = (f32[120,128]{1,0:T(8,128)S(1)}, f32[120,128]{1,0:T(8,128)S(1)}, u32[]{:S(2)}, u32[]{:S(2)}) collective-permute-start(f32[120,128]{1,0:T(8,128)S(1)} %get-tuple-element.25), channel_id=1, source_target_pairs={{0,1},{1,0},{2,3},{3,2},{4,5},{5,4},{6,7},{7,6},{8,9},{9,8},{10,11... | collective-permute-start | bytes 184328 | tf_op jit(solution)/shard_map/ppermute | solution.py:533
  14.5 0.9 collective-permute-done.4.from_core
  15.4 2.7 %collective-permute-start.5 = (f32[120,128]{1,0:T(8,128)S(1)}, f32[120,128]{1,0:T(8,128)S(1)}, u32[]{:S(2)}, u32[]{:S(2)}) collective-permute-start(f32[120,128]{1,0:T(8,128)S(1)} %get-tuple-element.26), channel_id=1, source_target_pairs={{0,3},{1,2},{2,1},{3,0},{4,7},{5,6},{6,5},{7,4},{8,11},{9,10},{10,... | collective-permute-start | bytes 184328 | tf_op jit(solution)/shard_map/ppermute | solution.py:577
  18.1 11.3 %collective-permute-done.5.from_cross = f32[120,128]{1,0:T(8,128)S(1)} collective-permute-done((f32[120,128]{1,0:T(8,128)S(1)}, f32[120,128]{1,0:T(8,128)S(1)}, u32[]{:S(2)}, u32[]{:S(2)}) %collective-permute-start.5) | collective-permute-done | bytes 61472 | tf_op jit(solution)/shard_map/ppermute | solution.py:577
  29.4 0.5 collective-permute-start.6
  29.9 14.6 %cells_within.1.within = f32[6144,128]{1,0:T(8,128)S(1)} custom-call(f32[48,128]{1,0:T(8,128)S(1)} %get-tuple-element.19.scales, f32[1536,128]{1,0:T(8,128)S(1)} %bitcast.21, f32[768,128]{1,0:T(8,128)S(1)} %bitcast.22, f32[768,128]{1,0:T(8,128)S(1)} %bitcast.23, f32[120,128]{1,0:T(8,128)S(1)} %collective-permute-done.4.from_core, ...), custom_call_target="tpu_custom_call" | custom-call | flops 20000000 | bytes 14000000 | tf_op jit(solution)/shard_map/cells_within/pallas_call | solution.py:283
  44.5 0.0 copy-start.1
  44.5 0.0 copy-start.2
  44.5 0.0 copy-start.3
  44.6 0.0 copy-start.4
  44.6 5.2 %gram.1 = (f32[384,128]{1,0:T(8,128)S(1)}, f32[384,128]{1,0:T(8,128)S(1)}, f32[6144,128]{1,0:T(8,128)S(1)}, f32[8,384]{1,0:T(8,128)S(1)}) custom-call(f32[48,128]{1,0:T(8,128)S(1)} %get-tuple-element.19.scales, f32[8,96,128]{2,1,0:T(8,128)S(1)} %collective-permute-done.yb, f32[8,96,128]{2,1,0:T(8,128)S(1)} %collective-permute-done.1.ya, ...), custom_call_target="tpu_custom_call" | custom-call | flops 1200000000 | bytes 8000000 | tf_op jit(solution)/shard_map/gram/pallas_call | solution.py:367
  49.8 0.1 collective-permute-start.7
  49.9 1.4 %collective-permute-done.7 = f32[384,128]{1,0:T(8,128)S(1)} collective-permute-done((f32[384,128]{1,0:T(8,128)S(1)}, f32[384,128]{1,0:T(8,128)S(1)}, u32[]{:S(2)}, u32[]{:S(2)}) %collective-permute-start.7) | collective-permute-done | bytes 196640 | tf_op jit(solution)/shard_map/ppermute | solution.py:533
  51.4 12.9 %all_to_all.15 = f32[16,24,128]{2,1,0:T(8,128)S(1)} all-to-all(f32[16,24,128]{2,1,0:T(8,128)S(1)} %bitcast.33), channel_id=1, replica_groups=mesh['y'=4,'z'=8,'xlo'=2,'xhi'=2,'core'=2] {'y','xlo','xhi'}, dimensions={0} | all-to-all | bytes 393216 | tf_op jit(solution)/shard_map/all_to_all | solution.py:537
  64.3 15.2 %all_to_all.16 = f32[8,24,128]{2,1,0:T(8,128)S(1)} all-to-all(f32[8,24,128]{2,1,0:T(8,128)S(1)} %broadcast_in_dim.6), channel_id=1, replica_groups=mesh['y'=4,'z'=8,'xlo'=2,'xhi'=2,'core'=2] {'z'}, dimensions={0} | all-to-all | bytes 196608 | tf_op jit(solution)/shard_map/all_to_all | solution.py:537
  79.6 10.1 %all_to_all.17 = f32[16,24,128]{2,1,0:T(8,128)S(1)} all-to-all(f32[16,24,128]{2,1,0:T(8,128)S(1)} %broadcast_in_dim.7), channel_id=1, replica_groups=mesh['y'=4,'z'=8,'xlo'=2,'xhi'=2,'core'=2] {'y','xlo','xhi'}, dimensions={0} | all-to-all | bytes 393216 | tf_op jit(solution)/shard_map/all_to_all | solution.py:537
  89.7 4.3 %collective-permute-start.8 = (f32[384,128]{1,0:T(8,128)S(1)}, f32[384,128]{1,0:T(8,128)S(1)}, u32[]{:S(2)}, u32[]{:S(2)}) collective-permute-start(f32[384,128]{1,0:T(8,128)S(1)} %bitcast.19), channel_id=1, source_target_pairs={{0,1},{1,0},{2,3},{3,2},{4,5},{5,4},{6,7},{7,6},{8,9},{9,8},{10,11... | collective-permute-start | bytes 589832 | tf_op jit(solution)/shard_map/ppermute | solution.py:533
  94.0 1.1 %collective-permute-done.8.other = f32[384,128]{1,0:T(8,128)S(1)} collective-permute-done((f32[384,128]{1,0:T(8,128)S(1)}, f32[384,128]{1,0:T(8,128)S(1)}, u32[]{:S(2)}, u32[]{:S(2)}) %collective-permute-start.8) | collective-permute-done | bytes 196640 | tf_op jit(solution)/shard_map/ppermute | solution.py:533
  95.1 3.3 %chain.1 = (f32[16,128]{1,0:T(8,128)}, f32[16,128]{1,0:T(8,128)}, f32[2,16,96]{2,1,0:T(8,128)}) custom-call(f32[384,128]{1,0:T(8,128)S(1)} %bitcast.20, f32[384,128]{1,0:T(8,128)S(1)} %collective-permute-done.8.other, f32[8,384]{1,0:T(8,128)S(1)} %get-tuple-element.30.stats, f32[6144,128]{1,0:T(8,128)S(1)} %get-tuple-element.31.cells, ...), custom_call_target="tpu_custom_call" | custom-call | tf_op jit(solution)/shard_map/chain/pallas_call | solution.py:514
  (16 shorter events, 0.1 us)
Async XLA Ops:
  2.9 27.0 %collective-permute-start.2 = (f32[96,8,128]{2,1,0:T(8,128)S(1)}, f32[96,8,128]{2,1,0:T(8,128)S(1)}, u32[]{:S(2)}, u32[]{:S(2)}) collective-permute-start(f32[96,8,128]{2,1,0:T(8,128)S(1)} %get-tuple-element.23), channel_id=1, source_target_pairs={{0,64},{64,128},{128,192},{192,0},{1,65},{65,129},{129,193},{193,1... | collective-permute-start | bytes 1179656 | tf_op jit(solution)/shard_map/ppermute | solution.py:529
  5.1 24.8 %collective-permute-start.3 = (f32[96,8,128]{2,1,0:T(8,128)S(1)}, f32[96,8,128]{2,1,0:T(8,128)S(1)}, u32[]{:S(2)}, u32[]{:S(2)}) collective-permute-start(f32[96,8,128]{2,1,0:T(8,128)S(1)} %get-tuple-element.24), channel_id=1, source_target_pairs={{0,192},{64,0},{128,64},{192,128},{1,193},{65,1},{129,65},{193,129... | collective-permute-start | bytes 1179656 | tf_op jit(solution)/shard_map/ppermute | solution.py:529
  6.6 37.9 %collective-permute-start = (f32[8,96,128]{2,1,0:T(8,128)S(1)}, f32[8,96,128]{2,1,0:T(8,128)S(1)}, u32[]{:S(2)}, u32[]{:S(2)}) collective-permute-start(f32[8,96,128]{2,1,0:T(8,128)S(1)} %get-tuple-element.20), channel_id=1, source_target_pairs={{0,4},{4,8},{8,12},{12,16},{16,20},{20,24},{24,28},{28,32},{32,36}... | collective-permute-start | bytes 1179656 | tf_op jit(solution)/shard_map/ppermute | solution.py:529
  7.8 36.7 %collective-permute-start.1 = (f32[8,96,128]{2,1,0:T(8,128)S(1)}, f32[8,96,128]{2,1,0:T(8,128)S(1)}, u32[]{:S(2)}, u32[]{:S(2)}) collective-permute-start(f32[8,96,128]{2,1,0:T(8,128)S(1)} %get-tuple-element.21), channel_id=1, source_target_pairs={{0,60},{4,0},{8,4},{12,8},{16,12},{20,16},{24,20},{28,24},{32,28},... | collective-permute-start | bytes 1179656 | tf_op jit(solution)/shard_map/ppermute | solution.py:529
  13.1 2.3 %collective-permute-start.4 = (f32[120,128]{1,0:T(8,128)S(1)}, f32[120,128]{1,0:T(8,128)S(1)}, u32[]{:S(2)}, u32[]{:S(2)}) collective-permute-start(f32[120,128]{1,0:T(8,128)S(1)} %get-tuple-element.25), channel_id=1, source_target_pairs={{0,1},{1,0},{2,3},{3,2},{4,5},{5,4},{6,7},{7,6},{8,9},{9,8},{10,11... | collective-permute-start | bytes 184328 | tf_op jit(solution)/shard_map/ppermute | solution.py:533
  15.4 14.0 %collective-permute-start.5 = (f32[120,128]{1,0:T(8,128)S(1)}, f32[120,128]{1,0:T(8,128)S(1)}, u32[]{:S(2)}, u32[]{:S(2)}) collective-permute-start(f32[120,128]{1,0:T(8,128)S(1)} %get-tuple-element.26), channel_id=1, source_target_pairs={{0,3},{1,2},{2,1},{3,0},{4,7},{5,6},{6,5},{7,4},{8,11},{9,10},{10,... | collective-permute-start | bytes 184328 | tf_op jit(solution)/shard_map/ppermute | solution.py:577
  29.4 15.1 %collective-permute-start.6 = (f32[24,128]{1,0:T(8,128)S(1)}, f32[24,128]{1,0:T(8,128)S(1)}, u32[]{:S(2)}, u32[]{:S(2)}) collective-permute-start(f32[24,128]{1,0:T(8,128)S(1)} %get-tuple-element.27.own), channel_id=1, source_target_pairs={{0,2},{2,0},{1,3},{3,1},{4,6},{6,4},{5,7},{7,5},{8,10},{10,8},{9,1... | collective-permute-start | bytes 36872 | tf_op jit(solution)/shard_map/ppermute | solution.py:533
  29.9 14.6 %copy-start = (bf16[12,16,6,2,4,4,128]{6,5,4,3,2,1,0:T(4,128)(2,1)S(1)}, bf16[12,16,6,2,4,4,128]{6,5,4,3,2,1,0:T(4,128)(2,1)}, u32[]{:S(2)}) copy-start(bf16[12,16,6,2,4,4,128]{6,5,4,3,2,1,0:T(4,128)(2,1)} %param.9) | copy-start | bytes 28311556
  44.5 50.6 %copy-start.1 = (f32[2,96,16]{1,2,0:T(8,128)S(1)}, f32[2,96,16]{1,2,0:T(8,128)}, u32[]{:S(2)}) copy-start(f32[2,96,16]{1,2,0:T(8,128)} %param.12) | copy-start | bytes 36868
  44.5 50.6 %copy-start.2 = (s32[96,16]{0,1:T(8,128)S(1)}, s32[96,16]{0,1:T(8,128)}, u32[]{:S(2)}) copy-start(s32[96,16]{0,1:T(8,128)} %param.14) | copy-start | bytes 18436
  44.5 50.6 %copy-start.3 = (s32[96,16]{0,1:T(8,128)S(1)}, s32[96,16]{0,1:T(8,128)}, u32[]{:S(2)}) copy-start(s32[96,16]{0,1:T(8,128)} %param.15) | copy-start | bytes 18436
  44.6 50.5 %copy-start.4 = (s32[96]{0:T(128)S(1)}, s32[96]{0:T(128)}, u32[]{:S(2)}) copy-start(s32[96]{0:T(128)} %param.13) | copy-start | bytes 1156
  49.8 1.5 %collective-permute-start.7 = (f32[384,128]{1,0:T(8,128)S(1)}, f32[384,128]{1,0:T(8,128)S(1)}, u32[]{:S(2)}, u32[]{:S(2)}) collective-permute-start(f32[384,128]{1,0:T(8,128)S(1)} %get-tuple-element.29), channel_id=1, source_target_pairs={{0,1},{1,0},{2,3},{3,2},{4,5},{5,4},{6,7},{7,6},{8,9},{9,8},{10,11... | collective-permute-start | bytes 589832 | tf_op jit(solution)/shard_map/ppermute | solution.py:533
  89.7 5.4 %collective-permute-start.8 = (f32[384,128]{1,0:T(8,128)S(1)}, f32[384,128]{1,0:T(8,128)S(1)}, u32[]{:S(2)}, u32[]{:S(2)}) collective-permute-start(f32[384,128]{1,0:T(8,128)S(1)} %bitcast.19), channel_id=1, source_target_pairs={{0,1},{1,0},{2,3},{3,2},{4,5},{5,4},{6,7},{7,6},{8,9},{9,8},{10,11... | collective-permute-start | bytes 589832 | tf_op jit(solution)/shard_map/ppermute | solution.py:533

commit v5 on v4

--- a/solution.py
+++ b/solution.py
@@ -100,7 +100,7 @@
 
 def pack_kernel(
     src_in, ids_in, table_in, observed_in, tensor_in, bins_in, window_in,
-    src, x_lo, x_hi, y_lo, y_hi, to_core, to_cross, stats, scales,
+    src, x_lo, x_hi, to_core, to_cross, stats, scales,
     ids, table, observed, tensor, bins, window, sems,
 ):
     copies = [
@@ -139,11 +139,6 @@
     high = jnp.zeros((FIELDS, LANES), F32)
     for plane in range(PLANES):
         value = src[:, plane, :]
-        x, y = divmod(plane, 4)
-        if y < 2:
-            y_lo[x * 2 + y] = value
-        else:
-            y_hi[x * 2 + y - 2] = value
         turned = pltpu.roll(value, 8 * plane, 1) if plane else value
         place = (lane - 8 * plane) & (LANES - 1)
         low = jnp.where(place < 2, turned, low)
@@ -153,9 +148,29 @@
     to_cross[:FIELDS, :] = jnp.where(upper, high, low)
 
 
+def sides_kernel(src, arrived, y_lo, y_hi):
+    for plane in range(PLANES):
+        x, y = divmod(plane, 4)
+        if y < 2:
+            y_lo[x * 2 + y] = src[:, plane, :]
+        else:
+            y_hi[x * 2 + y - 2] = src[:, plane, :]
+
+
+def sides(src, arrived):
+    side = jax.ShapeDtypeStruct((8, FIELDS, LANES), F32)
+    return pl.pallas_call(
+        sides_kernel,
+        out_shape=(side, side),
+        in_specs=[vmem(), vmem()],
+        out_specs=(vmem(), vmem()),
+        compiler_params=pltpu.CompilerParams(vmem_limit_bytes=VMEM_LIMIT),
+        name="sides",
+    )(src, arrived)
+
+
 def pack(src, ids, table, observed, tensor, bins, window):
     face = jax.ShapeDtypeStruct((FIELDS, 8, LANES), F32)
-    side = jax.ShapeDtypeStruct((8, FIELDS, LANES), F32)
     ends = jax.ShapeDtypeStruct((FIELDS + 24, LANES), F32)
     given = (src, ids, table, observed, tensor, bins, window)
     return pl.pallas_call(
@@ -164,15 +179,13 @@
             jax.ShapeDtypeStruct(src.shape, F32),
             face,
             face,
-            side,
-            side,
             ends,
             ends,
             jax.ShapeDtypeStruct((24, LANES), F32),
             jax.ShapeDtypeStruct((3 * PLANES, LANES), F32),
         ),
         in_specs=[hbm()] * 7,
-        out_specs=(vmem(),) * 9,
+        out_specs=(vmem(),) * 7,
         scratch_shapes=[pltpu.VMEM(ids.shape, ids.dtype), pltpu.SMEM(table.shape, table.dtype)]
         + [pltpu.VMEM(x.shape, x.dtype) for x in given[3:]]
         + [pltpu.SemaphoreType.DMA((7,))],
@@ -205,11 +218,12 @@
     return re, im
 
 
-def cells_kernel(scales, src, xb, xa, from_core, from_cross, receiver, cells, grads, slots, sems):
-    def fetch(b, slot):
-        return pltpu.make_async_copy(receiver.at[:, b], slots.at[slot], sems.at[slot])
-
-    fetch(0, 0).start()
+def cells_kernel(scales, src, xb, xa, from_core, from_cross, receiver_in, cells, receiver, grads, sems):
+    def fetch(b):
+        return pltpu.make_async_copy(receiver_in.at[:, b], receiver.at[:, b], sems.at[b])
+
+    for b in range(BINS):
+        fetch(b).start()
     lane = lane_ids((FIELDS, LANES))
     x_before, x_after = ends_of(GX)
     crossing = jnp.where(lax.axis_index("xhi") != lax.axis_index("core"), 1.0, 0.0).astype(F32)
@@ -241,12 +255,6 @@
             put(2, plane, 8.0 * (later - sooner) - (later_two - sooner_two))
 
     def body(b, carry):
-        slot = b & 1
-
-        @pl.when(b + 1 < BINS)
-        def _():
-            fetch(b + 1, 1 - slot).start()
-
         def grad(p, q, k):
             return tile(scales, p) * tile(grads, p * FIELDS + b * 6 + q * 2 + k)
 
@@ -261,10 +269,10 @@
             )
             for k in range(2)
         ]
-        fetch(b, slot).wait()
+        fetch(b).wait()
         for r in range(TENSORS):
             terms = [
-                (slots[slot, r, 2 * j], slots[slot, r, 2 * j + 1], real[j], imag[j])
+                (receiver[r, b, 2 * j], receiver[r, b, 2 * j + 1], real[j], imag[j])
                 for j in range(6)
             ]
             re, im = rows_of((None, None), terms, True)
@@ -275,20 +283,18 @@
     lax.fori_loop(0, BINS, body, 0)
 
 
-def whole(*shape):
-    return pl.BlockSpec(shape, lambda b: (0,) * len(shape))
-
-
 def cells_within(scales, src, halos, receiver):
     return pl.pallas_call(
         cells_kernel,
-        out_shape=jax.ShapeDtypeStruct((ROWS * PLANES, LANES), F32),
+        out_shape=(
+            jax.ShapeDtypeStruct((ROWS * PLANES, LANES), F32),
+            jax.ShapeDtypeStruct(receiver.shape, receiver.dtype),
+        ),
         in_specs=[vmem()] * 6 + [hbm()],
-        out_specs=vmem(),
+        out_specs=(vmem(), vmem()),
         scratch_shapes=[
             pltpu.VMEM((3 * FIELDS * PLANES, LANES), F32),
-            pltpu.VMEM((2, TENSORS, 12, PLANES, LANES), BF16),
-            pltpu.SemaphoreType.DMA((2,)),
+            pltpu.SemaphoreType.DMA((BINS,)),
         ],
         compiler_params=pltpu.CompilerParams(vmem_limit_bytes=VMEM_LIMIT),
         cost_estimate=pl.CostEstimate(
@@ -301,94 +307,75 @@
 def gram_kernel(
     scales, yb, ya, within, receiver, own, from_core, from_cross, from_xhi, keep, send, cells, stats, grads
 ):
-    step = pl.program_id(0)
-
-    @pl.when(step == 0)
-    def _():
-        before, after = ends_of(GY)
-        for x in range(4):
-            b_two, b_one = yb[x * 2] * before, yb[x * 2 + 1] * before
-            a_one, a_two = ya[x * 2] * after, ya[x * 2 + 1] * after
-            for y, value in enumerate(
-                (b_two - 8.0 * b_one, b_one, -a_one, 8.0 * a_one - a_two)
-            ):
-                grads[pl.ds(x * 4 + y, FIELDS, stride=PLANES), :] = value
-
-        def sums_of(value):
-            return jnp.concatenate([value[8 * j : 8 * j + 8, :] for j in range(3)], axis=1)
-
-        stats[...] = merge_sums(
-            merge_sums(sums_of(own[...]), sums_of(from_core[FIELDS:, :])),
-            merge_sums(sums_of(from_cross[FIELDS:, :]), sums_of(from_xhi[...])),
+    before, after = ends_of(GY)
+    for x in range(4):
+        b_two, b_one = yb[x * 2] * before, yb[x * 2 + 1] * before
+        a_one, a_two = ya[x * 2] * after, ya[x * 2 + 1] * after
+        for y, value in enumerate((b_two - 8.0 * b_one, b_one, -a_one, 8.0 * a_one - a_two)):
+            grads[pl.ds(x * 4 + y, FIELDS, stride=PLANES), :] = value
+
+    def body(b, carry):
+        def grad(q, k):
+            return tile(scales, 1) * tile(grads, b * 6 + q * 2 + k)
+
+        real, imag = [(grad(1, k), grad(2, k), grad(0, k)) for k in range(2)]
+        for r in range(TENSORS):
+            at = r * 32 + b * 2
+            terms = [
+                (receiver[r, b, 4 * j + 2], receiver[r, b, 4 * j + 3], real[j], imag[j])
+                for j in range(3)
+            ]
+            re, im = rows_of((tile(within, at), tile(within, at + 1)), terms, False)
+            set_tile(cells, at, re)
+            set_tile(cells, at + 1, im)
+        return carry
+
+    lax.fori_loop(0, BINS, body, 0)
+
+    total = jnp.zeros((ROWS, ROWS), F32)
+    for plane in range(0, PLANES, 2):
+        both = jnp.concatenate(
+            [cells[pl.ds(plane + i, ROWS, stride=PLANES), :] for i in range(2)], axis=1
         )
-
-    def grad(q, k):
-        return tile(scales, 1) * tile(grads, step * 6 + q * 2 + k)
-
-    real, imag = [(grad(1, k), grad(2, k), grad(0, k)) for k in range(2)]
-    for r in range(TENSORS):
-        at = r * 32 + step * 2
-        terms = [
-            (receiver[r, 0, j, 0, 0], receiver[r, 0, j, 0, 1], real[j], imag[j]) for j in range(3)
-        ]
-        re, im = rows_of((tile(within, at), tile(within, at + 1)), terms, False)
-        set_tile(cells, at, re)
-        set_tile(cells, at + 1, im)
-
-    @pl.when(step == BINS - 1)
-    def _():
-        total = jnp.zeros((ROWS, ROWS), F32)
-        for plane in range(0, PLANES, 2):
-            both = jnp.concatenate(
-                [cells[pl.ds(plane + i, ROWS, stride=PLANES), :] for i in range(2)], axis=1
-            )
-            high = both.astype(BF16)
-            low = (both - high.astype(F32)).astype(BF16)
-            left = jnp.concatenate([high, high], axis=1)
-            right = jnp.concatenate([high * BF16(0.5), low], axis=1)
-            total = total + lax.dot_general(
-                left, right, (((1,), (1,)), ((), ())), preferred_element_type=F32
-            )
-
-        def block(i, j):
-            return total[i * LANES : (i + 1) * LANES, j * LANES : (j + 1) * LANES]
-
-        full = [block(i, j) + block(j, i).T for i, j in BLOCKS]
-        upper = lax.axis_index("core") == 1
-        for n in range(3):
-            part = slice(n * LANES, (n + 1) * LANES)
-            keep[part, :] = jnp.where(upper, full[n + 3], full[n])
-            send[part, :] = jnp.where(upper, full[n], full[n + 3])
+        high = both.astype(BF16)
+        low = (both - high.astype(F32)).astype(BF16)
+        left = jnp.concatenate([high, high], axis=1)
+        right = jnp.concatenate([high * BF16(0.5), low], axis=1)
+        total = total + lax.dot_general(
+            left, right, (((1,), (1,)), ((), ())), preferred_element_type=F32
+        )
+
+    def block(i, j):
+        return total[i * LANES : (i + 1) * LANES, j * LANES : (j + 1) * LANES]
+
+    full = [block(i, j) + block(j, i).T for i, j in BLOCKS]
+    upper = lax.axis_index("core") == 1
+    for n in range(3):
+        part = slice(n * LANES, (n + 1) * LANES)
+        keep[part, :] = jnp.where(upper, full[n + 3], full[n])
+        send[part, :] = jnp.where(upper, full[n], full[n + 3])
+
+    def sums_of(value):
+        return jnp.concatenate([value[8 * j : 8 * j + 8, :] for j in range(3)], axis=1)
+
+    stats[...] = merge_sums(
+        merge_sums(sums_of(own[...]), sums_of(from_core[FIELDS:, :])),
+        merge_sums(sums_of(from_cross[FIELDS:, :]), sums_of(from_xhi[...])),
+    )
 
 
 def gram(scales, halos, within, receiver, sums):
-    side = whole(8, FIELDS, LANES)
     half = jax.ShapeDtypeStruct((3 * LANES, LANES), F32)
     return pl.pallas_call(
         gram_kernel,
-        grid=(BINS,),
         out_shape=(
             half,
             half,
             jax.ShapeDtypeStruct((ROWS * PLANES, LANES), F32),
             jax.ShapeDtypeStruct((8, ROWS), F32),
         ),
-        in_specs=[
-            whole(3 * PLANES, LANES),
-            side,
-            side,
-            whole(ROWS * PLANES, LANES),
-            pl.BlockSpec(
-                (TENSORS, 1, 3, 1, 2, PLANES, LANES), lambda b: (0, b, 0, 1, 0, 0, 0)
-            ),
-        ]
-        + [whole(24, LANES), whole(120, LANES), whole(120, LANES), whole(24, LANES)],
-        out_specs=(
-            whole(3 * LANES, LANES),
-            whole(3 * LANES, LANES),
-            whole(ROWS * PLANES, LANES),
-            whole(8, ROWS),
-        ),
+        in_specs=[vmem()] * 9,
+        out_specs=(vmem(),) * 4,
         scratch_shapes=[pltpu.VMEM((FIELDS * PLANES, LANES), F32)],
         compiler_params=pltpu.CompilerParams(vmem_limit_bytes=VMEM_LIMIT),
         cost_estimate=pl.CostEstimate(
@@ -564,30 +551,30 @@
 ):
     src = source_field.reshape(FIELDS, PLANES, LANES)
     receiver = receiver_tensor.reshape(TENSORS, BINS, 12, PLANES, LANES)
-    by_pairs = receiver_tensor.reshape(TENSORS, BINS, 3, 2, 2, PLANES, LANES)
     ids = metric_ids.reshape(PLANES, LANES)
     table = metric_table.T
     values = observed.transpose(0, 2, 1)
     tensor = receiver_index.reshape(1, -1)
     bins, marks = bin_ids.T, window.T
-    src, x_lo, x_hi, y_lo, y_hi, to_core, to_cross, stats, scales = pack(
+    src, x_lo, x_hi, to_core, to_cross, stats, scales = pack(
         src, ids, table, values, tensor, bins, marks
     )
     from_core = swap(to_core, "core")
     from_cross = lax.ppermute(to_cross, GZ, [(i, 3 - i) for i in range(4)])
     from_xhi = swap(stats, "xhi")
     xb, xa = shift(x_hi, GX, 1), shift(x_lo, GX, -1)
+    y_lo, y_hi = sides(src, from_cross)
     yb, ya = shift(y_hi, GY, 1), shift(y_lo, GY, -1)
 
     flat = (FIELDS * 8, LANES)
-    within = cells_within(
+    within, receiver = cells_within(
         scales,
         src.reshape(FIELDS * PLANES, LANES),
         (xb.reshape(flat), xa.reshape(flat), from_core, from_cross),
         receiver,
     )
     sums = (stats, from_core, from_cross, from_xhi)
-    keep, send, cells, stats = gram(scales, (yb, ya), within, by_pairs, sums)
+    keep, send, cells, stats = gram(scales, (yb, ya), within, receiver, sums)
     packed = keep + swap(send, "core")
     packed = scatter_sum(packed, PLANE)
     packed = whole_sum(packed, ("z",))

time: 98.8 us -> 85.8 us (0.87)
  waiting for transfers between devices: 14.7 us -> 5.51 us
  Pallas kernels: 25.3 us -> 18.1 us
  starting transfers between devices: 19.2 us -> 22.7 us
    ppermute x1, waiting for transfers between devices: 11.3 us -> 0.01 us  [per_device(): from_cross = lax.ppermute(to_cross, GZ, [(i, 3 - i) for i in range(4)])]
    pallas_call x2 -> x3, Pallas kernels: 19.8 us -> 12.6 us  [the longest x1 7.75 us: cells_within(): pl.pallas_call(cells_kernel, out_shape=(jax.ShapeDtypeStruct((ROWS * PLAN...]
    ppermute x4, starting transfers between devices: 6.29 us -> 9.06 us  [swap(): return lax.ppermute(value, axis, [(0, 1), (1, 0)])]
    ppermute x4, waiting for transfers between devices: 3.4 us -> 5.5 us  [swap(): return lax.ppermute(value, axis, [(0, 1), (1, 0)])]
    ppermute x1, starting transfers between devices: 2.69 us -> 4.22 us  [per_device(): from_cross = lax.ppermute(to_cross, GZ, [(i, 3 - i) for i in range(4)])]
  transfers between devices with their start and end apart: 9 -> 9, of which waited for: 4 -> 4; matrix products, arithmetic and copies ran while one was open for 0% -> 0% of each run, Pallas kernels for 15% -> 10%
where the time goes in v5:
time: 85.8 us; the launch traced here: 85.6 us
  blocking collectives  38.2 us (45%)
  starting transfers between devices  22.7 us (26%)
  Pallas kernels  18.1 us (21%)
  waiting for transfers between devices  5.51 us (6%)
  between operations  0.89 us (1%)
    all_to_all x3, blocking collectives, exchange(): return lax.all_to_all(value, axes, 0, 0, tiled=True)  38.2 us
    ppermute x4, starting transfers between devices, shift(): lax.ppermute(value, axes, [(i, (i + step) % count) for i in range(count)])  9.43 us
    ppermute x4, starting transfers between devices, swap(): return lax.ppermute(value, axis, [(0, 1), (1, 0)])  9.06 us
    pallas_call x1, Pallas kernels, cells_within(): pl.pallas_call(cells_kernel, out_shape=(jax.ShapeDtypeStruct((ROWS * PLAN...  7.75 us
    ppermute x4, waiting for transfers between devices, swap(): return lax.ppermute(value, axis, [(0, 1), (1, 0)])  5.5 us
    pallas_call x1, Pallas kernels, gram(): pl.pallas_call(gram_kernel, out_shape=(half, half, jax.ShapeDtypeStruct((...  4.42 us
    ppermute x1, starting transfers between devices, per_device(): from_cross = lax.ppermute(to_cross, GZ, [(i, 3 - i) for i in range(4)])  4.22 us
    pallas_call x1, Pallas kernels, chain(): pl.pallas_call(chain_kernel, out_shape=(field, field, jax.ShapeDtypeStruc...  3.32 us
  transfers between devices with their start and end apart: 9, of which 4 were waited for; matrix products, arithmetic and copies ran while one was open for 0% of the time, Pallas kernels for 10%

profile of v5, /device:TPU:1, one launch (start us, length us, event | category | flops | bytes accessed | tf_op | source)
XLA Modules:
  0.0 85.6 jit_solution(8234822937301141384)
XLA Ops:
  0.6 2.2 %pack.1 = (f32[96,16,128]{2,1,0:T(8,128)S(1)}, f32[96,8,128]{2,1,0:T(8,128)S(1)}, f32[96,8,128]{2,1,0:T(8,128)S(1)}, f32[120,128]{1,0:T(8,128)S(1)}, f32[120,128...) custom-call(f32[96,16,128]{2,1,0:T(8,128)} %bitcast.30, s32[16,128]{1,0:T(8,128)} %bitcast.32, ...), custom_call_target="tpu_custom_call" | custom-call | tf_op jit(solution)/shard_map/pack/pallas_call | solution.py:176
  2.9 4.2 %collective-permute-start = (f32[120,128]{1,0:T(8,128)S(1)}, f32[120,128]{1,0:T(8,128)S(1)}, u32[]{:S(2)}, u32[]{:S(2)}) collective-permute-start(f32[120,128]{1,0:T(8,128)S(1)} %get-tuple-element.23), channel_id=1, source_target_pairs={{0,3},{1,2},{2,1},{3,0},{4,7},{5,6},{6,5},{7,4},{8,11},{9,10},{10,... | collective-permute-start | bytes 184328 | tf_op jit(solution)/shard_map/ppermute | solution.py:563
  7.1 1.3 %collective-permute-start.3 = (f32[96,8,128]{2,1,0:T(8,128)S(1)}, f32[96,8,128]{2,1,0:T(8,128)S(1)}, u32[]{:S(2)}, u32[]{:S(2)}) collective-permute-start(f32[96,8,128]{2,1,0:T(8,128)S(1)} %get-tuple-element.26), channel_id=1, source_target_pairs={{0,64},{64,128},{128,192},{192,0},{1,65},{65,129},{129,193},{193,1... | collective-permute-start | bytes 1179656 | tf_op jit(solution)/shard_map/ppermute | solution.py:516
  8.4 1.4 %collective-permute-start.4 = (f32[96,8,128]{2,1,0:T(8,128)S(1)}, f32[96,8,128]{2,1,0:T(8,128)S(1)}, u32[]{:S(2)}, u32[]{:S(2)}) collective-permute-start(f32[96,8,128]{2,1,0:T(8,128)S(1)} %get-tuple-element.27), channel_id=1, source_target_pairs={{0,192},{64,0},{128,64},{192,128},{1,193},{65,1},{129,65},{193,129... | collective-permute-start | bytes 1179656 | tf_op jit(solution)/shard_map/ppermute | solution.py:516
  9.8 0.4 sides.1
  10.2 1.3 %collective-permute-start.1 = (f32[8,96,128]{2,1,0:T(8,128)S(1)}, f32[8,96,128]{2,1,0:T(8,128)S(1)}, u32[]{:S(2)}, u32[]{:S(2)}) collective-permute-start(f32[8,96,128]{2,1,0:T(8,128)S(1)} %get-tuple-element.24), channel_id=1, source_target_pairs={{0,4},{4,8},{8,12},{12,16},{16,20},{20,24},{24,28},{28,32},{32,36}... | collective-permute-start | bytes 1179656 | tf_op jit(solution)/shard_map/ppermute | solution.py:516
  11.6 5.4 %collective-permute-start.2 = (f32[8,96,128]{2,1,0:T(8,128)S(1)}, f32[8,96,128]{2,1,0:T(8,128)S(1)}, u32[]{:S(2)}, u32[]{:S(2)}) collective-permute-start(f32[8,96,128]{2,1,0:T(8,128)S(1)} %get-tuple-element.25), channel_id=1, source_target_pairs={{0,60},{4,0},{8,4},{12,8},{16,12},{20,16},{24,20},{28,24},{32,28},... | collective-permute-start | bytes 1179656 | tf_op jit(solution)/shard_map/ppermute | solution.py:516
  16.9 0.7 collective-permute-start.5
  17.6 0.9 %collective-permute-done.5.from_core = f32[120,128]{1,0:T(8,128)S(1)} collective-permute-done((f32[120,128]{1,0:T(8,128)S(1)}, f32[120,128]{1,0:T(8,128)S(1)}, u32[]{:S(2)}, u32[]{:S(2)}) %collective-permute-start.5) | collective-permute-done | bytes 61472 | tf_op jit(solution)/shard_map/ppermute | solution.py:520
  18.5 2.5 %collective-permute-start.6 = (f32[24,128]{1,0:T(8,128)S(1)}, f32[24,128]{1,0:T(8,128)S(1)}, u32[]{:S(2)}, u32[]{:S(2)}) collective-permute-start(f32[24,128]{1,0:T(8,128)S(1)} %get-tuple-element.31.own), channel_id=1, source_target_pairs={{0,2},{2,0},{1,3},{3,1},{4,6},{6,4},{5,7},{7,5},{8,10},{10,8},{9,1... | collective-permute-start | bytes 36872 | tf_op jit(solution)/shard_map/ppermute | solution.py:520
  21.0 7.8 %cells_within.1 = (f32[6144,128]{1,0:T(8,128)S(1)}, bf16[12,16,12,16,128]{4,3,2,1,0:T(8,128)(2,1)S(1)}) custom-call(f32[48,128]{1,0:T(8,128)S(1)} %get-tuple-element.21.scales, f32[1536,128]{1,0:T(8,128)S(1)} %bitcast.16, f32[768,128]{1,0:T(8,128)S(1)} %bitcast.19, f32[768,128]{1,0:T(8,128)S(1)} %bitcast.20, ...), custom_call_target="tpu_custom_call" | custom-call | flops 20000000 | bytes 14000000 | tf_op jit(solution)/shard_map/cells_within/pallas_call | solution.py:287
  28.7 0.0 copy-start
  28.7 0.0 copy-start.1
  28.7 0.0 copy-start.2
  28.8 2.5 %collective-permute-done.6.from_xhi = f32[24,128]{1,0:T(8,128)S(1)} collective-permute-done((f32[24,128]{1,0:T(8,128)S(1)}, f32[24,128]{1,0:T(8,128)S(1)}, u32[]{:S(2)}, u32[]{:S(2)}) %collective-permute-start.6) | collective-permute-done | bytes 12320 | tf_op jit(solution)/shard_map/ppermute | solution.py:520
  31.2 4.4 %gram.1 = (f32[384,128]{1,0:T(8,128)S(1)}, f32[384,128]{1,0:T(8,128)S(1)}, f32[6144,128]{1,0:T(8,128)S(1)}, f32[8,384]{1,0:T(8,128)S(1)}) custom-call(f32[48,128]{1,0:T(8,128)S(1)} %get-tuple-element.21.scales, f32[8,96,128]{2,1,0:T(8,128)S(1)} %collective-permute-done.1.yb, f32[8,96,128]{2,1,0:T(8,128)S(1)} %collective-permute-done.2.ya, ...), custom_call_target="tpu_custom_call" | custom-call | flops 1200000000 | bytes 8000000 | tf_op jit(solution)/shard_map/gram/pallas_call | solution.py:369
  35.7 1.6 %collective-permute-start.7 = (f32[384,128]{1,0:T(8,128)S(1)}, f32[384,128]{1,0:T(8,128)S(1)}, u32[]{:S(2)}, u32[]{:S(2)}) collective-permute-start(f32[384,128]{1,0:T(8,128)S(1)} %get-tuple-element.33), channel_id=1, source_target_pairs={{0,1},{1,0},{2,3},{3,2},{4,5},{5,4},{6,7},{7,6},{8,9},{9,8},{10,11... | collective-permute-start | bytes 589832 | tf_op jit(solution)/shard_map/ppermute | solution.py:520
  37.3 1.1 %collective-permute-done.7 = f32[384,128]{1,0:T(8,128)S(1)} collective-permute-done((f32[384,128]{1,0:T(8,128)S(1)}, f32[384,128]{1,0:T(8,128)S(1)}, u32[]{:S(2)}, u32[]{:S(2)}) %collective-permute-start.7) | collective-permute-done | bytes 196640 | tf_op jit(solution)/shard_map/ppermute | solution.py:520
  38.4 12.8 %all_to_all.15 = f32[16,24,128]{2,1,0:T(8,128)S(1)} all-to-all(f32[16,24,128]{2,1,0:T(8,128)S(1)} %bitcast.31), channel_id=1, replica_groups=mesh['y'=4,'z'=8,'xlo'=2,'xhi'=2,'core'=2] {'y','xlo','xhi'}, dimensions={0} | all-to-all | bytes 393216 | tf_op jit(solution)/shard_map/all_to_all | solution.py:524
  51.2 15.3 %all_to_all.16 = f32[8,24,128]{2,1,0:T(8,128)S(1)} all-to-all(f32[8,24,128]{2,1,0:T(8,128)S(1)} %broadcast_in_dim.6), channel_id=1, replica_groups=mesh['y'=4,'z'=8,'xlo'=2,'xhi'=2,'core'=2] {'z'}, dimensions={0} | all-to-all | bytes 196608 | tf_op jit(solution)/shard_map/all_to_all | solution.py:524
  66.6 10.1 %all_to_all.17 = f32[16,24,128]{2,1,0:T(8,128)S(1)} all-to-all(f32[16,24,128]{2,1,0:T(8,128)S(1)} %broadcast_in_dim.7), channel_id=1, replica_groups=mesh['y'=4,'z'=8,'xlo'=2,'xhi'=2,'core'=2] {'y','xlo','xhi'}, dimensions={0} | all-to-all | bytes 393216 | tf_op jit(solution)/shard_map/all_to_all | solution.py:524
  76.7 4.3 %collective-permute-start.8 = (f32[384,128]{1,0:T(8,128)S(1)}, f32[384,128]{1,0:T(8,128)S(1)}, u32[]{:S(2)}, u32[]{:S(2)}) collective-permute-start(f32[384,128]{1,0:T(8,128)S(1)} %bitcast.17), channel_id=1, source_target_pairs={{0,1},{1,0},{2,3},{3,2},{4,5},{5,4},{6,7},{7,6},{8,9},{9,8},{10,11... | collective-permute-start | bytes 589832 | tf_op jit(solution)/shard_map/ppermute | solution.py:520
  81.0 1.1 %collective-permute-done.8.other = f32[384,128]{1,0:T(8,128)S(1)} collective-permute-done((f32[384,128]{1,0:T(8,128)S(1)}, f32[384,128]{1,0:T(8,128)S(1)}, u32[]{:S(2)}, u32[]{:S(2)}) %collective-permute-start.8) | collective-permute-done | bytes 196640 | tf_op jit(solution)/shard_map/ppermute | solution.py:520
  82.1 3.3 %chain.1 = (f32[16,128]{1,0:T(8,128)}, f32[16,128]{1,0:T(8,128)}, f32[2,16,96]{2,1,0:T(8,128)}) custom-call(f32[384,128]{1,0:T(8,128)S(1)} %bitcast.18, f32[384,128]{1,0:T(8,128)S(1)} %collective-permute-done.8.other, f32[8,384]{1,0:T(8,128)S(1)} %get-tuple-element.34.stats, f32[6144,128]{1,0:T(8,128)S(1)} %get-tuple-element.35.cells, ...), custom_call_target="tpu_custom_call" | custom-call | tf_op jit(solution)/shard_map/chain/pallas_call | solution.py:501
  (15 shorter events, 0.1 us)
Async XLA Ops:
  2.9 7.0 %collective-permute-start = (f32[120,128]{1,0:T(8,128)S(1)}, f32[120,128]{1,0:T(8,128)S(1)}, u32[]{:S(2)}, u32[]{:S(2)}) collective-permute-start(f32[120,128]{1,0:T(8,128)S(1)} %get-tuple-element.23), channel_id=1, source_target_pairs={{0,3},{1,2},{2,1},{3,0},{4,7},{5,6},{6,5},{7,4},{8,11},{9,10},{10,... | collective-permute-start | bytes 184328 | tf_op jit(solution)/shard_map/ppermute | solution.py:563
  7.1 13.9 %collective-permute-start.3 = (f32[96,8,128]{2,1,0:T(8,128)S(1)}, f32[96,8,128]{2,1,0:T(8,128)S(1)}, u32[]{:S(2)}, u32[]{:S(2)}) collective-permute-start(f32[96,8,128]{2,1,0:T(8,128)S(1)} %get-tuple-element.26), channel_id=1, source_target_pairs={{0,64},{64,128},{128,192},{192,0},{1,65},{65,129},{129,193},{193,1... | collective-permute-start | bytes 1179656 | tf_op jit(solution)/shard_map/ppermute | solution.py:516
  8.4 12.6 %collective-permute-start.4 = (f32[96,8,128]{2,1,0:T(8,128)S(1)}, f32[96,8,128]{2,1,0:T(8,128)S(1)}, u32[]{:S(2)}, u32[]{:S(2)}) collective-permute-start(f32[96,8,128]{2,1,0:T(8,128)S(1)} %get-tuple-element.27), channel_id=1, source_target_pairs={{0,192},{64,0},{128,64},{192,128},{1,193},{65,1},{129,65},{193,129... | collective-permute-start | bytes 1179656 | tf_op jit(solution)/shard_map/ppermute | solution.py:516
  10.2 21.0 %collective-permute-start.1 = (f32[8,96,128]{2,1,0:T(8,128)S(1)}, f32[8,96,128]{2,1,0:T(8,128)S(1)}, u32[]{:S(2)}, u32[]{:S(2)}) collective-permute-start(f32[8,96,128]{2,1,0:T(8,128)S(1)} %get-tuple-element.24), channel_id=1, source_target_pairs={{0,4},{4,8},{8,12},{12,16},{16,20},{20,24},{24,28},{28,32},{32,36}... | collective-permute-start | bytes 1179656 | tf_op jit(solution)/shard_map/ppermute | solution.py:516
  11.6 19.7 %collective-permute-start.2 = (f32[8,96,128]{2,1,0:T(8,128)S(1)}, f32[8,96,128]{2,1,0:T(8,128)S(1)}, u32[]{:S(2)}, u32[]{:S(2)}) collective-permute-start(f32[8,96,128]{2,1,0:T(8,128)S(1)} %get-tuple-element.25), channel_id=1, source_target_pairs={{0,60},{4,0},{8,4},{12,8},{16,12},{20,16},{24,20},{28,24},{32,28},... | collective-permute-start | bytes 1179656 | tf_op jit(solution)/shard_map/ppermute | solution.py:516
  16.9 1.6 %collective-permute-start.5 = (f32[120,128]{1,0:T(8,128)S(1)}, f32[120,128]{1,0:T(8,128)S(1)}, u32[]{:S(2)}, u32[]{:S(2)}) collective-permute-start(f32[120,128]{1,0:T(8,128)S(1)} %get-tuple-element.28), channel_id=1, source_target_pairs={{0,1},{1,0},{2,3},{3,2},{4,5},{5,4},{6,7},{7,6},{8,9},{9,8},{10,11... | collective-permute-start | bytes 184328 | tf_op jit(solution)/shard_map/ppermute | solution.py:520
  18.5 12.7 %collective-permute-start.6 = (f32[24,128]{1,0:T(8,128)S(1)}, f32[24,128]{1,0:T(8,128)S(1)}, u32[]{:S(2)}, u32[]{:S(2)}) collective-permute-start(f32[24,128]{1,0:T(8,128)S(1)} %get-tuple-element.31.own), channel_id=1, source_target_pairs={{0,2},{2,0},{1,3},{3,1},{4,6},{6,4},{5,7},{7,5},{8,10},{10,8},{9,1... | collective-permute-start | bytes 36872 | tf_op jit(solution)/shard_map/ppermute | solution.py:520
  28.7 53.4 %copy-start = (f32[2,96,16]{1,2,0:T(8,128)S(1)}, f32[2,96,16]{1,2,0:T(8,128)}, u32[]{:S(2)}) copy-start(f32[2,96,16]{1,2,0:T(8,128)} %param.12) | copy-start | bytes 36868
  28.7 53.4 %copy-start.1 = (s32[96,16]{0,1:T(8,128)S(1)}, s32[96,16]{0,1:T(8,128)}, u32[]{:S(2)}) copy-start(s32[96,16]{0,1:T(8,128)} %param.14) | copy-start | bytes 18436
  28.7 53.3 %copy-start.2 = (s32[96,16]{0,1:T(8,128)S(1)}, s32[96,16]{0,1:T(8,128)}, u32[]{:S(2)}) copy-start(s32[96,16]{0,1:T(8,128)} %param.15) | copy-start | bytes 18436
  28.8 53.3 %copy-start.3 = (s32[96]{0:T(128)S(1)}, s32[96]{0:T(128)}, u32[]{:S(2)}) copy-start(s32[96]{0:T(128)} %param.13) | copy-start | bytes 1156
  35.7 2.7 %collective-permute-start.7 = (f32[384,128]{1,0:T(8,128)S(1)}, f32[384,128]{1,0:T(8,128)S(1)}, u32[]{:S(2)}, u32[]{:S(2)}) collective-permute-start(f32[384,128]{1,0:T(8,128)S(1)} %get-tuple-element.33), channel_id=1, source_target_pairs={{0,1},{1,0},{2,3},{3,2},{4,5},{5,4},{6,7},{7,6},{8,9},{9,8},{10,11... | collective-permute-start | bytes 589832 | tf_op jit(solution)/shard_map/ppermute | solution.py:520
  76.7 5.4 %collective-permute-start.8 = (f32[384,128]{1,0:T(8,128)S(1)}, f32[384,128]{1,0:T(8,128)S(1)}, u32[]{:S(2)}, u32[]{:S(2)}) collective-permute-start(f32[384,128]{1,0:T(8,128)S(1)} %bitcast.17), channel_id=1, source_target_pairs={{0,1},{1,0},{2,3},{3,2},{4,5},{5,4},{6,7},{7,6},{8,9},{9,8},{10,11... | collective-permute-start | bytes 589832 | tf_op jit(solution)/shard_map/ppermute | solution.py:520

commit v6 on v5

--- a/solution.py
+++ b/solution.py
@@ -100,7 +100,7 @@
 
 def pack_kernel(
     src_in, ids_in, table_in, observed_in, tensor_in, bins_in, window_in,
-    src, x_lo, x_hi, to_core, to_cross, stats, scales,
+    src, y_lo, y_hi, to_core, to_cross, stats, scales,
     ids, table, observed, tensor, bins, window, sems,
 ):
     copies = [
@@ -132,8 +132,17 @@
     to_cross[FIELDS:, :] = sums
 
     copies[0].wait()
-    x_lo[...] = src[:, 0:8, :]
-    x_hi[...] = src[:, 8:16, :]
+    y = lax.broadcasted_iota(jnp.int32, (FIELDS, 8, LANES), 1) & 3
+    first, second = src[:, 0:8, :], src[:, 8:16, :]
+    low = [
+        jnp.where(y == 1, 8.0 * pltpu.roll(half, 1, 1), 0.0) - half for half in (first, second)
+    ]
+    high = [
+        half - jnp.where(y == 2, 8.0 * pltpu.roll(half, 7, 1), 0.0) for half in (first, second)
+    ]
+    y_lo[...] = jnp.where(y < 2, low[1], pltpu.roll(low[0], 2, 1))
+    y_hi[...] = jnp.where(y < 2, pltpu.roll(high[0], 6, 1), high[1])
+
     lane = lane_ids((FIELDS, LANES))
     low = jnp.zeros((FIELDS, LANES), F32)
     high = jnp.zeros((FIELDS, LANES), F32)
@@ -143,30 +152,14 @@
         place = (lane - 8 * plane) & (LANES - 1)
         low = jnp.where(place < 2, turned, low)
         high = jnp.where(place >= LANES - 2, turned, high)
+    place = lane & 7
+    low = jnp.where(place == 1, 8.0 * pltpu.roll(low, 1, 1), 0.0) - low
+    high = high - jnp.where(place == 6, 8.0 * pltpu.roll(high, LANES - 1, 1), 0.0)
+    low = pltpu.roll(low, LANES - 2, 1)
+    high = pltpu.roll(high, 2, 1)
     upper = lax.axis_index("core") == 1
     to_core[:FIELDS, :] = jnp.where(upper, low, high)
     to_cross[:FIELDS, :] = jnp.where(upper, high, low)
-
-
-def sides_kernel(src, arrived, y_lo, y_hi):
-    for plane in range(PLANES):
-        x, y = divmod(plane, 4)
-        if y < 2:
-            y_lo[x * 2 + y] = src[:, plane, :]
-        else:
-            y_hi[x * 2 + y - 2] = src[:, plane, :]
-
-
-def sides(src, arrived):
-    side = jax.ShapeDtypeStruct((8, FIELDS, LANES), F32)
-    return pl.pallas_call(
-        sides_kernel,
-        out_shape=(side, side),
-        in_specs=[vmem(), vmem()],
-        out_specs=(vmem(), vmem()),
-        compiler_params=pltpu.CompilerParams(vmem_limit_bytes=VMEM_LIMIT),
-        name="sides",
-    )(src, arrived)
 
 
 def pack(src, ids, table, observed, tensor, bins, window):
@@ -194,6 +187,27 @@
     )(*(in_hbm(x) for x in given))
 
 
+def strike_kernel(src, part, from_core, x_lo, x_hi, to_cross):
+    to_cross[: FIELDS + 24, :] = part[...]
+    to_cross[FIELDS + 24 :, :] = from_core[FIELDS:, :]
+    first, second = src[:, 0:8, :], src[:, 8:16, :]
+    row = lax.broadcasted_iota(jnp.int32, (FIELDS, 8, LANES), 1)
+    x_lo[...] = jnp.where(row < 4, 0.0, 8.0 * pltpu.roll(first, 4, 1)) - first
+    x_hi[...] = second - jnp.where(row < 4, 8.0 * pltpu.roll(second, 4, 1), 0.0)
+
+
+def strike_faces(src, part, from_core):
+    face = jax.ShapeDtypeStruct((FIELDS, 8, LANES), F32)
+    return pl.pallas_call(
+        strike_kernel,
+        out_shape=(face, face, jax.ShapeDtypeStruct((FIELDS + 48, LANES), F32)),
+        in_specs=[vmem()] * 3,
+        out_specs=(vmem(),) * 3,
+        compiler_params=pltpu.CompilerParams(vmem_limit_bytes=VMEM_LIMIT),
+        name="strike_faces",
+    )(src, part, from_core)
+
+
 def ends_of(axes):
     at = lax.axis_index(axes)
     last = math.prod(SIZES[a] for a in axes) - 1
@@ -208,33 +222,14 @@
     ref[pl.ds(pl.multiple_of(at * PLANES, PLANES), PLANES), :] = value
 
 
-def rows_of(start, strains, first):
-    re, im = start
-    for rec_re, rec_im, real, imag in strains:
-        rec_re, rec_im = rec_re.astype(F32), rec_im.astype(F32)
-        add_re, add_im = rec_re * real - rec_im * imag, rec_re * imag + rec_im * real
-        re, im = (add_re, add_im) if first else (re + add_re, im + add_im)
-        first = False
-    return re, im
-
-
-def cells_kernel(scales, src, xb, xa, from_core, from_cross, receiver_in, cells, receiver, grads, sems):
-    def fetch(b):
-        return pltpu.make_async_copy(receiver_in.at[:, b], receiver.at[:, b], sems.at[b])
-
-    for b in range(BINS):
-        fetch(b).start()
+def within_kernel(src, from_core, receiver_in, grads, receiver, sem):
+    load = pltpu.make_async_copy(receiver_in, receiver, sem)
+    load.start()
     lane = lane_ids((FIELDS, LANES))
-    x_before, x_after = ends_of(GX)
-    crossing = jnp.where(lax.axis_index("xhi") != lax.axis_index("core"), 1.0, 0.0).astype(F32)
-    halo = from_core[:FIELDS, :] + from_cross[:FIELDS, :] * crossing
+    halo = from_core[:FIELDS, :]
 
     def at(x, y):
-        if x < 0:
-            return xb[pl.ds((x + 2) * 4 + y, FIELDS, stride=8), :] * x_before
-        if x > 3:
-            return xa[pl.ds((x - 4) * 4 + y, FIELDS, stride=8), :] * x_after
-        if y < 0 or y > 3:
+        if min(x, y) < 0 or max(x, y) > 3:
             return 0.0
         return src[pl.ds(x * 4 + y, FIELDS, stride=PLANES), :]
 
@@ -247,16 +242,69 @@
             put(0, plane, 8.0 * (at(x + 1, y) - at(x - 1, y)) - (at(x + 2, y) - at(x - 2, y)))
             put(1, plane, 8.0 * (at(x, y + 1) - at(x, y - 1)) - (at(x, y + 2) - at(x, y - 2)))
             mid = at(x, y)
-            ends = pltpu.roll(halo, LANES - 8 * plane, 1) if plane else halo
-            later = pltpu.roll(jnp.where(lane < 1, ends, mid), LANES - 1, 1)
-            sooner = pltpu.roll(jnp.where(lane >= LANES - 1, ends, mid), 1, 1)
-            later_two = pltpu.roll(jnp.where(lane < 2, ends, mid), LANES - 2, 1)
-            sooner_two = pltpu.roll(jnp.where(lane >= LANES - 2, ends, mid), 2, 1)
-            put(2, plane, 8.0 * (later - sooner) - (later_two - sooner_two))
+            later = jnp.where(lane < LANES - 1, pltpu.roll(mid, LANES - 1, 1), 0.0)
+            sooner = jnp.where(lane > 0, pltpu.roll(mid, 1, 1), 0.0)
+            later_two = jnp.where(lane < LANES - 2, pltpu.roll(mid, LANES - 2, 1), 0.0)
+            sooner_two = jnp.where(lane > 1, pltpu.roll(mid, 2, 1), 0.0)
+            value = 8.0 * (later - sooner) - (later_two - sooner_two)
+            put(2, plane, value + ends_at(halo, plane, lane))
+    load.wait()
+
+
+def ends_at(halo, plane, lane):
+    turned = pltpu.roll(halo, LANES - 8 * plane, 1) if plane else halo
+    return jnp.where((lane < 2) | (lane >= LANES - 2), turned, 0.0)
+
+
+def within(src, from_core, receiver):
+    return pl.pallas_call(
+        within_kernel,
+        out_shape=(
+            jax.ShapeDtypeStruct((3 * FIELDS * PLANES, LANES), F32),
+            jax.ShapeDtypeStruct(receiver.shape, receiver.dtype),
+        ),
+        in_specs=[vmem(), vmem(), hbm()],
+        out_specs=(vmem(), vmem()),
+        scratch_shapes=[pltpu.SemaphoreType.DMA],
+        compiler_params=pltpu.CompilerParams(vmem_limit_bytes=VMEM_LIMIT),
+        cost_estimate=pl.CostEstimate(
+            flops=4_000_000, bytes_accessed=14_000_000, transcendentals=0
+        ),
+        name="within",
+    )(src, from_core, in_hbm(receiver))
+
+
+def gram_kernel(
+    scales, grads, receiver, xb, xa, yb, ya, own, from_core, from_cross,
+    keep, send, cells, stats, ends
+):
+    lane = lane_ids((FIELDS, LANES))
+    crossing = jnp.where(lax.axis_index("xhi") != lax.axis_index("core"), 1.0, 0.0).astype(F32)
+    halo = from_cross[:FIELDS, :] * crossing
+    for plane in range(PLANES):
+        ends[pl.ds(plane, FIELDS, stride=PLANES), :] = ends_at(halo, plane, lane)
+    x_before, x_after = ends_of(GX)
+    y_before, y_after = ends_of(GY)
+    low_y = (lax.broadcasted_iota(jnp.int32, (8, LANES), 0) & 3) < 2
 
     def body(b, carry):
         def grad(p, q, k):
-            return tile(scales, p) * tile(grads, p * FIELDS + b * 6 + q * 2 + k)
+            field = b * 6 + q * 2 + k
+            value = tile(grads, p * FIELDS + field)
+            if p == 0:
+                value = value + jnp.concatenate([xb[field] * x_before, xa[field] * x_after], axis=0)
+            elif p == 1:
+                below, above = yb[field] * y_before, ya[field] * y_after
+                value = value + jnp.concatenate(
+                    [
+                        jnp.where(low_y, below, above),
+                        jnp.where(low_y, pltpu.roll(below, 6, 0), pltpu.roll(above, 2, 0)),
+                    ],
+                    axis=0,
+                )
+            else:
+                value = value + tile(ends, field)
+            return tile(scales, p) * value
 
         real, imag = [
             (
@@ -269,65 +317,16 @@
             )
             for k in range(2)
         ]
-        fetch(b).wait()
         for r in range(TENSORS):
-            terms = [
-                (receiver[r, b, 2 * j], receiver[r, b, 2 * j + 1], real[j], imag[j])
-                for j in range(6)
-            ]
-            re, im = rows_of((None, None), terms, True)
+            re = im = None
+            for j in range(6):
+                rec_re = receiver[r, b, 2 * j].astype(F32)
+                rec_im = receiver[r, b, 2 * j + 1].astype(F32)
+                add_re = rec_re * real[j] - rec_im * imag[j]
+                add_im = rec_re * imag[j] + rec_im * real[j]
+                re, im = (re + add_re, im + add_im) if j else (add_re, add_im)
             set_tile(cells, r * 32 + b * 2, re)
             set_tile(cells, r * 32 + b * 2 + 1, im)
-        return carry
-
-    lax.fori_loop(0, BINS, body, 0)
-
-
-def cells_within(scales, src, halos, receiver):
-    return pl.pallas_call(
-        cells_kernel,
-        out_shape=(
-            jax.ShapeDtypeStruct((ROWS * PLANES, LANES), F32),
-            jax.ShapeDtypeStruct(receiver.shape, receiver.dtype),
-        ),
-        in_specs=[vmem()] * 6 + [hbm()],
-        out_specs=(vmem(), vmem()),
-        scratch_shapes=[
-            pltpu.VMEM((3 * FIELDS * PLANES, LANES), F32),
-            pltpu.SemaphoreType.DMA((BINS,)),
-        ],
-        compiler_params=pltpu.CompilerParams(vmem_limit_bytes=VMEM_LIMIT),
-        cost_estimate=pl.CostEstimate(
-            flops=20_000_000, bytes_accessed=14_000_000, transcendentals=0
-        ),
-        name="cells_within",
-    )(scales, src, *halos, in_hbm(receiver))
-
-
-def gram_kernel(
-    scales, yb, ya, within, receiver, own, from_core, from_cross, from_xhi, keep, send, cells, stats, grads
-):
-    before, after = ends_of(GY)
-    for x in range(4):
-        b_two, b_one = yb[x * 2] * before, yb[x * 2 + 1] * before
-        a_one, a_two = ya[x * 2] * after, ya[x * 2 + 1] * after
-        for y, value in enumerate((b_two - 8.0 * b_one, b_one, -a_one, 8.0 * a_one - a_two)):
-            grads[pl.ds(x * 4 + y, FIELDS, stride=PLANES), :] = value
-
-    def body(b, carry):
-        def grad(q, k):
-            return tile(scales, 1) * tile(grads, b * 6 + q * 2 + k)
-
-        real, imag = [(grad(1, k), grad(2, k), grad(0, k)) for k in range(2)]
-        for r in range(TENSORS):
-            at = r * 32 + b * 2
-            terms = [
-                (receiver[r, b, 4 * j + 2], receiver[r, b, 4 * j + 3], real[j], imag[j])
-                for j in range(3)
-            ]
-            re, im = rows_of((tile(within, at), tile(within, at + 1)), terms, False)
-            set_tile(cells, at, re)
-            set_tile(cells, at + 1, im)
         return carry
 
     lax.fori_loop(0, BINS, body, 0)
@@ -360,11 +359,11 @@
 
     stats[...] = merge_sums(
         merge_sums(sums_of(own[...]), sums_of(from_core[FIELDS:, :])),
-        merge_sums(sums_of(from_cross[FIELDS:, :]), sums_of(from_xhi[...])),
+        merge_sums(sums_of(from_cross[FIELDS : FIELDS + 24, :]), sums_of(from_cross[FIELDS + 24 :, :])),
     )
 
 
-def gram(scales, halos, within, receiver, sums):
+def gram(scales, grads, receiver, halos, sums):
     half = jax.ShapeDtypeStruct((3 * LANES, LANES), F32)
     return pl.pallas_call(
         gram_kernel,
@@ -374,7 +373,7 @@
             jax.ShapeDtypeStruct((ROWS * PLANES, LANES), F32),
             jax.ShapeDtypeStruct((8, ROWS), F32),
         ),
-        in_specs=[vmem()] * 9,
+        in_specs=[vmem()] * 10,
         out_specs=(vmem(),) * 4,
         scratch_shapes=[pltpu.VMEM((FIELDS * PLANES, LANES), F32)],
         compiler_params=pltpu.CompilerParams(vmem_limit_bytes=VMEM_LIMIT),
@@ -382,7 +381,7 @@
             flops=1_200_000_000, bytes_accessed=8_000_000, transcendentals=0
         ),
         name="gram",
-    )(scales, *halos, within, receiver, *sums)
+    )(scales, grads, receiver, *halos, *sums)
 
 
 def chain_kernel(
@@ -556,25 +555,18 @@
     values = observed.transpose(0, 2, 1)
     tensor = receiver_index.reshape(1, -1)
     bins, marks = bin_ids.T, window.T
-    src, x_lo, x_hi, to_core, to_cross, stats, scales = pack(
+    src, y_lo, y_hi, to_core, to_cross, stats, scales = pack(
         src, ids, table, values, tensor, bins, marks
     )
+    yb, ya = shift(y_hi, GY, 1), shift(y_lo, GY, -1)
     from_core = swap(to_core, "core")
+    x_lo, x_hi, to_cross = strike_faces(src, to_cross, from_core)
+    xb, xa = shift(x_hi, GX, 1), shift(x_lo, GX, -1)
     from_cross = lax.ppermute(to_cross, GZ, [(i, 3 - i) for i in range(4)])
-    from_xhi = swap(stats, "xhi")
-    xb, xa = shift(x_hi, GX, 1), shift(x_lo, GX, -1)
-    y_lo, y_hi = sides(src, from_cross)
-    yb, ya = shift(y_hi, GY, 1), shift(y_lo, GY, -1)
-
-    flat = (FIELDS * 8, LANES)
-    within, receiver = cells_within(
-        scales,
-        src.reshape(FIELDS * PLANES, LANES),
-        (xb.reshape(flat), xa.reshape(flat), from_core, from_cross),
-        receiver,
-    )
-    sums = (stats, from_core, from_cross, from_xhi)
-    keep, send, cells, stats = gram(scales, (yb, ya), within, receiver, sums)
+
+    grads, receiver = within(src.reshape(FIELDS * PLANES, LANES), from_core, receiver)
+    sums = (stats, from_core, from_cross)
+    keep, send, cells, stats = gram(scales, grads, receiver, (xb, xa, yb, ya), sums)
     packed = keep + swap(send, "core")
     packed = scatter_sum(packed, PLANE)
     packed = whole_sum(packed, ("z",))

time: 85.8 us -> 83.5 us (0.973)
  starting transfers between devices: 22.7 us -> 18.8 us
  waiting for transfers between devices: 5.51 us -> 7.89 us
    ppermute x1, waiting for transfers between devices: 0.01 us -> 5.59 us  [per_device(): from_cross = lax.ppermute(to_cross, GZ, [(i, 3 - i) for i in range(4)])]
    pallas_call x2, Pallas kernels: 8.16 us -> 4.79 us  [the longest x1 4.68 us: within(): pl.pallas_call(within_kernel, out_shape=(jax.ShapeDtypeStruct((3 * FIELDS...]
    ppermute x4 -> x3, waiting for transfers between devices: 5.5 us -> 2.29 us  [swap(): return lax.ppermute(value, axis, [(0, 1), (1, 0)])]
    pallas_call x1, Pallas kernels: 4.42 us -> 6.59 us  [gram(): pl.pallas_call(gram_kernel, out_shape=(half, half, jax.ShapeDtypeStruct((...]
    ppermute x4, starting transfers between devices: 9.43 us -> 7.67 us  [shift(): lax.ppermute(value, axes, [(i, (i + step) % count) for i in range(count)])]
    ppermute x4 -> x3, starting transfers between devices: 9.06 us -> 7.9 us  [swap(): return lax.ppermute(value, axis, [(0, 1), (1, 0)])]
    ppermute x1, starting transfers between devices: 4.22 us -> 3.2 us  [per_device(): from_cross = lax.ppermute(to_cross, GZ, [(i, 3 - i) for i in range(4)])]
  transfers between devices with their start and end apart: 9 -> 8, of which waited for: 4 -> 3; matrix products, arithmetic and copies ran while one was open for 0% -> 0% of each run, Pallas kernels for 10% -> 6%
where the time goes in v6:
time: 83.5 us; the launch traced here: 83.2 us
  blocking collectives  38.2 us (46%)
  starting transfers between devices  18.8 us (23%)
  Pallas kernels  17.5 us (21%)
  waiting for transfers between devices  7.89 us (9%)
    all_to_all x3, blocking collectives, exchange(): return lax.all_to_all(value, axes, 0, 0, tiled=True)  38.2 us
    ppermute x3, starting transfers between devices, swap(): return lax.ppermute(value, axis, [(0, 1), (1, 0)])  7.9 us
    ppermute x4, starting transfers between devices, shift(): lax.ppermute(value, axes, [(i, (i + step) % count) for i in range(count)])  7.67 us
    pallas_call x1, Pallas kernels, gram(): pl.pallas_call(gram_kernel, out_shape=(half, half, jax.ShapeDtypeStruct((...  6.59 us
    ppermute x1, waiting for transfers between devices, per_device(): from_cross = lax.ppermute(to_cross, GZ, [(i, 3 - i) for i in range(4)])  5.59 us
    pallas_call x1, Pallas kernels, within(): pl.pallas_call(within_kernel, out_shape=(jax.ShapeDtypeStruct((3 * FIELDS...  4.68 us
    pallas_call x1, Pallas kernels, chain(): pl.pallas_call(chain_kernel, out_shape=(field, field, jax.ShapeDtypeStruc...  3.32 us
    ppermute x1, starting transfers between devices, per_device(): from_cross = lax.ppermute(to_cross, GZ, [(i, 3 - i) for i in range(4)])  3.2 us
  transfers between devices with their start and end apart: 8, of which 3 were waited for; matrix products, arithmetic and copies ran while one was open for 0% of the time, Pallas kernels for 6%

profile of v6, /device:TPU:1, one launch (start us, length us, event | category | flops | bytes accessed | tf_op | source)
XLA Modules:
  0.0 83.2 jit_solution(14867071446655822816)
XLA Ops:
  0.6 2.8 %pack.1 = (f32[96,16,128]{2,1,0:T(8,128)S(1)}, f32[96,8,128]{2,1,0:T(8,128)S(1)}, f32[96,8,128]{2,1,0:T(8,128)S(1)}, f32[120,128]{1,0:T(8,128)S(1)}, f32[120,128...) custom-call(f32[96,16,128]{2,1,0:T(8,128)} %bitcast.26, s32[16,128]{1,0:T(8,128)} %bitcast.28, ...), custom_call_target="tpu_custom_call" | custom-call | tf_op jit(solution)/shard_map/pack/pallas_call | solution.py:169
  3.4 3.3 %collective-permute-start = (f32[120,128]{1,0:T(8,128)S(1)}, f32[120,128]{1,0:T(8,128)S(1)}, u32[]{:S(2)}, u32[]{:S(2)}) collective-permute-start(f32[120,128]{1,0:T(8,128)S(1)} %get-tuple-element.24), channel_id=1, source_target_pairs={{0,1},{1,0},{2,3},{3,2},{4,5},{5,4},{6,7},{7,6},{8,9},{9,8},{10,11... | collective-permute-start | bytes 184328 | tf_op jit(solution)/shard_map/ppermute | solution.py:519
  6.7 4.8 %collective-permute-start.4 = (f32[96,8,128]{2,1,0:T(8,128)S(1)}, f32[96,8,128]{2,1,0:T(8,128)S(1)}, u32[]{:S(2)}, u32[]{:S(2)}) collective-permute-start(f32[96,8,128]{2,1,0:T(8,128)S(1)} %get-tuple-element.31), channel_id=1, source_target_pairs={{0,60},{4,0},{8,4},{12,8},{16,12},{20,16},{24,20},{28,24},{32,28},... | collective-permute-start | bytes 1179656 | tf_op jit(solution)/shard_map/ppermute | solution.py:515
  11.5 0.0 collective-permute-done.from_core
  11.5 0.1 strike_faces.1
  11.6 1.4 %collective-permute-start.1 = (f32[96,8,128]{2,1,0:T(8,128)S(1)}, f32[96,8,128]{2,1,0:T(8,128)S(1)}, u32[]{:S(2)}, u32[]{:S(2)}) collective-permute-start(f32[96,8,128]{2,1,0:T(8,128)S(1)} %get-tuple-element.28), channel_id=1, source_target_pairs={{0,64},{64,128},{128,192},{192,0},{1,65},{65,129},{129,193},{193,1... | collective-permute-start | bytes 1179656 | tf_op jit(solution)/shard_map/ppermute | solution.py:515
  13.0 1.5 %collective-permute-start.2 = (f32[96,8,128]{2,1,0:T(8,128)S(1)}, f32[96,8,128]{2,1,0:T(8,128)S(1)}, u32[]{:S(2)}, u32[]{:S(2)}) collective-permute-start(f32[96,8,128]{2,1,0:T(8,128)S(1)} %get-tuple-element.29), channel_id=1, source_target_pairs={{0,192},{64,0},{128,64},{192,128},{1,193},{65,1},{129,65},{193,129... | collective-permute-start | bytes 1179656 | tf_op jit(solution)/shard_map/ppermute | solution.py:515
  14.5 3.2 %collective-permute-start.5 = (f32[144,128]{1,0:T(8,128)S(1)}, f32[144,128]{1,0:T(8,128)S(1)}, u32[]{:S(2)}, u32[]{:S(2)}) collective-permute-start(f32[144,128]{1,0:T(8,128)S(1)} %get-tuple-element.33), channel_id=1, source_target_pairs={{0,3},{1,2},{2,1},{3,0},{4,7},{5,6},{6,5},{7,4},{8,11},{9,10},{10,... | collective-permute-start | bytes 221192 | tf_op jit(solution)/shard_map/ppermute | solution.py:565
  17.7 4.7 %within.1 = (f32[4608,128]{1,0:T(8,128)S(1)}, bf16[12,16,12,16,128]{4,3,2,1,0:T(8,128)(2,1)S(1)}) custom-call(f32[1536,128]{1,0:T(8,128)S(1)} %bitcast.14, f32[120,128]{1,0:T(8,128)S(1)} %collective-permute-done.from_core, bf16[12,16,12,16,128]{4,3,2,1,0:T(8,128)(2,1)} %bitcast.25), custom_call_target="tpu_custom_call" | custom-call | flops 4000000 | bytes 14000000 | tf_op jit(solution)/shard_map/within/pallas_call | solution.py:260
  22.4 0.0 copy-start
  22.4 0.0 copy-start.1
  22.5 0.0 copy-start.2
  22.5 0.0 copy-start.3
  22.5 5.6 %collective-permute-done.5.from_cross = f32[144,128]{1,0:T(8,128)S(1)} collective-permute-done((f32[144,128]{1,0:T(8,128)S(1)}, f32[144,128]{1,0:T(8,128)S(1)}, u32[]{:S(2)}, u32[]{:S(2)}) %collective-permute-start.5) | collective-permute-done | bytes 73760 | tf_op jit(solution)/shard_map/ppermute | solution.py:565
  28.1 0.0 collective-permute-done.3.yb
  28.1 6.6 %gram.1 = (f32[384,128]{1,0:T(8,128)S(1)}, f32[384,128]{1,0:T(8,128)S(1)}, f32[6144,128]{1,0:T(8,128)S(1)}, f32[8,384]{1,0:T(8,128)S(1)}) custom-call(f32[48,128]{1,0:T(8,128)S(1)} %get-tuple-element.22.scales, f32[4608,128]{1,0:T(8,128)S(1)} %get-tuple-element.25.grads, bf16[12,16,12,16,128]{4,3,2,1,0:T(8,128)(2,1)S(1)} %get-tuple-element.26.receiver, ...), custom_call_target="tpu_custom_call" | custom-call | flops 1200000000 | bytes 8000000 | tf_op jit(solution)/shard_map/gram/pallas_call | solution.py:368
  34.7 0.3 collective-permute-start.6
  35.0 1.2 %collective-permute-done.6 = f32[384,128]{1,0:T(8,128)S(1)} collective-permute-done((f32[384,128]{1,0:T(8,128)S(1)}, f32[384,128]{1,0:T(8,128)S(1)}, u32[]{:S(2)}, u32[]{:S(2)}) %collective-permute-start.6) | collective-permute-done | bytes 196640 | tf_op jit(solution)/shard_map/ppermute | solution.py:519
  36.2 12.6 %all_to_all.15 = f32[16,24,128]{2,1,0:T(8,128)S(1)} all-to-all(f32[16,24,128]{2,1,0:T(8,128)S(1)} %bitcast.27), channel_id=1, replica_groups=mesh['y'=4,'z'=8,'xlo'=2,'xhi'=2,'core'=2] {'y','xlo','xhi'}, dimensions={0} | all-to-all | bytes 393216 | tf_op jit(solution)/shard_map/all_to_all | solution.py:523
  48.9 15.5 %all_to_all.16 = f32[8,24,128]{2,1,0:T(8,128)S(1)} all-to-all(f32[8,24,128]{2,1,0:T(8,128)S(1)} %broadcast_in_dim.6), channel_id=1, replica_groups=mesh['y'=4,'z'=8,'xlo'=2,'xhi'=2,'core'=2] {'z'}, dimensions={0} | all-to-all | bytes 196608 | tf_op jit(solution)/shard_map/all_to_all | solution.py:523
  64.4 10.1 %all_to_all.17 = f32[16,24,128]{2,1,0:T(8,128)S(1)} all-to-all(f32[16,24,128]{2,1,0:T(8,128)S(1)} %broadcast_in_dim.7), channel_id=1, replica_groups=mesh['y'=4,'z'=8,'xlo'=2,'xhi'=2,'core'=2] {'y','xlo','xhi'}, dimensions={0} | all-to-all | bytes 393216 | tf_op jit(solution)/shard_map/all_to_all | solution.py:523
  74.5 4.3 %collective-permute-start.7 = (f32[384,128]{1,0:T(8,128)S(1)}, f32[384,128]{1,0:T(8,128)S(1)}, u32[]{:S(2)}, u32[]{:S(2)}) collective-permute-start(f32[384,128]{1,0:T(8,128)S(1)} %bitcast.15), channel_id=1, source_target_pairs={{0,1},{1,0},{2,3},{3,2},{4,5},{5,4},{6,7},{7,6},{8,9},{9,8},{10,11... | collective-permute-start | bytes 589832 | tf_op jit(solution)/shard_map/ppermute | solution.py:519
  78.8 1.1 %collective-permute-done.7.other = f32[384,128]{1,0:T(8,128)S(1)} collective-permute-done((f32[384,128]{1,0:T(8,128)S(1)}, f32[384,128]{1,0:T(8,128)S(1)}, u32[]{:S(2)}, u32[]{:S(2)}) %collective-permute-start.7) | collective-permute-done | bytes 196640 | tf_op jit(solution)/shard_map/ppermute | solution.py:519
  79.9 3.3 %chain.1 = (f32[16,128]{1,0:T(8,128)}, f32[16,128]{1,0:T(8,128)}, f32[2,16,96]{2,1,0:T(8,128)}) custom-call(f32[384,128]{1,0:T(8,128)S(1)} %bitcast.16, f32[384,128]{1,0:T(8,128)S(1)} %collective-permute-done.7.other, f32[8,384]{1,0:T(8,128)S(1)} %get-tuple-element.36.stats, f32[6144,128]{1,0:T(8,128)S(1)} %get-tuple-element.37.cells, ...), custom_call_target="tpu_custom_call" | custom-call | tf_op jit(solution)/shard_map/chain/pallas_call | solution.py:500
  (13 shorter events, 0.1 us)
Async XLA Ops:
  3.4 8.1 %collective-permute-start = (f32[120,128]{1,0:T(8,128)S(1)}, f32[120,128]{1,0:T(8,128)S(1)}, u32[]{:S(2)}, u32[]{:S(2)}) collective-permute-start(f32[120,128]{1,0:T(8,128)S(1)} %get-tuple-element.24), channel_id=1, source_target_pairs={{0,1},{1,0},{2,3},{3,2},{4,5},{5,4},{6,7},{7,6},{8,9},{9,8},{10,11... | collective-permute-start | bytes 184328 | tf_op jit(solution)/shard_map/ppermute | solution.py:519
  6.7 21.3 %collective-permute-start.3 = (f32[96,8,128]{2,1,0:T(8,128)S(1)}, f32[96,8,128]{2,1,0:T(8,128)S(1)}, u32[]{:S(2)}, u32[]{:S(2)}) collective-permute-start(f32[96,8,128]{2,1,0:T(8,128)S(1)} %get-tuple-element.30), channel_id=1, source_target_pairs={{0,4},{4,8},{8,12},{12,16},{16,20},{20,24},{24,28},{28,32},{32,36}... | collective-permute-start | bytes 1179656 | tf_op jit(solution)/shard_map/ppermute | solution.py:515
  6.7 21.3 %collective-permute-start.4 = (f32[96,8,128]{2,1,0:T(8,128)S(1)}, f32[96,8,128]{2,1,0:T(8,128)S(1)}, u32[]{:S(2)}, u32[]{:S(2)}) collective-permute-start(f32[96,8,128]{2,1,0:T(8,128)S(1)} %get-tuple-element.31), channel_id=1, source_target_pairs={{0,60},{4,0},{8,4},{12,8},{16,12},{20,16},{24,20},{28,24},{32,28},... | collective-permute-start | bytes 1179656 | tf_op jit(solution)/shard_map/ppermute | solution.py:515
  11.6 16.4 %collective-permute-start.1 = (f32[96,8,128]{2,1,0:T(8,128)S(1)}, f32[96,8,128]{2,1,0:T(8,128)S(1)}, u32[]{:S(2)}, u32[]{:S(2)}) collective-permute-start(f32[96,8,128]{2,1,0:T(8,128)S(1)} %get-tuple-element.28), channel_id=1, source_target_pairs={{0,64},{64,128},{128,192},{192,0},{1,65},{65,129},{129,193},{193,1... | collective-permute-start | bytes 1179656 | tf_op jit(solution)/shard_map/ppermute | solution.py:515
  13.0 15.1 %collective-permute-start.2 = (f32[96,8,128]{2,1,0:T(8,128)S(1)}, f32[96,8,128]{2,1,0:T(8,128)S(1)}, u32[]{:S(2)}, u32[]{:S(2)}) collective-permute-start(f32[96,8,128]{2,1,0:T(8,128)S(1)} %get-tuple-element.29), channel_id=1, source_target_pairs={{0,192},{64,0},{128,64},{192,128},{1,193},{65,1},{129,65},{193,129... | collective-permute-start | bytes 1179656 | tf_op jit(solution)/shard_map/ppermute | solution.py:515
  14.5 13.5 %collective-permute-start.5 = (f32[144,128]{1,0:T(8,128)S(1)}, f32[144,128]{1,0:T(8,128)S(1)}, u32[]{:S(2)}, u32[]{:S(2)}) collective-permute-start(f32[144,128]{1,0:T(8,128)S(1)} %get-tuple-element.33), channel_id=1, source_target_pairs={{0,3},{1,2},{2,1},{3,0},{4,7},{5,6},{6,5},{7,4},{8,11},{9,10},{10,... | collective-permute-start | bytes 221192 | tf_op jit(solution)/shard_map/ppermute | solution.py:565
  22.4 57.5 %copy-start = (f32[2,96,16]{1,2,0:T(8,128)S(1)}, f32[2,96,16]{1,2,0:T(8,128)}, u32[]{:S(2)}) copy-start(f32[2,96,16]{1,2,0:T(8,128)} %param.12) | copy-start | bytes 36868
  22.4 57.4 %copy-start.1 = (s32[96,16]{0,1:T(8,128)S(1)}, s32[96,16]{0,1:T(8,128)}, u32[]{:S(2)}) copy-start(s32[96,16]{0,1:T(8,128)} %param.14) | copy-start | bytes 18436
  22.5 57.4 %copy-start.2 = (s32[96,16]{0,1:T(8,128)S(1)}, s32[96,16]{0,1:T(8,128)}, u32[]{:S(2)}) copy-start(s32[96,16]{0,1:T(8,128)} %param.15) | copy-start | bytes 18436
  22.5 57.4 %copy-start.3 = (s32[96]{0:T(128)S(1)}, s32[96]{0:T(128)}, u32[]{:S(2)}) copy-start(s32[96]{0:T(128)} %param.13) | copy-start | bytes 1156
  34.7 1.5 %collective-permute-start.6 = (f32[384,128]{1,0:T(8,128)S(1)}, f32[384,128]{1,0:T(8,128)S(1)}, u32[]{:S(2)}, u32[]{:S(2)}) collective-permute-start(f32[384,128]{1,0:T(8,128)S(1)} %get-tuple-element.35), channel_id=1, source_target_pairs={{0,1},{1,0},{2,3},{3,2},{4,5},{5,4},{6,7},{7,6},{8,9},{9,8},{10,11... | collective-permute-start | bytes 589832 | tf_op jit(solution)/shard_map/ppermute | solution.py:519
  74.5 5.3 %collective-permute-start.7 = (f32[384,128]{1,0:T(8,128)S(1)}, f32[384,128]{1,0:T(8,128)S(1)}, u32[]{:S(2)}, u32[]{:S(2)}) collective-permute-start(f32[384,128]{1,0:T(8,128)S(1)} %bitcast.15), channel_id=1, source_target_pairs={{0,1},{1,0},{2,3},{3,2},{4,5},{5,4},{6,7},{7,6},{8,9},{9,8},{10,11... | collective-permute-start | bytes 589832 | tf_op jit(solution)/shard_map/ppermute | solution.py:519

commit v7 on v6

--- a/solution.py
+++ b/solution.py
@@ -222,9 +222,12 @@
     ref[pl.ds(pl.multiple_of(at * PLANES, PLANES), PLANES), :] = value
 
 
-def within_kernel(src, from_core, receiver_in, grads, receiver, sem):
-    load = pltpu.make_async_copy(receiver_in, receiver, sem)
-    load.start()
+def within_kernel(scales, src, from_core, receiver_in, strain, receiver, grads, slots, sems):
+    def fetch(b):
+        return pltpu.make_async_copy(receiver_in.at[:, b], slots.at[b], sems.at[b])
+
+    for b in range(BINS):
+        fetch(b).start()
     lane = lane_ids((FIELDS, LANES))
     halo = from_core[:FIELDS, :]
 
@@ -248,7 +251,29 @@
             sooner_two = jnp.where(lane > 1, pltpu.roll(mid, 2, 1), 0.0)
             value = 8.0 * (later - sooner) - (later_two - sooner_two)
             put(2, plane, value + ends_at(halo, plane, lane))
-    load.wait()
+
+    def body(b, carry):
+        def grad(p, q, k):
+            return tile(scales, p) * tile(grads, p * FIELDS + b * 6 + q * 2 + k)
+
+        for k in range(2):
+            for j, value in enumerate(
+                (
+                    grad(0, 0, k),
+                    grad(1, 1, k),
+                    grad(2, 2, k),
+                    grad(1, 2, k) + grad(2, 1, k),
+                    grad(0, 2, k) + grad(2, 0, k),
+                    grad(0, 1, k) + grad(1, 0, k),
+                )
+            ):
+                set_tile(strain, b * 12 + j * 2 + k, value)
+        fetch(b).wait()
+        for r in range(TENSORS):
+            receiver[r, b] = slots[b, r].astype(F32)
+        return carry
+
+    lax.fori_loop(0, BINS, body, 0)
 
 
 def ends_at(halo, plane, lane):
@@ -256,26 +281,30 @@
     return jnp.where((lane < 2) | (lane >= LANES - 2), turned, 0.0)
 
 
-def within(src, from_core, receiver):
+def within(scales, src, from_core, receiver):
     return pl.pallas_call(
         within_kernel,
         out_shape=(
-            jax.ShapeDtypeStruct((3 * FIELDS * PLANES, LANES), F32),
-            jax.ShapeDtypeStruct(receiver.shape, receiver.dtype),
+            jax.ShapeDtypeStruct((BINS * 12 * PLANES, LANES), F32),
+            jax.ShapeDtypeStruct(receiver.shape, F32),
         ),
-        in_specs=[vmem(), vmem(), hbm()],
+        in_specs=[vmem(), vmem(), vmem(), hbm()],
         out_specs=(vmem(), vmem()),
-        scratch_shapes=[pltpu.SemaphoreType.DMA],
+        scratch_shapes=[
+            pltpu.VMEM((3 * FIELDS * PLANES, LANES), F32),
+            pltpu.VMEM((BINS, TENSORS, 12, PLANES, LANES), BF16),
+            pltpu.SemaphoreType.DMA((BINS,)),
+        ],
         compiler_params=pltpu.CompilerParams(vmem_limit_bytes=VMEM_LIMIT),
         cost_estimate=pl.CostEstimate(
             flops=4_000_000, bytes_accessed=14_000_000, transcendentals=0
         ),
         name="within",
-    )(src, from_core, in_hbm(receiver))
+    )(scales, src, from_core, in_hbm(receiver))
 
 
 def gram_kernel(
-    scales, grads, receiver, xb, xa, yb, ya, own, from_core, from_cross,
+    scales, within, receiver, xb, xa, yb, ya, own, from_core, from_cross,
     keep, send, cells, stats, ends
 ):
     lane = lane_ids((FIELDS, LANES))
@@ -286,42 +315,43 @@
     x_before, x_after = ends_of(GX)
     y_before, y_after = ends_of(GY)
     low_y = (lax.broadcasted_iota(jnp.int32, (8, LANES), 0) & 3) < 2
+    side = jnp.where(low_y, y_before, y_after)
+    scale_x = (scales[0:8, :] * x_before, scales[8:16, :] * x_after)
+    scale_y = (scales[16:24, :] * side, scales[24:32, :] * side)
+    scale_z = tile(scales, 2)
 
     def body(b, carry):
-        def grad(p, q, k):
-            field = b * 6 + q * 2 + k
-            value = tile(grads, p * FIELDS + field)
-            if p == 0:
-                value = value + jnp.concatenate([xb[field] * x_before, xa[field] * x_after], axis=0)
-            elif p == 1:
-                below, above = yb[field] * y_before, ya[field] * y_after
-                value = value + jnp.concatenate(
-                    [
-                        jnp.where(low_y, below, above),
-                        jnp.where(low_y, pltpu.roll(below, 6, 0), pltpu.roll(above, 2, 0)),
-                    ],
-                    axis=0,
+        def from_x(field):
+            return jnp.concatenate([scale_x[0] * xb[field], scale_x[1] * xa[field]], axis=0)
+
+        def from_y(field):
+            below, above = yb[field], ya[field]
+            first = jnp.where(low_y, below, above)
+            second = jnp.where(low_y, pltpu.roll(below, 6, 0), pltpu.roll(above, 2, 0))
+            return jnp.concatenate([scale_y[0] * first, scale_y[1] * second], axis=0)
+
+        def from_z(field):
+            return scale_z * tile(ends, field)
+
+        strain = []
+        for k in range(2):
+            inner = [tile(within, b * 12 + j * 2 + k) for j in range(6)]
+            ux, uy, uz = [b * 6 + q * 2 + k for q in range(3)]
+            strain.append(
+                (
+                    inner[0] + from_x(ux),
+                    inner[1] + from_y(uy),
+                    inner[2] + from_z(uz),
+                    inner[3] + (from_y(uz) + from_z(uy)),
+                    inner[4] + (from_x(uz) + from_z(ux)),
+                    inner[5] + (from_x(uy) + from_y(ux)),
                 )
-            else:
-                value = value + tile(ends, field)
-            return tile(scales, p) * value
-
-        real, imag = [
-            (
-                grad(0, 0, k),
-                grad(1, 1, k),
-                grad(2, 2, k),
-                grad(1, 2, k) + grad(2, 1, k),
-                grad(0, 2, k) + grad(2, 0, k),
-                grad(0, 1, k) + grad(1, 0, k),
             )
-            for k in range(2)
-        ]
+        real, imag = strain
         for r in range(TENSORS):
             re = im = None
             for j in range(6):
-                rec_re = receiver[r, b, 2 * j].astype(F32)
-                rec_im = receiver[r, b, 2 * j + 1].astype(F32)
+                rec_re, rec_im = receiver[r, b, 2 * j], receiver[r, b, 2 * j + 1]
                 add_re = rec_re * real[j] - rec_im * imag[j]
                 add_im = rec_re * imag[j] + rec_im * real[j]
                 re, im = (re + add_re, im + add_im) if j else (add_re, add_im)
@@ -363,7 +393,7 @@
     )
 
 
-def gram(scales, grads, receiver, halos, sums):
+def gram(scales, within, receiver, halos, sums):
     half = jax.ShapeDtypeStruct((3 * LANES, LANES), F32)
     return pl.pallas_call(
         gram_kernel,
@@ -381,7 +411,7 @@
             flops=1_200_000_000, bytes_accessed=8_000_000, transcendentals=0
         ),
         name="gram",
-    )(scales, grads, receiver, *halos, *sums)
+    )(scales, within, receiver, *halos, *sums)
 
 
 def chain_kernel(
@@ -564,9 +594,9 @@
     xb, xa = shift(x_hi, GX, 1), shift(x_lo, GX, -1)
     from_cross = lax.ppermute(to_cross, GZ, [(i, 3 - i) for i in range(4)])
 
-    grads, receiver = within(src.reshape(FIELDS * PLANES, LANES), from_core, receiver)
+    strain, receiver = within(scales, src.reshape(FIELDS * PLANES, LANES), from_core, receiver)
     sums = (stats, from_core, from_cross)
-    keep, send, cells, stats = gram(scales, grads, receiver, (xb, xa, yb, ya), sums)
+    keep, send, cells, stats = gram(scales, strain, receiver, (xb, xa, yb, ya), sums)
     packed = keep + swap(send, "core")
     packed = scatter_sum(packed, PLANE)
     packed = whole_sum(packed, ("z",))

time: 83.5 us -> 82.8 us (level)
  no operation moved by 1% of the time
where the time goes in v7:
time: 82.8 us; the launch traced here: 82.6 us
  blocking collectives  38.2 us (46%)
  starting transfers between devices  18.8 us (23%)
  Pallas kernels  17 us (21%)
  waiting for transfers between devices  7.7 us (9%)
    all_to_all x3, blocking collectives, exchange(): return lax.all_to_all(value, axes, 0, 0, tiled=True)  38.2 us
    ppermute x3, starting transfers between devices, swap(): return lax.ppermute(value, axis, [(0, 1), (1, 0)])  7.9 us
    ppermute x4, starting transfers between devices, shift(): lax.ppermute(value, axes, [(i, (i + step) % count) for i in range(count)])  7.67 us
    pallas_call x1, Pallas kernels, gram(): pl.pallas_call(gram_kernel, out_shape=(half, half, jax.ShapeDtypeStruct((...  5.87 us
    ppermute x1, waiting for transfers between devices, per_device(): from_cross = lax.ppermute(to_cross, GZ, [(i, 3 - i) for i in range(4)])  5.39 us
    pallas_call x1, Pallas kernels, within(): pl.pallas_call(within_kernel, out_shape=(jax.ShapeDtypeStruct((BINS * 12...  4.92 us
    pallas_call x1, Pallas kernels, chain(): pl.pallas_call(chain_kernel, out_shape=(field, field, jax.ShapeDtypeStruc...  3.32 us
    ppermute x1, starting transfers between devices, per_device(): from_cross = lax.ppermute(to_cross, GZ, [(i, 3 - i) for i in range(4)])  3.2 us
  transfers between devices with their start and end apart: 8, of which 3 were waited for; matrix products, arithmetic and copies ran while one was open for 0% of the time, Pallas kernels for 6%

profile of v7, /device:TPU:1, one launch (start us, length us, event | category | flops | bytes accessed | tf_op | source)
XLA Modules:
  0.0 82.6 jit_solution(4101203195289039850)
XLA Ops:
  0.6 2.8 %pack.1 = (f32[96,16,128]{2,1,0:T(8,128)S(1)}, f32[96,8,128]{2,1,0:T(8,128)S(1)}, f32[96,8,128]{2,1,0:T(8,128)S(1)}, f32[120,128]{1,0:T(8,128)S(1)}, f32[120,128...) custom-call(f32[96,16,128]{2,1,0:T(8,128)} %bitcast.26, s32[16,128]{1,0:T(8,128)} %bitcast.28, ...), custom_call_target="tpu_custom_call" | custom-call | tf_op jit(solution)/shard_map/pack/pallas_call | solution.py:169
  3.4 3.3 %collective-permute-start = (f32[120,128]{1,0:T(8,128)S(1)}, f32[120,128]{1,0:T(8,128)S(1)}, u32[]{:S(2)}, u32[]{:S(2)}) collective-permute-start(f32[120,128]{1,0:T(8,128)S(1)} %get-tuple-element.24), channel_id=1, source_target_pairs={{0,1},{1,0},{2,3},{3,2},{4,5},{5,4},{6,7},{7,6},{8,9},{9,8},{10,11... | collective-permute-start | bytes 184328 | tf_op jit(solution)/shard_map/ppermute | solution.py:549
  6.7 4.8 %collective-permute-start.4 = (f32[96,8,128]{2,1,0:T(8,128)S(1)}, f32[96,8,128]{2,1,0:T(8,128)S(1)}, u32[]{:S(2)}, u32[]{:S(2)}) collective-permute-start(f32[96,8,128]{2,1,0:T(8,128)S(1)} %get-tuple-element.31), channel_id=1, source_target_pairs={{0,60},{4,0},{8,4},{12,8},{16,12},{20,16},{24,20},{28,24},{32,28},... | collective-permute-start | bytes 1179656 | tf_op jit(solution)/shard_map/ppermute | solution.py:545
  11.5 0.0 collective-permute-done.from_core
  11.5 0.1 strike_faces.1
  11.6 1.4 %collective-permute-start.1 = (f32[96,8,128]{2,1,0:T(8,128)S(1)}, f32[96,8,128]{2,1,0:T(8,128)S(1)}, u32[]{:S(2)}, u32[]{:S(2)}) collective-permute-start(f32[96,8,128]{2,1,0:T(8,128)S(1)} %get-tuple-element.28), channel_id=1, source_target_pairs={{0,64},{64,128},{128,192},{192,0},{1,65},{65,129},{129,193},{193,1... | collective-permute-start | bytes 1179656 | tf_op jit(solution)/shard_map/ppermute | solution.py:545
  13.0 1.5 %collective-permute-start.2 = (f32[96,8,128]{2,1,0:T(8,128)S(1)}, f32[96,8,128]{2,1,0:T(8,128)S(1)}, u32[]{:S(2)}, u32[]{:S(2)}) collective-permute-start(f32[96,8,128]{2,1,0:T(8,128)S(1)} %get-tuple-element.29), channel_id=1, source_target_pairs={{0,192},{64,0},{128,64},{192,128},{1,193},{65,1},{129,65},{193,129... | collective-permute-start | bytes 1179656 | tf_op jit(solution)/shard_map/ppermute | solution.py:545
  14.5 3.2 %collective-permute-start.5 = (f32[144,128]{1,0:T(8,128)S(1)}, f32[144,128]{1,0:T(8,128)S(1)}, u32[]{:S(2)}, u32[]{:S(2)}) collective-permute-start(f32[144,128]{1,0:T(8,128)S(1)} %get-tuple-element.33), channel_id=1, source_target_pairs={{0,3},{1,2},{2,1},{3,0},{4,7},{5,6},{6,5},{7,4},{8,11},{9,10},{10,... | collective-permute-start | bytes 221192 | tf_op jit(solution)/shard_map/ppermute | solution.py:595
  17.7 4.9 %within.1 = (f32[3072,128]{1,0:T(8,128)S(1)}, f32[12,16,12,16,128]{4,3,2,1,0:T(8,128)S(1)}) custom-call(f32[48,128]{1,0:T(8,128)S(1)} %get-tuple-element.22.scales, f32[1536,128]{1,0:T(8,128)S(1)} %bitcast.14, f32[120,128]{1,0:T(8,128)S(1)} %collective-permute-done.from_core, bf16[12,16,12,16,128]{4,3,2,1,0:T(8,128)(2,1)} %bitcast.25), custom_call_target="tpu_custom_call" | custom-call | flops 4000000 | bytes 14000000 | tf_op jit(solution)/shard_map/within/pallas_call | solution.py:285
  22.7 5.4 %collective-permute-done.5.from_cross = f32[144,128]{1,0:T(8,128)S(1)} collective-permute-done((f32[144,128]{1,0:T(8,128)S(1)}, f32[144,128]{1,0:T(8,128)S(1)}, u32[]{:S(2)}, u32[]{:S(2)}) %collective-permute-start.5) | collective-permute-done | bytes 73760 | tf_op jit(solution)/shard_map/ppermute | solution.py:595
  28.1 0.0 collective-permute-done.3.yb
  28.1 0.0 copy-start
  28.1 0.0 copy-start.1
  28.1 0.0 copy-start.2
  28.1 0.0 copy-start.3
  28.1 5.9 %gram.1 = (f32[384,128]{1,0:T(8,128)S(1)}, f32[384,128]{1,0:T(8,128)S(1)}, f32[6144,128]{1,0:T(8,128)S(1)}, f32[8,384]{1,0:T(8,128)S(1)}) custom-call(f32[48,128]{1,0:T(8,128)S(1)} %get-tuple-element.22.scales, f32[3072,128]{1,0:T(8,128)S(1)} %get-tuple-element.25.within, f32[12,16,12,16,128]{4,3,2,1,0:T(8,128)S(1)} %get-tuple-element.26.receiver, ...), custom_call_target="tpu_custom_call" | custom-call | flops 1200000000 | bytes 8000000 | tf_op jit(solution)/shard_map/gram/pallas_call | solution.py:398
  34.0 0.3 collective-permute-start.6
  34.3 1.2 %collective-permute-done.6 = f32[384,128]{1,0:T(8,128)S(1)} collective-permute-done((f32[384,128]{1,0:T(8,128)S(1)}, f32[384,128]{1,0:T(8,128)S(1)}, u32[]{:S(2)}, u32[]{:S(2)}) %collective-permute-start.6) | collective-permute-done | bytes 196640 | tf_op jit(solution)/shard_map/ppermute | solution.py:549
  35.6 12.6 %all_to_all.15 = f32[16,24,128]{2,1,0:T(8,128)S(1)} all-to-all(f32[16,24,128]{2,1,0:T(8,128)S(1)} %bitcast.27), channel_id=1, replica_groups=mesh['y'=4,'z'=8,'xlo'=2,'xhi'=2,'core'=2] {'y','xlo','xhi'}, dimensions={0} | all-to-all | bytes 393216 | tf_op jit(solution)/shard_map/all_to_all | solution.py:553
  48.2 15.5 %all_to_all.16 = f32[8,24,128]{2,1,0:T(8,128)S(1)} all-to-all(f32[8,24,128]{2,1,0:T(8,128)S(1)} %broadcast_in_dim.6), channel_id=1, replica_groups=mesh['y'=4,'z'=8,'xlo'=2,'xhi'=2,'core'=2] {'z'}, dimensions={0} | all-to-all | bytes 196608 | tf_op jit(solution)/shard_map/all_to_all | solution.py:553
  63.8 10.1 %all_to_all.17 = f32[16,24,128]{2,1,0:T(8,128)S(1)} all-to-all(f32[16,24,128]{2,1,0:T(8,128)S(1)} %broadcast_in_dim.7), channel_id=1, replica_groups=mesh['y'=4,'z'=8,'xlo'=2,'xhi'=2,'core'=2] {'y','xlo','xhi'}, dimensions={0} | all-to-all | bytes 393216 | tf_op jit(solution)/shard_map/all_to_all | solution.py:553
  73.9 4.3 %collective-permute-start.7 = (f32[384,128]{1,0:T(8,128)S(1)}, f32[384,128]{1,0:T(8,128)S(1)}, u32[]{:S(2)}, u32[]{:S(2)}) collective-permute-start(f32[384,128]{1,0:T(8,128)S(1)} %bitcast.15), channel_id=1, source_target_pairs={{0,1},{1,0},{2,3},{3,2},{4,5},{5,4},{6,7},{7,6},{8,9},{9,8},{10,11... | collective-permute-start | bytes 589832 | tf_op jit(solution)/shard_map/ppermute | solution.py:549
  78.1 1.1 %collective-permute-done.7.other = f32[384,128]{1,0:T(8,128)S(1)} collective-permute-done((f32[384,128]{1,0:T(8,128)S(1)}, f32[384,128]{1,0:T(8,128)S(1)}, u32[]{:S(2)}, u32[]{:S(2)}) %collective-permute-start.7) | collective-permute-done | bytes 196640 | tf_op jit(solution)/shard_map/ppermute | solution.py:549
  79.2 3.3 %chain.1 = (f32[16,128]{1,0:T(8,128)}, f32[16,128]{1,0:T(8,128)}, f32[2,16,96]{2,1,0:T(8,128)}) custom-call(f32[384,128]{1,0:T(8,128)S(1)} %bitcast.16, f32[384,128]{1,0:T(8,128)S(1)} %collective-permute-done.7.other, f32[8,384]{1,0:T(8,128)S(1)} %get-tuple-element.36.stats, f32[6144,128]{1,0:T(8,128)S(1)} %get-tuple-element.37.cells, ...), custom_call_target="tpu_custom_call" | custom-call | tf_op jit(solution)/shard_map/chain/pallas_call | solution.py:530
  (13 shorter events, 0.1 us)
Async XLA Ops:
  3.4 8.1 %collective-permute-start = (f32[120,128]{1,0:T(8,128)S(1)}, f32[120,128]{1,0:T(8,128)S(1)}, u32[]{:S(2)}, u32[]{:S(2)}) collective-permute-start(f32[120,128]{1,0:T(8,128)S(1)} %get-tuple-element.24), channel_id=1, source_target_pairs={{0,1},{1,0},{2,3},{3,2},{4,5},{5,4},{6,7},{7,6},{8,9},{9,8},{10,11... | collective-permute-start | bytes 184328 | tf_op jit(solution)/shard_map/ppermute | solution.py:549
  6.7 21.3 %collective-permute-start.3 = (f32[96,8,128]{2,1,0:T(8,128)S(1)}, f32[96,8,128]{2,1,0:T(8,128)S(1)}, u32[]{:S(2)}, u32[]{:S(2)}) collective-permute-start(f32[96,8,128]{2,1,0:T(8,128)S(1)} %get-tuple-element.30), channel_id=1, source_target_pairs={{0,4},{4,8},{8,12},{12,16},{16,20},{20,24},{24,28},{28,32},{32,36}... | collective-permute-start | bytes 1179656 | tf_op jit(solution)/shard_map/ppermute | solution.py:545
  6.7 21.3 %collective-permute-start.4 = (f32[96,8,128]{2,1,0:T(8,128)S(1)}, f32[96,8,128]{2,1,0:T(8,128)S(1)}, u32[]{:S(2)}, u32[]{:S(2)}) collective-permute-start(f32[96,8,128]{2,1,0:T(8,128)S(1)} %get-tuple-element.31), channel_id=1, source_target_pairs={{0,60},{4,0},{8,4},{12,8},{16,12},{20,16},{24,20},{28,24},{32,28},... | collective-permute-start | bytes 1179656 | tf_op jit(solution)/shard_map/ppermute | solution.py:545
  11.6 16.4 %collective-permute-start.1 = (f32[96,8,128]{2,1,0:T(8,128)S(1)}, f32[96,8,128]{2,1,0:T(8,128)S(1)}, u32[]{:S(2)}, u32[]{:S(2)}) collective-permute-start(f32[96,8,128]{2,1,0:T(8,128)S(1)} %get-tuple-element.28), channel_id=1, source_target_pairs={{0,64},{64,128},{128,192},{192,0},{1,65},{65,129},{129,193},{193,1... | collective-permute-start | bytes 1179656 | tf_op jit(solution)/shard_map/ppermute | solution.py:545
  13.0 15.1 %collective-permute-start.2 = (f32[96,8,128]{2,1,0:T(8,128)S(1)}, f32[96,8,128]{2,1,0:T(8,128)S(1)}, u32[]{:S(2)}, u32[]{:S(2)}) collective-permute-start(f32[96,8,128]{2,1,0:T(8,128)S(1)} %get-tuple-element.29), channel_id=1, source_target_pairs={{0,192},{64,0},{128,64},{192,128},{1,193},{65,1},{129,65},{193,129... | collective-permute-start | bytes 1179656 | tf_op jit(solution)/shard_map/ppermute | solution.py:545
  14.5 13.5 %collective-permute-start.5 = (f32[144,128]{1,0:T(8,128)S(1)}, f32[144,128]{1,0:T(8,128)S(1)}, u32[]{:S(2)}, u32[]{:S(2)}) collective-permute-start(f32[144,128]{1,0:T(8,128)S(1)} %get-tuple-element.33), channel_id=1, source_target_pairs={{0,3},{1,2},{2,1},{3,0},{4,7},{5,6},{6,5},{7,4},{8,11},{9,10},{10,... | collective-permute-start | bytes 221192 | tf_op jit(solution)/shard_map/ppermute | solution.py:595
  28.1 51.1 %copy-start = (f32[2,96,16]{1,2,0:T(8,128)S(1)}, f32[2,96,16]{1,2,0:T(8,128)}, u32[]{:S(2)}) copy-start(f32[2,96,16]{1,2,0:T(8,128)} %param.12) | copy-start | bytes 36868
  28.1 51.1 %copy-start.1 = (s32[96,16]{0,1:T(8,128)S(1)}, s32[96,16]{0,1:T(8,128)}, u32[]{:S(2)}) copy-start(s32[96,16]{0,1:T(8,128)} %param.14) | copy-start | bytes 18436
  28.1 51.1 %copy-start.2 = (s32[96,16]{0,1:T(8,128)S(1)}, s32[96,16]{0,1:T(8,128)}, u32[]{:S(2)}) copy-start(s32[96,16]{0,1:T(8,128)} %param.15) | copy-start | bytes 18436
  28.1 51.1 %copy-start.3 = (s32[96]{0:T(128)S(1)}, s32[96]{0:T(128)}, u32[]{:S(2)}) copy-start(s32[96]{0:T(128)} %param.13) | copy-start | bytes 1156
  34.0 1.5 %collective-permute-start.6 = (f32[384,128]{1,0:T(8,128)S(1)}, f32[384,128]{1,0:T(8,128)S(1)}, u32[]{:S(2)}, u32[]{:S(2)}) collective-permute-start(f32[384,128]{1,0:T(8,128)S(1)} %get-tuple-element.35), channel_id=1, source_target_pairs={{0,1},{1,0},{2,3},{3,2},{4,5},{5,4},{6,7},{7,6},{8,9},{9,8},{10,11... | collective-permute-start | bytes 589832 | tf_op jit(solution)/shard_map/ppermute | solution.py:549
  73.9 5.3 %collective-permute-start.7 = (f32[384,128]{1,0:T(8,128)S(1)}, f32[384,128]{1,0:T(8,128)S(1)}, u32[]{:S(2)}, u32[]{:S(2)}) collective-permute-start(f32[384,128]{1,0:T(8,128)S(1)} %bitcast.15), channel_id=1, source_target_pairs={{0,1},{1,0},{2,3},{3,2},{4,5},{5,4},{6,7},{7,6},{8,9},{9,8},{10,11... | collective-permute-start | bytes 589832 | tf_op jit(solution)/shard_map/ppermute | solution.py:549

commit v8 on v7

--- a/solution.py
+++ b/solution.py
@@ -187,25 +187,23 @@
     )(*(in_hbm(x) for x in given))
 
 
-def strike_kernel(src, part, from_core, x_lo, x_hi, to_cross):
-    to_cross[: FIELDS + 24, :] = part[...]
-    to_cross[FIELDS + 24 :, :] = from_core[FIELDS:, :]
+def strike_kernel(src, arrived, x_lo, x_hi):
     first, second = src[:, 0:8, :], src[:, 8:16, :]
     row = lax.broadcasted_iota(jnp.int32, (FIELDS, 8, LANES), 1)
     x_lo[...] = jnp.where(row < 4, 0.0, 8.0 * pltpu.roll(first, 4, 1)) - first
     x_hi[...] = second - jnp.where(row < 4, 8.0 * pltpu.roll(second, 4, 1), 0.0)
 
 
-def strike_faces(src, part, from_core):
+def strike_faces(src, arrived):
     face = jax.ShapeDtypeStruct((FIELDS, 8, LANES), F32)
     return pl.pallas_call(
         strike_kernel,
-        out_shape=(face, face, jax.ShapeDtypeStruct((FIELDS + 48, LANES), F32)),
-        in_specs=[vmem()] * 3,
-        out_specs=(vmem(),) * 3,
+        out_shape=(face, face),
+        in_specs=[vmem()] * 2,
+        out_specs=(vmem(),) * 2,
         compiler_params=pltpu.CompilerParams(vmem_limit_bytes=VMEM_LIMIT),
         name="strike_faces",
-    )(src, part, from_core)
+    )(src, arrived)
 
 
 def ends_of(axes):
@@ -222,14 +220,17 @@
     ref[pl.ds(pl.multiple_of(at * PLANES, PLANES), PLANES), :] = value
 
 
-def within_kernel(scales, src, from_core, receiver_in, strain, receiver, grads, slots, sems):
+def within_kernel(
+    scales, src, from_core, from_cross, receiver_in, strain, receiver, grads, slots, sems
+):
     def fetch(b):
         return pltpu.make_async_copy(receiver_in.at[:, b], slots.at[b], sems.at[b])
 
     for b in range(BINS):
         fetch(b).start()
     lane = lane_ids((FIELDS, LANES))
-    halo = from_core[:FIELDS, :]
+    crossing = jnp.where(lax.axis_index("xhi") != lax.axis_index("core"), 1.0, 0.0).astype(F32)
+    halo = from_core[:FIELDS, :] + from_cross[:FIELDS, :] * crossing
 
     def at(x, y):
         if min(x, y) < 0 or max(x, y) > 3:
@@ -281,14 +282,14 @@
     return jnp.where((lane < 2) | (lane >= LANES - 2), turned, 0.0)
 
 
-def within(scales, src, from_core, receiver):
+def within(scales, src, from_core, from_cross, receiver):
     return pl.pallas_call(
         within_kernel,
         out_shape=(
             jax.ShapeDtypeStruct((BINS * 12 * PLANES, LANES), F32),
             jax.ShapeDtypeStruct(receiver.shape, F32),
         ),
-        in_specs=[vmem(), vmem(), vmem(), hbm()],
+        in_specs=[vmem()] * 4 + [hbm()],
         out_specs=(vmem(), vmem()),
         scratch_shapes=[
             pltpu.VMEM((3 * FIELDS * PLANES, LANES), F32),
@@ -300,25 +301,16 @@
             flops=4_000_000, bytes_accessed=14_000_000, transcendentals=0
         ),
         name="within",
-    )(scales, src, from_core, in_hbm(receiver))
-
-
-def gram_kernel(
-    scales, within, receiver, xb, xa, yb, ya, own, from_core, from_cross,
-    keep, send, cells, stats, ends
-):
-    lane = lane_ids((FIELDS, LANES))
-    crossing = jnp.where(lax.axis_index("xhi") != lax.axis_index("core"), 1.0, 0.0).astype(F32)
-    halo = from_cross[:FIELDS, :] * crossing
-    for plane in range(PLANES):
-        ends[pl.ds(plane, FIELDS, stride=PLANES), :] = ends_at(halo, plane, lane)
+    )(scales, src, from_core, from_cross, in_hbm(receiver))
+
+
+def gram_kernel(scales, within, receiver, xb, xa, yb, ya, from_cross, keep, send, cells):
     x_before, x_after = ends_of(GX)
     y_before, y_after = ends_of(GY)
     low_y = (lax.broadcasted_iota(jnp.int32, (8, LANES), 0) & 3) < 2
     side = jnp.where(low_y, y_before, y_after)
     scale_x = (scales[0:8, :] * x_before, scales[8:16, :] * x_after)
     scale_y = (scales[16:24, :] * side, scales[24:32, :] * side)
-    scale_z = tile(scales, 2)
 
     def body(b, carry):
         def from_x(field):
@@ -329,9 +321,6 @@
             first = jnp.where(low_y, below, above)
             second = jnp.where(low_y, pltpu.roll(below, 6, 0), pltpu.roll(above, 2, 0))
             return jnp.concatenate([scale_y[0] * first, scale_y[1] * second], axis=0)
-
-        def from_z(field):
-            return scale_z * tile(ends, field)
 
         strain = []
         for k in range(2):
@@ -341,9 +330,9 @@
                 (
                     inner[0] + from_x(ux),
                     inner[1] + from_y(uy),
-                    inner[2] + from_z(uz),
-                    inner[3] + (from_y(uz) + from_z(uy)),
-                    inner[4] + (from_x(uz) + from_z(ux)),
+                    inner[2],
+                    inner[3] + from_y(uz),
+                    inner[4] + from_x(uz),
                     inner[5] + (from_x(uy) + from_y(ux)),
                 )
             )
@@ -383,39 +372,29 @@
         part = slice(n * LANES, (n + 1) * LANES)
         keep[part, :] = jnp.where(upper, full[n + 3], full[n])
         send[part, :] = jnp.where(upper, full[n], full[n + 3])
-
-    def sums_of(value):
-        return jnp.concatenate([value[8 * j : 8 * j + 8, :] for j in range(3)], axis=1)
-
-    stats[...] = merge_sums(
-        merge_sums(sums_of(own[...]), sums_of(from_core[FIELDS:, :])),
-        merge_sums(sums_of(from_cross[FIELDS : FIELDS + 24, :]), sums_of(from_cross[FIELDS + 24 :, :])),
-    )
-
-
-def gram(scales, within, receiver, halos, sums):
-    half = jax.ShapeDtypeStruct((3 * LANES, LANES), F32)
+    send[ROWS:, :] = from_cross[FIELDS:, :]
+
+
+def gram(scales, within, receiver, halos, from_cross):
     return pl.pallas_call(
         gram_kernel,
         out_shape=(
-            half,
-            half,
+            jax.ShapeDtypeStruct((ROWS, LANES), F32),
+            jax.ShapeDtypeStruct((ROWS + 24, LANES), F32),
             jax.ShapeDtypeStruct((ROWS * PLANES, LANES), F32),
-            jax.ShapeDtypeStruct((8, ROWS), F32),
         ),
-        in_specs=[vmem()] * 10,
-        out_specs=(vmem(),) * 4,
-        scratch_shapes=[pltpu.VMEM((FIELDS * PLANES, LANES), F32)],
+        in_specs=[vmem()] * 8,
+        out_specs=(vmem(),) * 3,
         compiler_params=pltpu.CompilerParams(vmem_limit_bytes=VMEM_LIMIT),
         cost_estimate=pl.CostEstimate(
             flops=1_200_000_000, bytes_accessed=8_000_000, transcendentals=0
         ),
         name="gram",
-    )(scales, within, receiver, *halos, *sums)
+    )(scales, within, receiver, *halos, from_cross)
 
 
 def chain_kernel(
-    mine, other, stats, cells, observed_in, tensor_in, bins_in, window_in, update, direction, data,
+    mine, other, own, from_core, from_cross, received, cells, observed_in, tensor_in, bins_in, window_in, update, direction, data,
     full, coef, observed, tensor_ref, bins_ref, window, sems
 ):
     copies = [
@@ -461,6 +440,13 @@
     def norm_of(square):
         return jnp.sqrt(square + EPSILON)
 
+    def sums_of(value):
+        return jnp.concatenate([value[8 * j : 8 * j + 8, :] for j in range(3)], axis=1)
+
+    stats = merge_sums(
+        merge_sums(sums_of(own[...]), sums_of(from_core[FIELDS:, :])),
+        merge_sums(sums_of(from_cross[FIELDS:, :]), sums_of(received[ROWS:, :])),
+    )
     sums, count, rest = stats[0:1, :], stats[1:2, :], stats[2:3, 0:1]
     mean = sums / jnp.maximum(count, 1.0)
 
@@ -524,20 +510,20 @@
         data[k] = (observed[k] * (scale * size) + near[k]) * mask
 
 
-def chain(mine, other, stats, cells, observed, tensor, bins, window):
+def chain(halves, sums, cells, observed, tensor, bins, window):
     field = jax.ShapeDtypeStruct((PLANES, LANES), F32)
     given = (observed, tensor, bins, window)
     return pl.pallas_call(
         chain_kernel,
         out_shape=(field, field, jax.ShapeDtypeStruct(observed.shape, F32)),
-        in_specs=[vmem()] * 4 + [pl.BlockSpec(memory_space=pl.ANY)] * 4,
+        in_specs=[vmem()] * 7 + [pl.BlockSpec(memory_space=pl.ANY)] * 4,
         out_specs=(vmem(),) * 3,
         scratch_shapes=[pltpu.VMEM((ROWS, ROWS), F32), pltpu.VMEM((2, ROWS, LANES), F32)]
         + [pltpu.VMEM(x.shape, x.dtype) for x in given]
         + [pltpu.SemaphoreType.DMA((4,))],
         compiler_params=pltpu.CompilerParams(vmem_limit_bytes=VMEM_LIMIT),
         name="chain",
-    )(mine, other, stats, cells, *given)
+    )(*halves, *sums, cells, *given)
 
 
 def shift(value, axes, step):
@@ -588,21 +574,23 @@
     src, y_lo, y_hi, to_core, to_cross, stats, scales = pack(
         src, ids, table, values, tensor, bins, marks
     )
+    from_cross = lax.ppermute(to_cross, GZ, [(i, 3 - i) for i in range(4)])
     yb, ya = shift(y_hi, GY, 1), shift(y_lo, GY, -1)
+    x_lo, x_hi = strike_faces(src, from_cross)
+    xb, xa = shift(x_hi, GX, 1), shift(x_lo, GX, -1)
     from_core = swap(to_core, "core")
-    x_lo, x_hi, to_cross = strike_faces(src, to_cross, from_core)
-    xb, xa = shift(x_hi, GX, 1), shift(x_lo, GX, -1)
-    from_cross = lax.ppermute(to_cross, GZ, [(i, 3 - i) for i in range(4)])
-
-    strain, receiver = within(scales, src.reshape(FIELDS * PLANES, LANES), from_core, receiver)
-    sums = (stats, from_core, from_cross)
-    keep, send, cells, stats = gram(scales, strain, receiver, (xb, xa, yb, ya), sums)
-    packed = keep + swap(send, "core")
+
+    flat = src.reshape(FIELDS * PLANES, LANES)
+    strain, receiver = within(scales, flat, from_core, from_cross, receiver)
+    keep, send, cells = gram(scales, strain, receiver, (xb, xa, yb, ya), from_cross)
+    received = swap(send, "core")
+    packed = keep + received[:ROWS]
     packed = scatter_sum(packed, PLANE)
     packed = whole_sum(packed, ("z",))
     packed = gather(packed, PLANE)
     other = swap(packed, "core")
-    update, direction, data = chain(packed, other, stats, cells, values, tensor, bins, marks)
+    sums = (stats, from_core, from_cross, received)
+    update, direction, data = chain((packed, other), sums, cells, values, tensor, bins, marks)
     return (
         update.reshape(metric_ids.shape),
         direction.reshape(metric_ids.shape),

time: 82.8 us -> 87 us (1.051)
  blocking collectives: 38.2 us -> 40.5 us
  other arithmetic: 0.05 us -> 1.88 us
  waiting for transfers between devices: 7.7 us -> 8.57 us
    ppermute x4, waiting for transfers between devices: 0.01 us -> 5.51 us  [shift(): lax.ppermute(value, axes, [(i, (i + step) % count) for i in range(count)])]
    ppermute x1, waiting for transfers between devices: 5.39 us -> 0.01 us  [per_device(): from_cross = lax.ppermute(to_cross, GZ, [(i, 3 - i) for i in range(4)])]
    all_to_all x3, blocking collectives: 38.2 us -> 40.5 us  [exchange(): return lax.all_to_all(value, axes, 0, 0, tiled=True)]
    ppermute x3, starting transfers between devices: 7.9 us -> 5.62 us  [swap(): return lax.ppermute(value, axis, [(0, 1), (1, 0)])]
    ppermute x1, starting transfers between devices: 3.2 us -> 4.22 us  [per_device(): from_cross = lax.ppermute(to_cross, GZ, [(i, 3 - i) for i in range(4)])]
    reduce_sum x1, other arithmetic: 0.02 us -> 0.95 us  [scatter_sum(): return jnp.sum(exchange(value.reshape(count, -1, LANES), axes), axis=0)]
    reduce_sum x1, other arithmetic: 0.01 us -> 0.91 us  [whole_sum(): jnp.sum(exchange(jnp.broadcast_to(value, (count,) + value.shape), axes),...]
  transfers between devices with their start and end apart: 8 -> 8, of which waited for: 3 -> 5; matrix products, arithmetic and copies ran while one was open for 0% -> 0% of each run, Pallas kernels for 6% -> 6%
where the time goes in v8:
time: 87 us; the launch traced here: 86.7 us
  blocking collectives  40.5 us (47%)
  starting transfers between devices  18.3 us (21%)
  Pallas kernels  16.6 us (19%)
  waiting for transfers between devices  8.57 us (10%)
  other arithmetic  1.88 us (2%)
    all_to_all x3, blocking collectives, exchange(): return lax.all_to_all(value, axes, 0, 0, tiled=True)  40.5 us
    ppermute x4, starting transfers between devices, shift(): lax.ppermute(value, axes, [(i, (i + step) % count) for i in range(count)])  8.51 us
    ppermute x3, starting transfers between devices, swap(): return lax.ppermute(value, axis, [(0, 1), (1, 0)])  5.62 us
    ppermute x4, waiting for transfers between devices, shift(): lax.ppermute(value, axes, [(i, (i + step) % count) for i in range(count)])  5.51 us
    pallas_call x1, Pallas kernels, gram(): pl.pallas_call(gram_kernel, out_shape=(jax.ShapeDtypeStruct((ROWS, LANES)...  5.24 us
    pallas_call x1, Pallas kernels, within(): pl.pallas_call(within_kernel, out_shape=(jax.ShapeDtypeStruct((BINS * 12...  5.06 us
    ppermute x1, starting transfers between devices, per_device(): from_cross = lax.ppermute(to_cross, GZ, [(i, 3 - i) for i in range(4)])  4.22 us
    pallas_call x1, Pallas kernels, chain(): pl.pallas_call(chain_kernel, out_shape=(field, field, jax.ShapeDtypeStruc...  3.45 us
  transfers between devices with their start and end apart: 8, of which 5 were waited for; matrix products, arithmetic and copies ran while one was open for 0% of the time, Pallas kernels for 6%

profile of v8, /device:TPU:1, one launch (start us, length us, event | category | flops | bytes accessed | tf_op | source)
XLA Modules:
  0.0 86.7 jit_solution(11783937154852222099)
XLA Ops:
  0.6 2.8 %pack.1 = (f32[96,16,128]{2,1,0:T(8,128)S(1)}, f32[96,8,128]{2,1,0:T(8,128)S(1)}, f32[96,8,128]{2,1,0:T(8,128)S(1)}, f32[120,128]{1,0:T(8,128)S(1)}, f32[120,128...) custom-call(f32[96,16,128]{2,1,0:T(8,128)} %bitcast.26, s32[16,128]{1,0:T(8,128)} %bitcast.28, ...), custom_call_target="tpu_custom_call" | custom-call | tf_op jit(solution)/shard_map/pack/pallas_call | solution.py:169
  3.4 4.2 %collective-permute-start.1 = (f32[120,128]{1,0:T(8,128)S(1)}, f32[120,128]{1,0:T(8,128)S(1)}, u32[]{:S(2)}, u32[]{:S(2)}) collective-permute-start(f32[120,128]{1,0:T(8,128)S(1)} %get-tuple-element.23), channel_id=1, source_target_pairs={{0,3},{1,2},{2,1},{3,0},{4,7},{5,6},{6,5},{7,4},{8,11},{9,10},{10,... | collective-permute-start | bytes 184328 | tf_op jit(solution)/shard_map/ppermute | solution.py:577
  7.6 0.3 collective-permute-start.4
  7.9 5.3 %collective-permute-start.5 = (f32[96,8,128]{2,1,0:T(8,128)S(1)}, f32[96,8,128]{2,1,0:T(8,128)S(1)}, u32[]{:S(2)}, u32[]{:S(2)}) collective-permute-start(f32[96,8,128]{2,1,0:T(8,128)S(1)} %get-tuple-element.29), channel_id=1, source_target_pairs={{0,60},{4,0},{8,4},{12,8},{16,12},{20,16},{24,20},{28,24},{32,28},... | collective-permute-start | bytes 1179656 | tf_op jit(solution)/shard_map/ppermute | solution.py:531
  13.2 0.1 strike_faces.1
  13.3 1.4 %collective-permute-start.2 = (f32[96,8,128]{2,1,0:T(8,128)S(1)}, f32[96,8,128]{2,1,0:T(8,128)S(1)}, u32[]{:S(2)}, u32[]{:S(2)}) collective-permute-start(f32[96,8,128]{2,1,0:T(8,128)S(1)} %get-tuple-element.26), channel_id=1, source_target_pairs={{0,64},{64,128},{128,192},{192,0},{1,65},{65,129},{129,193},{193,1... | collective-permute-start | bytes 1179656 | tf_op jit(solution)/shard_map/ppermute | solution.py:531
  14.7 1.5 %collective-permute-start.3 = (f32[96,8,128]{2,1,0:T(8,128)S(1)}, f32[96,8,128]{2,1,0:T(8,128)S(1)}, u32[]{:S(2)}, u32[]{:S(2)}) collective-permute-start(f32[96,8,128]{2,1,0:T(8,128)S(1)} %get-tuple-element.27), channel_id=1, source_target_pairs={{0,192},{64,0},{128,64},{192,128},{1,193},{65,1},{129,65},{193,129... | collective-permute-start | bytes 1179656 | tf_op jit(solution)/shard_map/ppermute | solution.py:531
  16.2 0.5 collective-permute-start
  16.8 0.9 %collective-permute-done.from_core = f32[120,128]{1,0:T(8,128)S(1)} collective-permute-done((f32[120,128]{1,0:T(8,128)S(1)}, f32[120,128]{1,0:T(8,128)S(1)}, u32[]{:S(2)}, u32[]{:S(2)}) %collective-permute-start) | collective-permute-done | bytes 61472 | tf_op jit(solution)/shard_map/ppermute | solution.py:535
  17.7 5.1 %within.1 = (f32[3072,128]{1,0:T(8,128)S(1)}, f32[12,16,12,16,128]{4,3,2,1,0:T(8,128)S(1)}) custom-call(f32[48,128]{1,0:T(8,128)S(1)} %get-tuple-element.20.scales, f32[1536,128]{1,0:T(8,128)S(1)} %bitcast.14, f32[120,128]{1,0:T(8,128)S(1)} %collective-permute-done.from_core, f32[120,128]{1,0:T(8,128)S(1)} %collective-permute-done.1.from_cross.arrived, ...), custom_call_target="tpu_custom_call" | custom-call | flops 4000000 | bytes 14000000 | tf_op jit(solution)/shard_map/within/pallas_call | solution.py:286
  22.7 3.5 %collective-permute-done.4.yb = f32[96,8,128]{2,1,0:T(8,128)S(1)} collective-permute-done((f32[96,8,128]{2,1,0:T(8,128)S(1)}, f32[96,8,128]{2,1,0:T(8,128)S(1)}, u32[]{:S(2)}, u32[]{:S(2)}) %collective-permute-start.4) | collective-permute-done | bytes 393248 | tf_op jit(solution)/shard_map/ppermute | solution.py:531
  26.3 2.0 %collective-permute-done.5.ya = f32[96,8,128]{2,1,0:T(8,128)S(1)} collective-permute-done((f32[96,8,128]{2,1,0:T(8,128)S(1)}, f32[96,8,128]{2,1,0:T(8,128)S(1)}, u32[]{:S(2)}, u32[]{:S(2)}) %collective-permute-start.5) | collective-permute-done | bytes 393248 | tf_op jit(solution)/shard_map/ppermute | solution.py:531
  28.3 0.0 copy-start.2
  28.3 5.2 %gram.1 = (f32[384,128]{1,0:T(8,128)S(1)}, f32[408,128]{1,0:T(8,128)S(1)}, f32[6144,128]{1,0:T(8,128)S(1)}) custom-call(f32[48,128]{1,0:T(8,128)S(1)} %get-tuple-element.20.scales, f32[3072,128]{1,0:T(8,128)S(1)} %get-tuple-element.24.within, f32[12,16,12,16,128]{4,3,2,1,0:T(8,128)S(1)} %get-tuple-element.25.receiver, ...), custom_call_target="tpu_custom_call" | custom-call | flops 1200000000 | bytes 8000000 | tf_op jit(solution)/shard_map/gram/pallas_call | solution.py:379
  33.5 0.8 collective-permute-start.6
  34.3 1.1 %collective-permute-done.6.received = f32[408,128]{1,0:T(8,128)S(1)} collective-permute-done((f32[408,128]{1,0:T(8,128)S(1)}, f32[408,128]{1,0:T(8,128)S(1)}, u32[]{:S(2)}, u32[]{:S(2)}) %collective-permute-start.6) | collective-permute-done | bytes 208928 | tf_op jit(solution)/shard_map/ppermute | solution.py:535
  35.4 11.9 %all_to_all.15 = f32[16,24,128]{2,1,0:T(8,128)} all-to-all(f32[16,24,128]{2,1,0:T(8,128)S(1)} %bitcast.27), channel_id=1, replica_groups=mesh['y'=4,'z'=8,'xlo'=2,'xhi'=2,'core'=2] {'y','xlo','xhi'}, dimensions={0} | all-to-all | bytes 393216 | tf_op jit(solution)/shard_map/all_to_all | solution.py:539
  47.3 0.9 %reduce_sum.18 = f32[24,128]{1,0:T(8,128)S(1)} reduce(f32[16,24,128]{2,1,0:T(8,128)} %all_to_all.15, f32[]{:T(128)} %constant.0.clone.1), dimensions={0}, to_apply=%region_0.0 | reduce | flops 46080 | bytes 208900 | tf_op jit(solution)/shard_map/reduce_sum | solution.py:544
  48.3 18.5 %all_to_all.16 = f32[8,24,128]{2,1,0:T(8,128)} all-to-all(f32[8,24,128]{2,1,0:T(8,128)S(1)} %broadcast_in_dim.6), channel_id=1, replica_groups=mesh['y'=4,'z'=8,'xlo'=2,'xhi'=2,'core'=2] {'z'}, dimensions={0} | all-to-all | bytes 196608 | tf_op jit(solution)/shard_map/all_to_all | solution.py:539
  66.8 0.9 %reduce_sum.19 = f32[24,128]{1,0:T(8,128)S(1)} reduce(f32[8,24,128]{2,1,0:T(8,128)} %all_to_all.16, f32[]{:T(128)} %constant.0.clone.1), dimensions={0}, to_apply=%region_1.0 | reduce | flops 21504 | bytes 110596 | tf_op jit(solution)/shard_map/reduce_sum | solution.py:549
  67.7 10.1 %all_to_all.17 = f32[16,24,128]{2,1,0:T(8,128)S(1)} all-to-all(f32[16,24,128]{2,1,0:T(8,128)S(1)} %broadcast_in_dim.7), channel_id=1, replica_groups=mesh['y'=4,'z'=8,'xlo'=2,'xhi'=2,'core'=2] {'y','xlo','xhi'}, dimensions={0} | all-to-all | bytes 393216 | tf_op jit(solution)/shard_map/all_to_all | solution.py:539
  77.9 4.3 %collective-permute-start.7 = (f32[384,128]{1,0:T(8,128)S(1)}, f32[384,128]{1,0:T(8,128)S(1)}, u32[]{:S(2)}, u32[]{:S(2)}) collective-permute-start(f32[384,128]{1,0:T(8,128)S(1)} %bitcast.15), channel_id=1, source_target_pairs={{0,1},{1,0},{2,3},{3,2},{4,5},{5,4},{6,7},{7,6},{8,9},{9,8},{10,11... | collective-permute-start | bytes 589832 | tf_op jit(solution)/shard_map/ppermute | solution.py:535
  82.2 1.1 %collective-permute-done.7.other = f32[384,128]{1,0:T(8,128)S(1)} collective-permute-done((f32[384,128]{1,0:T(8,128)S(1)}, f32[384,128]{1,0:T(8,128)S(1)}, u32[]{:S(2)}, u32[]{:S(2)}) %collective-permute-start.7) | collective-permute-done | bytes 196640 | tf_op jit(solution)/shard_map/ppermute | solution.py:535
  83.3 3.5 %chain.1 = (f32[16,128]{1,0:T(8,128)}, f32[16,128]{1,0:T(8,128)}, f32[2,16,96]{2,1,0:T(8,128)}) custom-call(f32[384,128]{1,0:T(8,128)S(1)} %bitcast.16, f32[384,128]{1,0:T(8,128)S(1)} %collective-permute-done.7.other, f32[24,128]{1,0:T(8,128)S(1)} %get-tuple-element.32.own, f32[120,128]{1,0:T(8,128)S(1)} %collective-permute-done.from_core, ...), custom_call_target="tpu_custom_call" | custom-call | tf_op jit(solution)/shard_map/chain/pallas_call | solution.py:516
  (13 shorter events, 0.1 us)
Async XLA Ops:
  3.4 9.8 %collective-permute-start.1 = (f32[120,128]{1,0:T(8,128)S(1)}, f32[120,128]{1,0:T(8,128)S(1)}, u32[]{:S(2)}, u32[]{:S(2)}) collective-permute-start(f32[120,128]{1,0:T(8,128)S(1)} %get-tuple-element.23), channel_id=1, source_target_pairs={{0,3},{1,2},{2,1},{3,0},{4,7},{5,6},{6,5},{7,4},{8,11},{9,10},{10,... | collective-permute-start | bytes 184328 | tf_op jit(solution)/shard_map/ppermute | solution.py:577
  7.6 18.7 %collective-permute-start.4 = (f32[96,8,128]{2,1,0:T(8,128)S(1)}, f32[96,8,128]{2,1,0:T(8,128)S(1)}, u32[]{:S(2)}, u32[]{:S(2)}) collective-permute-start(f32[96,8,128]{2,1,0:T(8,128)S(1)} %get-tuple-element.28), channel_id=1, source_target_pairs={{0,4},{4,8},{8,12},{12,16},{16,20},{20,24},{24,28},{28,32},{32,36}... | collective-permute-start | bytes 1179656 | tf_op jit(solution)/shard_map/ppermute | solution.py:531
  7.9 20.3 %collective-permute-start.5 = (f32[96,8,128]{2,1,0:T(8,128)S(1)}, f32[96,8,128]{2,1,0:T(8,128)S(1)}, u32[]{:S(2)}, u32[]{:S(2)}) collective-permute-start(f32[96,8,128]{2,1,0:T(8,128)S(1)} %get-tuple-element.29), channel_id=1, source_target_pairs={{0,60},{4,0},{8,4},{12,8},{16,12},{20,16},{24,20},{28,24},{32,28},... | collective-permute-start | bytes 1179656 | tf_op jit(solution)/shard_map/ppermute | solution.py:531
  13.3 14.9 %collective-permute-start.2 = (f32[96,8,128]{2,1,0:T(8,128)S(1)}, f32[96,8,128]{2,1,0:T(8,128)S(1)}, u32[]{:S(2)}, u32[]{:S(2)}) collective-permute-start(f32[96,8,128]{2,1,0:T(8,128)S(1)} %get-tuple-element.26), channel_id=1, source_target_pairs={{0,64},{64,128},{128,192},{192,0},{1,65},{65,129},{129,193},{193,1... | collective-permute-start | bytes 1179656 | tf_op jit(solution)/shard_map/ppermute | solution.py:531
  14.7 13.5 %collective-permute-start.3 = (f32[96,8,128]{2,1,0:T(8,128)S(1)}, f32[96,8,128]{2,1,0:T(8,128)S(1)}, u32[]{:S(2)}, u32[]{:S(2)}) collective-permute-start(f32[96,8,128]{2,1,0:T(8,128)S(1)} %get-tuple-element.27), channel_id=1, source_target_pairs={{0,192},{64,0},{128,64},{192,128},{1,193},{65,1},{129,65},{193,129... | collective-permute-start | bytes 1179656 | tf_op jit(solution)/shard_map/ppermute | solution.py:531
  16.2 1.4 %collective-permute-start = (f32[120,128]{1,0:T(8,128)S(1)}, f32[120,128]{1,0:T(8,128)S(1)}, u32[]{:S(2)}, u32[]{:S(2)}) collective-permute-start(f32[120,128]{1,0:T(8,128)S(1)} %get-tuple-element.22), channel_id=1, source_target_pairs={{0,1},{1,0},{2,3},{3,2},{4,5},{5,4},{6,7},{7,6},{8,9},{9,8},{10,11... | collective-permute-start | bytes 184328 | tf_op jit(solution)/shard_map/ppermute | solution.py:535
  28.2 55.0 %copy-start = (f32[2,96,16]{1,2,0:T(8,128)S(1)}, f32[2,96,16]{1,2,0:T(8,128)}, u32[]{:S(2)}) copy-start(f32[2,96,16]{1,2,0:T(8,128)} %param.12) | copy-start | bytes 36868
  28.3 55.0 %copy-start.1 = (s32[96,16]{0,1:T(8,128)S(1)}, s32[96,16]{0,1:T(8,128)}, u32[]{:S(2)}) copy-start(s32[96,16]{0,1:T(8,128)} %param.14) | copy-start | bytes 18436
  28.3 55.0 %copy-start.2 = (s32[96,16]{0,1:T(8,128)S(1)}, s32[96,16]{0,1:T(8,128)}, u32[]{:S(2)}) copy-start(s32[96,16]{0,1:T(8,128)} %param.15) | copy-start | bytes 18436
  28.3 55.0 %copy-start.3 = (s32[96]{0:T(128)S(1)}, s32[96]{0:T(128)}, u32[]{:S(2)}) copy-start(s32[96]{0:T(128)} %param.13) | copy-start | bytes 1156
  33.5 1.9 %collective-permute-start.6 = (f32[408,128]{1,0:T(8,128)S(1)}, f32[408,128]{1,0:T(8,128)S(1)}, u32[]{:S(2)}, u32[]{:S(2)}) collective-permute-start(f32[408,128]{1,0:T(8,128)S(1)} %get-tuple-element.31), channel_id=1, source_target_pairs={{0,1},{1,0},{2,3},{3,2},{4,5},{5,4},{6,7},{7,6},{8,9},{9,8},{10,11... | collective-permute-start | bytes 626696 | tf_op jit(solution)/shard_map/ppermute | solution.py:535
  77.9 5.4 %collective-permute-start.7 = (f32[384,128]{1,0:T(8,128)S(1)}, f32[384,128]{1,0:T(8,128)S(1)}, u32[]{:S(2)}, u32[]{:S(2)}) collective-permute-start(f32[384,128]{1,0:T(8,128)S(1)} %bitcast.15), channel_id=1, source_target_pairs={{0,1},{1,0},{2,3},{3,2},{4,5},{5,4},{6,7},{7,6},{8,9},{9,8},{10,11... | collective-permute-start | bytes 589832 | tf_op jit(solution)/shard_map/ppermute | solution.py:535

commit v9 on v7

--- a/solution.py
+++ b/solution.py
@@ -26,6 +26,7 @@
 FIELDS = 96
 PLANES = 16
 LANES = 128
+DENSE = 24
 ROWS = 384
 BLOCKS = ((0, 0), (0, 1), (0, 2), (1, 1), (1, 2), (2, 2))
 
@@ -85,7 +86,15 @@
     square = jnp.sum(rest[0] * rest[0] + rest[1] * rest[1], axis=(0, 1), keepdims=True)
     lane = lane_ids((ROWS, LANES))
     wide = jnp.where(lane == 0, total, jnp.where(lane == 1, count, square))
-    return jnp.concatenate([wide[j * LANES : (j + 1) * LANES, :].T[:8] for j in range(3)], axis=0)
+    part = [wide[j * LANES : (j + 1) * LANES, :].T[:8] for j in range(3)]
+    rows = [part[j][k : k + 1] for k in range(2) for j in range(3)] + [part[0][2:3]] * 2
+    return jnp.concatenate(rows, axis=0)
+
+
+def sums_of(value):
+    total = jnp.concatenate([value[j : j + 1, :] for j in range(3)], axis=1)
+    count = jnp.concatenate([value[j : j + 1, :] for j in range(3, 6)], axis=1)
+    return jnp.concatenate([total, count, jnp.concatenate([value[6:7, :]] * 3, axis=1)], axis=0)
 
 
 def merge_sums(one, two):
@@ -101,7 +110,7 @@
 def pack_kernel(
     src_in, ids_in, table_in, observed_in, tensor_in, bins_in, window_in,
     src, y_lo, y_hi, to_core, to_cross, stats, scales,
-    ids, table, observed, tensor, bins, window, sems,
+    ids, table, observed, tensor, bins, window, sparse, sems,
 ):
     copies = [
         pltpu.make_async_copy(here, there, sems.at[n])
@@ -128,8 +137,8 @@
         scales[p * PLANES : (p + 1) * PLANES, :] = scale * (1.0 / 12.0)
     sums = data_sums(observed, tensor[...], bins[...], window[...])
     stats[...] = sums
-    to_core[FIELDS:, :] = sums
-    to_cross[FIELDS:, :] = sums
+    to_core[DENSE:, :] = sums
+    to_cross[DENSE:, :] = sums
 
     copies[0].wait()
     y = lax.broadcasted_iota(jnp.int32, (FIELDS, 8, LANES), 1) & 3
@@ -155,16 +164,36 @@
     place = lane & 7
     low = jnp.where(place == 1, 8.0 * pltpu.roll(low, 1, 1), 0.0) - low
     high = high - jnp.where(place == 6, 8.0 * pltpu.roll(high, LANES - 1, 1), 0.0)
-    low = pltpu.roll(low, LANES - 2, 1)
     high = pltpu.roll(high, 2, 1)
     upper = lax.axis_index("core") == 1
-    to_core[:FIELDS, :] = jnp.where(upper, low, high)
-    to_cross[:FIELDS, :] = jnp.where(upper, high, low)
+    to_core[:DENSE, :] = dense(jnp.where(upper, low, high), sparse)
+    to_cross[:DENSE, :] = dense(jnp.where(upper, high, low), sparse)
+
+
+def dense(value, sparse):
+    sparse[...] = value
+    lane = lane_ids((DENSE, LANES)) & 7
+    out = jnp.zeros((DENSE, LANES), F32)
+    for n in range(4):
+        part = sparse[pl.ds(n, DENSE, stride=4), :]
+        out = jnp.where(lane >> 1 == n, pltpu.roll(part, 2 * n, 1) if n else part, out)
+    return out
+
+
+def spread_out(value, sparse, lower):
+    lane = lane_ids((DENSE, LANES)) & 7
+    for n in range(4):
+        part = pltpu.roll(value, LANES - 2 * n, 1) if n else value
+        part = jnp.where(lane < 2, part, 0.0)
+        sparse[pl.ds(n, DENSE, stride=4), :] = jnp.where(
+            lower, part, pltpu.roll(part, LANES - 2, 1)
+        )
+    return sparse[...]
 
 
 def pack(src, ids, table, observed, tensor, bins, window):
     face = jax.ShapeDtypeStruct((FIELDS, 8, LANES), F32)
-    ends = jax.ShapeDtypeStruct((FIELDS + 24, LANES), F32)
+    ends = jax.ShapeDtypeStruct((DENSE + 8, LANES), F32)
     given = (src, ids, table, observed, tensor, bins, window)
     return pl.pallas_call(
         pack_kernel,
@@ -174,22 +203,22 @@
             face,
             ends,
             ends,
-            jax.ShapeDtypeStruct((24, LANES), F32),
+            jax.ShapeDtypeStruct((8, LANES), F32),
             jax.ShapeDtypeStruct((3 * PLANES, LANES), F32),
         ),
         in_specs=[hbm()] * 7,
         out_specs=(vmem(),) * 7,
         scratch_shapes=[pltpu.VMEM(ids.shape, ids.dtype), pltpu.SMEM(table.shape, table.dtype)]
         + [pltpu.VMEM(x.shape, x.dtype) for x in given[3:]]
-        + [pltpu.SemaphoreType.DMA((7,))],
+        + [pltpu.VMEM((FIELDS, LANES), F32), pltpu.SemaphoreType.DMA((7,))],
         compiler_params=pltpu.CompilerParams(vmem_limit_bytes=VMEM_LIMIT),
         name="pack",
     )(*(in_hbm(x) for x in given))
 
 
 def strike_kernel(src, part, from_core, x_lo, x_hi, to_cross):
-    to_cross[: FIELDS + 24, :] = part[...]
-    to_cross[FIELDS + 24 :, :] = from_core[FIELDS:, :]
+    to_cross[: DENSE + 8, :] = part[...]
+    to_cross[DENSE + 8 :, :] = from_core[DENSE:, :]
     first, second = src[:, 0:8, :], src[:, 8:16, :]
     row = lax.broadcasted_iota(jnp.int32, (FIELDS, 8, LANES), 1)
     x_lo[...] = jnp.where(row < 4, 0.0, 8.0 * pltpu.roll(first, 4, 1)) - first
@@ -200,7 +229,7 @@
     face = jax.ShapeDtypeStruct((FIELDS, 8, LANES), F32)
     return pl.pallas_call(
         strike_kernel,
-        out_shape=(face, face, jax.ShapeDtypeStruct((FIELDS + 48, LANES), F32)),
+        out_shape=(face, face, jax.ShapeDtypeStruct((DENSE + 16, LANES), F32)),
         in_specs=[vmem()] * 3,
         out_specs=(vmem(),) * 3,
         compiler_params=pltpu.CompilerParams(vmem_limit_bytes=VMEM_LIMIT),
@@ -222,14 +251,16 @@
     ref[pl.ds(pl.multiple_of(at * PLANES, PLANES), PLANES), :] = value
 
 
-def within_kernel(scales, src, from_core, receiver_in, strain, receiver, grads, slots, sems):
+def within_kernel(
+    scales, src, from_core, receiver_in, strain, receiver, grads, slots, sparse, sems
+):
     def fetch(b):
         return pltpu.make_async_copy(receiver_in.at[:, b], slots.at[b], sems.at[b])
 
     for b in range(BINS):
         fetch(b).start()
     lane = lane_ids((FIELDS, LANES))
-    halo = from_core[:FIELDS, :]
+    halo = spread_out(from_core[:DENSE, :], sparse, lax.axis_index("core") == 1)
 
     def at(x, y):
         if min(x, y) < 0 or max(x, y) > 3:
@@ -293,6 +324,7 @@
         scratch_shapes=[
             pltpu.VMEM((3 * FIELDS * PLANES, LANES), F32),
             pltpu.VMEM((BINS, TENSORS, 12, PLANES, LANES), BF16),
+            pltpu.VMEM((FIELDS, LANES), F32),
             pltpu.SemaphoreType.DMA((BINS,)),
         ],
         compiler_params=pltpu.CompilerParams(vmem_limit_bytes=VMEM_LIMIT),
@@ -305,11 +337,12 @@
 
 def gram_kernel(
     scales, within, receiver, xb, xa, yb, ya, own, from_core, from_cross,
-    keep, send, cells, stats, ends
+    keep, send, cells, stats, ends, sparse
 ):
     lane = lane_ids((FIELDS, LANES))
     crossing = jnp.where(lax.axis_index("xhi") != lax.axis_index("core"), 1.0, 0.0).astype(F32)
-    halo = from_cross[:FIELDS, :] * crossing
+    lower = lax.axis_index("core") == 0
+    halo = spread_out(from_cross[:DENSE, :] * crossing, sparse, lower)
     for plane in range(PLANES):
         ends[pl.ds(plane, FIELDS, stride=PLANES), :] = ends_at(halo, plane, lane)
     x_before, x_after = ends_of(GX)
@@ -384,12 +417,11 @@
         keep[part, :] = jnp.where(upper, full[n + 3], full[n])
         send[part, :] = jnp.where(upper, full[n], full[n + 3])
 
-    def sums_of(value):
-        return jnp.concatenate([value[8 * j : 8 * j + 8, :] for j in range(3)], axis=1)
-
     stats[...] = merge_sums(
-        merge_sums(sums_of(own[...]), sums_of(from_core[FIELDS:, :])),
-        merge_sums(sums_of(from_cross[FIELDS : FIELDS + 24, :]), sums_of(from_cross[FIELDS + 24 :, :])),
+        merge_sums(sums_of(own[...]), sums_of(from_core[DENSE:, :])),
+        merge_sums(
+            sums_of(from_cross[DENSE : DENSE + 8, :]), sums_of(from_cross[DENSE + 8 :, :])
+        ),
     )
 
 
@@ -405,7 +437,10 @@
         ),
         in_specs=[vmem()] * 10,
         out_specs=(vmem(),) * 4,
-        scratch_shapes=[pltpu.VMEM((FIELDS * PLANES, LANES), F32)],
+        scratch_shapes=[
+            pltpu.VMEM((FIELDS * PLANES, LANES), F32),
+            pltpu.VMEM((FIELDS, LANES), F32),
+        ],
         compiler_params=pltpu.CompilerParams(vmem_limit_bytes=VMEM_LIMIT),
         cost_estimate=pl.CostEstimate(
             flops=1_200_000_000, bytes_accessed=8_000_000, transcendentals=0

time: 82.8 us -> 82.1 us (level)
  waiting for transfers between devices: 7.7 us -> 6.41 us
    ppermute x1, waiting for transfers between devices: 5.39 us -> 4.1 us  [per_device(): from_cross = lax.ppermute(to_cross, GZ, [(i, 3 - i) for i in range(4)])]
where the time goes in v9:
time: 82.1 us; the launch traced here: 81.9 us
  blocking collectives  38.4 us (47%)
  starting transfers between devices  18.8 us (23%)
  Pallas kernels  17.5 us (21%)
  waiting for transfers between devices  6.41 us (8%)
    all_to_all x3, blocking collectives, exchange(): return lax.all_to_all(value, axes, 0, 0, tiled=True)  38.4 us
    ppermute x3, starting transfers between devices, swap(): return lax.ppermute(value, axis, [(0, 1), (1, 0)])  7.94 us
    ppermute x4, starting transfers between devices, shift(): lax.ppermute(value, axes, [(i, (i + step) % count) for i in range(count)])  7.67 us
    pallas_call x1, Pallas kernels, gram(): pl.pallas_call(gram_kernel, out_shape=(half, half, jax.ShapeDtypeStruct((...  6.08 us
    pallas_call x1, Pallas kernels, within(): pl.pallas_call(within_kernel, out_shape=(jax.ShapeDtypeStruct((BINS * 12...  5.08 us
    ppermute x1, waiting for transfers between devices, per_device(): from_cross = lax.ppermute(to_cross, GZ, [(i, 3 - i) for i in range(4)])  4.1 us
    pallas_call x1, Pallas kernels, chain(): pl.pallas_call(chain_kernel, out_shape=(field, field, jax.ShapeDtypeStruc...  3.32 us
    ppermute x1, starting transfers between devices, per_device(): from_cross = lax.ppermute(to_cross, GZ, [(i, 3 - i) for i in range(4)])  3.2 us
  transfers between devices with their start and end apart: 8, of which 3 were waited for; matrix products, arithmetic and copies ran while one was open for 0% of the time, Pallas kernels for 6%

profile of v9, /device:TPU:1, one launch (start us, length us, event | category | flops | bytes accessed | tf_op | source)
XLA Modules:
  0.0 81.9 jit_solution(5407443875233942089)
XLA Ops:
  0.6 2.9 %pack.1 = (f32[96,16,128]{2,1,0:T(8,128)S(1)}, f32[96,8,128]{2,1,0:T(8,128)S(1)}, f32[96,8,128]{2,1,0:T(8,128)S(1)}, f32[32,128]{1,0:T(8,128)S(1)}, f32[32,128]{...) custom-call(f32[96,16,128]{2,1,0:T(8,128)} %bitcast.26, s32[16,128]{1,0:T(8,128)} %bitcast.28, ...), custom_call_target="tpu_custom_call" | custom-call | tf_op jit(solution)/shard_map/pack/pallas_call | solution.py:198
  3.5 3.3 %collective-permute-start = (f32[32,128]{1,0:T(8,128)S(1)}, f32[32,128]{1,0:T(8,128)S(1)}, u32[]{:S(2)}, u32[]{:S(2)}) collective-permute-start(f32[32,128]{1,0:T(8,128)S(1)} %get-tuple-element.24), channel_id=1, source_target_pairs={{0,1},{1,0},{2,3},{3,2},{4,5},{5,4},{6,7},{7,6},{8,9},{9,8},{10,11... | collective-permute-start | bytes 49160 | tf_op jit(solution)/shard_map/ppermute | solution.py:584
  6.8 4.8 %collective-permute-start.4 = (f32[96,8,128]{2,1,0:T(8,128)S(1)}, f32[96,8,128]{2,1,0:T(8,128)S(1)}, u32[]{:S(2)}, u32[]{:S(2)}) collective-permute-start(f32[96,8,128]{2,1,0:T(8,128)S(1)} %get-tuple-element.31), channel_id=1, source_target_pairs={{0,60},{4,0},{8,4},{12,8},{16,12},{20,16},{24,20},{28,24},{32,28},... | collective-permute-start | bytes 1179656 | tf_op jit(solution)/shard_map/ppermute | solution.py:580
  11.6 0.0 collective-permute-done.from_core
  11.6 0.1 strike_faces.1
  11.7 1.4 %collective-permute-start.1 = (f32[96,8,128]{2,1,0:T(8,128)S(1)}, f32[96,8,128]{2,1,0:T(8,128)S(1)}, u32[]{:S(2)}, u32[]{:S(2)}) collective-permute-start(f32[96,8,128]{2,1,0:T(8,128)S(1)} %get-tuple-element.28), channel_id=1, source_target_pairs={{0,64},{64,128},{128,192},{192,0},{1,65},{65,129},{129,193},{193,1... | collective-permute-start | bytes 1179656 | tf_op jit(solution)/shard_map/ppermute | solution.py:580
  13.1 1.5 %collective-permute-start.2 = (f32[96,8,128]{2,1,0:T(8,128)S(1)}, f32[96,8,128]{2,1,0:T(8,128)S(1)}, u32[]{:S(2)}, u32[]{:S(2)}) collective-permute-start(f32[96,8,128]{2,1,0:T(8,128)S(1)} %get-tuple-element.29), channel_id=1, source_target_pairs={{0,192},{64,0},{128,64},{192,128},{1,193},{65,1},{129,65},{193,129... | collective-permute-start | bytes 1179656 | tf_op jit(solution)/shard_map/ppermute | solution.py:580
  14.6 3.2 %collective-permute-start.5 = (f32[40,128]{1,0:T(8,128)S(1)}, f32[40,128]{1,0:T(8,128)S(1)}, u32[]{:S(2)}, u32[]{:S(2)}) collective-permute-start(f32[40,128]{1,0:T(8,128)S(1)} %get-tuple-element.33), channel_id=1, source_target_pairs={{0,3},{1,2},{2,1},{3,0},{4,7},{5,6},{6,5},{7,4},{8,11},{9,10},{10,... | collective-permute-start | bytes 61448 | tf_op jit(solution)/shard_map/ppermute | solution.py:630
  17.8 5.1 %within.1 = (f32[3072,128]{1,0:T(8,128)S(1)}, f32[12,16,12,16,128]{4,3,2,1,0:T(8,128)S(1)}) custom-call(f32[48,128]{1,0:T(8,128)S(1)} %get-tuple-element.22.scales, f32[1536,128]{1,0:T(8,128)S(1)} %bitcast.14, f32[32,128]{1,0:T(8,128)S(1)} %collective-permute-done.from_core, bf16[12,16,12,16,128]{4,3,2,1,0:T(8,128)(2,1)} %bitcast.25), custom_call_target="tpu_custom_call" | custom-call | flops 4000000 | bytes 14000000 | tf_op jit(solution)/shard_map/within/pallas_call | solution.py:316
  22.9 4.1 %collective-permute-done.5.from_cross = f32[40,128]{1,0:T(8,128)S(1)} collective-permute-done((f32[40,128]{1,0:T(8,128)S(1)}, f32[40,128]{1,0:T(8,128)S(1)}, u32[]{:S(2)}, u32[]{:S(2)}) %collective-permute-start.5) | collective-permute-done | bytes 20512 | tf_op jit(solution)/shard_map/ppermute | solution.py:630
  27.0 0.0 collective-permute-done.2.xa
  27.0 0.0 copy-start
  27.0 0.0 copy-start.1
  27.1 0.0 copy-start.2
  27.1 0.0 copy-start.3
  27.1 6.1 %gram.1 = (f32[384,128]{1,0:T(8,128)S(1)}, f32[384,128]{1,0:T(8,128)S(1)}, f32[6144,128]{1,0:T(8,128)S(1)}, f32[8,384]{1,0:T(8,128)S(1)}) custom-call(f32[48,128]{1,0:T(8,128)S(1)} %get-tuple-element.22.scales, f32[3072,128]{1,0:T(8,128)S(1)} %get-tuple-element.25.within, f32[12,16,12,16,128]{4,3,2,1,0:T(8,128)S(1)} %get-tuple-element.26.receiver, ...), custom_call_target="tpu_custom_call" | custom-call | flops 1200000000 | bytes 8000000 | tf_op jit(solution)/shard_map/gram/pallas_call | solution.py:430
  33.2 0.3 collective-permute-start.6
  33.5 1.2 %collective-permute-done.6 = f32[384,128]{1,0:T(8,128)S(1)} collective-permute-done((f32[384,128]{1,0:T(8,128)S(1)}, f32[384,128]{1,0:T(8,128)S(1)}, u32[]{:S(2)}, u32[]{:S(2)}) %collective-permute-start.6) | collective-permute-done | bytes 196640 | tf_op jit(solution)/shard_map/ppermute | solution.py:584
  34.7 13.0 %all_to_all.15 = f32[16,24,128]{2,1,0:T(8,128)S(1)} all-to-all(f32[16,24,128]{2,1,0:T(8,128)S(1)} %bitcast.27), channel_id=1, replica_groups=mesh['y'=4,'z'=8,'xlo'=2,'xhi'=2,'core'=2] {'y','xlo','xhi'}, dimensions={0} | all-to-all | bytes 393216 | tf_op jit(solution)/shard_map/all_to_all | solution.py:588
  47.8 15.2 %all_to_all.16 = f32[8,24,128]{2,1,0:T(8,128)S(1)} all-to-all(f32[8,24,128]{2,1,0:T(8,128)S(1)} %broadcast_in_dim.6), channel_id=1, replica_groups=mesh['y'=4,'z'=8,'xlo'=2,'xhi'=2,'core'=2] {'z'}, dimensions={0} | all-to-all | bytes 196608 | tf_op jit(solution)/shard_map/all_to_all | solution.py:588
  63.0 10.1 %all_to_all.17 = f32[16,24,128]{2,1,0:T(8,128)S(1)} all-to-all(f32[16,24,128]{2,1,0:T(8,128)S(1)} %broadcast_in_dim.7), channel_id=1, replica_groups=mesh['y'=4,'z'=8,'xlo'=2,'xhi'=2,'core'=2] {'y','xlo','xhi'}, dimensions={0} | all-to-all | bytes 393216 | tf_op jit(solution)/shard_map/all_to_all | solution.py:588
  73.2 4.3 %collective-permute-start.7 = (f32[384,128]{1,0:T(8,128)S(1)}, f32[384,128]{1,0:T(8,128)S(1)}, u32[]{:S(2)}, u32[]{:S(2)}) collective-permute-start(f32[384,128]{1,0:T(8,128)S(1)} %bitcast.15), channel_id=1, source_target_pairs={{0,1},{1,0},{2,3},{3,2},{4,5},{5,4},{6,7},{7,6},{8,9},{9,8},{10,11... | collective-permute-start | bytes 589832 | tf_op jit(solution)/shard_map/ppermute | solution.py:584
  77.5 1.1 %collective-permute-done.7.other = f32[384,128]{1,0:T(8,128)S(1)} collective-permute-done((f32[384,128]{1,0:T(8,128)S(1)}, f32[384,128]{1,0:T(8,128)S(1)}, u32[]{:S(2)}, u32[]{:S(2)}) %collective-permute-start.7) | collective-permute-done | bytes 196640 | tf_op jit(solution)/shard_map/ppermute | solution.py:584
  78.6 3.3 %chain.1 = (f32[16,128]{1,0:T(8,128)}, f32[16,128]{1,0:T(8,128)}, f32[2,16,96]{2,1,0:T(8,128)}) custom-call(f32[384,128]{1,0:T(8,128)S(1)} %bitcast.16, f32[384,128]{1,0:T(8,128)S(1)} %collective-permute-done.7.other, f32[8,384]{1,0:T(8,128)S(1)} %get-tuple-element.36.stats, f32[6144,128]{1,0:T(8,128)S(1)} %get-tuple-element.37.cells, ...), custom_call_target="tpu_custom_call" | custom-call | tf_op jit(solution)/shard_map/chain/pallas_call | solution.py:565
  (13 shorter events, 0.1 us)
Async XLA Ops:
  3.5 8.1 %collective-permute-start = (f32[32,128]{1,0:T(8,128)S(1)}, f32[32,128]{1,0:T(8,128)S(1)}, u32[]{:S(2)}, u32[]{:S(2)}) collective-permute-start(f32[32,128]{1,0:T(8,128)S(1)} %get-tuple-element.24), channel_id=1, source_target_pairs={{0,1},{1,0},{2,3},{3,2},{4,5},{5,4},{6,7},{7,6},{8,9},{9,8},{10,11... | collective-permute-start | bytes 49160 | tf_op jit(solution)/shard_map/ppermute | solution.py:584
  6.8 20.2 %collective-permute-start.3 = (f32[96,8,128]{2,1,0:T(8,128)S(1)}, f32[96,8,128]{2,1,0:T(8,128)S(1)}, u32[]{:S(2)}, u32[]{:S(2)}) collective-permute-start(f32[96,8,128]{2,1,0:T(8,128)S(1)} %get-tuple-element.30), channel_id=1, source_target_pairs={{0,4},{4,8},{8,12},{12,16},{16,20},{20,24},{24,28},{28,32},{32,36}... | collective-permute-start | bytes 1179656 | tf_op jit(solution)/shard_map/ppermute | solution.py:580
  6.8 20.2 %collective-permute-start.4 = (f32[96,8,128]{2,1,0:T(8,128)S(1)}, f32[96,8,128]{2,1,0:T(8,128)S(1)}, u32[]{:S(2)}, u32[]{:S(2)}) collective-permute-start(f32[96,8,128]{2,1,0:T(8,128)S(1)} %get-tuple-element.31), channel_id=1, source_target_pairs={{0,60},{4,0},{8,4},{12,8},{16,12},{20,16},{24,20},{28,24},{32,28},... | collective-permute-start | bytes 1179656 | tf_op jit(solution)/shard_map/ppermute | solution.py:580
  11.7 15.3 %collective-permute-start.1 = (f32[96,8,128]{2,1,0:T(8,128)S(1)}, f32[96,8,128]{2,1,0:T(8,128)S(1)}, u32[]{:S(2)}, u32[]{:S(2)}) collective-permute-start(f32[96,8,128]{2,1,0:T(8,128)S(1)} %get-tuple-element.28), channel_id=1, source_target_pairs={{0,64},{64,128},{128,192},{192,0},{1,65},{65,129},{129,193},{193,1... | collective-permute-start | bytes 1179656 | tf_op jit(solution)/shard_map/ppermute | solution.py:580
  13.1 13.9 %collective-permute-start.2 = (f32[96,8,128]{2,1,0:T(8,128)S(1)}, f32[96,8,128]{2,1,0:T(8,128)S(1)}, u32[]{:S(2)}, u32[]{:S(2)}) collective-permute-start(f32[96,8,128]{2,1,0:T(8,128)S(1)} %get-tuple-element.29), channel_id=1, source_target_pairs={{0,192},{64,0},{128,64},{192,128},{1,193},{65,1},{129,65},{193,129... | collective-permute-start | bytes 1179656 | tf_op jit(solution)/shard_map/ppermute | solution.py:580
  14.6 12.4 %collective-permute-start.5 = (f32[40,128]{1,0:T(8,128)S(1)}, f32[40,128]{1,0:T(8,128)S(1)}, u32[]{:S(2)}, u32[]{:S(2)}) collective-permute-start(f32[40,128]{1,0:T(8,128)S(1)} %get-tuple-element.33), channel_id=1, source_target_pairs={{0,3},{1,2},{2,1},{3,0},{4,7},{5,6},{6,5},{7,4},{8,11},{9,10},{10,... | collective-permute-start | bytes 61448 | tf_op jit(solution)/shard_map/ppermute | solution.py:630
  27.0 51.5 %copy-start = (f32[2,96,16]{1,2,0:T(8,128)S(1)}, f32[2,96,16]{1,2,0:T(8,128)}, u32[]{:S(2)}) copy-start(f32[2,96,16]{1,2,0:T(8,128)} %param.12) | copy-start | bytes 36868
  27.0 51.5 %copy-start.1 = (s32[96,16]{0,1:T(8,128)S(1)}, s32[96,16]{0,1:T(8,128)}, u32[]{:S(2)}) copy-start(s32[96,16]{0,1:T(8,128)} %param.14) | copy-start | bytes 18436
  27.1 51.5 %copy-start.2 = (s32[96,16]{0,1:T(8,128)S(1)}, s32[96,16]{0,1:T(8,128)}, u32[]{:S(2)}) copy-start(s32[96,16]{0,1:T(8,128)} %param.15) | copy-start | bytes 18436
  27.1 51.5 %copy-start.3 = (s32[96]{0:T(128)S(1)}, s32[96]{0:T(128)}, u32[]{:S(2)}) copy-start(s32[96]{0:T(128)} %param.13) | copy-start | bytes 1156
  33.2 1.5 %collective-permute-start.6 = (f32[384,128]{1,0:T(8,128)S(1)}, f32[384,128]{1,0:T(8,128)S(1)}, u32[]{:S(2)}, u32[]{:S(2)}) collective-permute-start(f32[384,128]{1,0:T(8,128)S(1)} %get-tuple-element.35), channel_id=1, source_target_pairs={{0,1},{1,0},{2,3},{3,2},{4,5},{5,4},{6,7},{7,6},{8,9},{9,8},{10,11... | collective-permute-start | bytes 589832 | tf_op jit(solution)/shard_map/ppermute | solution.py:584
  73.2 5.4 %collective-permute-start.7 = (f32[384,128]{1,0:T(8,128)S(1)}, f32[384,128]{1,0:T(8,128)S(1)}, u32[]{:S(2)}, u32[]{:S(2)}) collective-permute-start(f32[384,128]{1,0:T(8,128)S(1)} %bitcast.15), channel_id=1, source_target_pairs={{0,1},{1,0},{2,3},{3,2},{4,5},{5,4},{6,7},{7,6},{8,9},{9,8},{10,11... | collective-permute-start | bytes 589832 | tf_op jit(solution)/shard_map/ppermute | solution.py:584

commit v10 on v9

--- a/solution.py
+++ b/solution.py
@@ -52,7 +52,9 @@
     for b in range(BINS):
         here = bins == b
         for k in range(2):
-            parts.append(jnp.sum(jnp.where(here, values[k], 0.0), axis=0, keepdims=True))
+            if k == 0 or len(values) == 2:
+                part = jnp.sum(jnp.where(here, values[k], 0.0), axis=0, keepdims=True)
+            parts.append(part)
     table = jnp.concatenate(parts, axis=0)
     return jnp.concatenate(
         [
@@ -79,7 +81,7 @@
     mask = window.astype(F32)
     rhs = [observed[k] * mask for k in range(2)]
     total = spread(rhs, bins, tensor)
-    count = spread([mask, mask], bins, tensor)
+    count = spread([mask], bins, tensor)
     mean = total / jnp.maximum(count, 1.0)
     near = pick(mean, bins, tensor)
     rest = [rhs[k] - near[k] * mask for k in range(2)]
@@ -126,7 +128,7 @@
             )
         )
     ]
-    for copy in copies:
+    for copy in copies[1:] + copies[:1]:
         copy.start()
     for copy in copies[1:]:
         copy.wait()
@@ -395,9 +397,9 @@
     lax.fori_loop(0, BINS, body, 0)
 
     total = jnp.zeros((ROWS, ROWS), F32)
-    for plane in range(0, PLANES, 2):
+    for plane in range(0, PLANES, 4):
         both = jnp.concatenate(
-            [cells[pl.ds(plane + i, ROWS, stride=PLANES), :] for i in range(2)], axis=1
+            [cells[pl.ds(plane + i, ROWS, stride=PLANES), :] for i in range(4)], axis=1
         )
         high = both.astype(BF16)
         low = (both - high.astype(F32)).astype(BF16)
@@ -517,11 +519,15 @@
     answer = jnp.zeros((1, ROWS), F32)
     phi_bar, rho_bar = beta, alpha
     for _ in range(ITERS):
-        scale, row = -alpha * scale, image / alpha - alpha * row
+        model_image = image / alpha
+        scale, row = -alpha * scale, model_image - alpha * row
+        back = scale * sums + count * row
+        back_image = product(back)
         beta = data_norm(scale, row)
-        scale, row = scale / beta, row / beta
-        raw = scale * sums + count * row - beta * model
-        image = product(raw)
+        inverse = one / beta
+        scale, row = scale * inverse, row * inverse
+        raw = back * inverse - beta * model
+        image = back_image * inverse - beta * model_image
         alpha = norm_of(total(raw * image))
         model = raw / alpha
         rho = jnp.sqrt(rho_bar * rho_bar + beta * beta)
@@ -538,15 +544,18 @@
     )
     coef[1] = jnp.broadcast_to(column(model * cell_scale), (ROWS, LANES))
 
-    def body(n, sums_of):
-        value = tile(cells, n)
+    def body(n, totals):
+        one, two = tile(cells, 2 * n), tile(cells, 2 * n + 1)
         return (
-            sums_of[0] + coef[0, pl.ds(n, 1), :] * value,
-            sums_of[1] + coef[1, pl.ds(n, 1), :] * value,
+            totals[0] + coef[0, pl.ds(2 * n, 1), :] * one,
+            totals[1] + coef[1, pl.ds(2 * n, 1), :] * one,
+            totals[2] + coef[0, pl.ds(2 * n + 1, 1), :] * two,
+            totals[3] + coef[1, pl.ds(2 * n + 1, 1), :] * two,
         )
 
-    start = (jnp.zeros((PLANES, LANES), F32), jnp.zeros((PLANES, LANES), F32))
-    first, second = lax.fori_loop(0, ROWS, body, start, unroll=16)
+    start = (jnp.zeros((PLANES, LANES), F32),) * 4
+    totals = lax.fori_loop(0, ROWS // 2, body, start, unroll=16)
+    first, second = totals[0] + totals[2], totals[1] + totals[3]
     update[...] = first
     direction[...] = second
 

time: 82.1 us -> 81.5 us (level)
  no operation moved by 1% of the time
where the time goes in v10:
time: 81.5 us; the launch traced here: 81.2 us
  blocking collectives  38.4 us (47%)
  starting transfers between devices  18.8 us (23%)
  Pallas kernels  16.8 us (21%)
  waiting for transfers between devices  6.41 us (8%)
    all_to_all x3, blocking collectives, exchange(): return lax.all_to_all(value, axes, 0, 0, tiled=True)  38.4 us
    ppermute x3, starting transfers between devices, swap(): return lax.ppermute(value, axis, [(0, 1), (1, 0)])  7.94 us
    ppermute x4, starting transfers between devices, shift(): lax.ppermute(value, axes, [(i, (i + step) % count) for i in range(count)])  7.67 us
    pallas_call x1, Pallas kernels, gram(): pl.pallas_call(gram_kernel, out_shape=(half, half, jax.ShapeDtypeStruct((...  5.99 us
    pallas_call x1, Pallas kernels, within(): pl.pallas_call(within_kernel, out_shape=(jax.ShapeDtypeStruct((BINS * 12...  5.08 us
    ppermute x1, waiting for transfers between devices, per_device(): from_cross = lax.ppermute(to_cross, GZ, [(i, 3 - i) for i in range(4)])  4.1 us
    ppermute x1, starting transfers between devices, per_device(): from_cross = lax.ppermute(to_cross, GZ, [(i, 3 - i) for i in range(4)])  3.2 us
    pallas_call x1, Pallas kernels, chain(): pl.pallas_call(chain_kernel, out_shape=(field, field, jax.ShapeDtypeStruc...  2.93 us
  transfers between devices with their start and end apart: 8, of which 3 were waited for; matrix products, arithmetic and copies ran while one was open for 0% of the time, Pallas kernels for 6%

profile of v10, /device:TPU:1, one launch (start us, length us, event | category | flops | bytes accessed | tf_op | source)
XLA Modules:
  0.0 81.2 jit_solution(6322552758908728993)
XLA Ops:
  0.6 2.7 %pack.1 = (f32[96,16,128]{2,1,0:T(8,128)S(1)}, f32[96,8,128]{2,1,0:T(8,128)S(1)}, f32[96,8,128]{2,1,0:T(8,128)S(1)}, f32[32,128]{1,0:T(8,128)S(1)}, f32[32,128]{...) custom-call(f32[96,16,128]{2,1,0:T(8,128)} %bitcast.26, s32[16,128]{1,0:T(8,128)} %bitcast.28, ...), custom_call_target="tpu_custom_call" | custom-call | tf_op jit(solution)/shard_map/pack/pallas_call | solution.py:200
  3.3 3.3 %collective-permute-start = (f32[32,128]{1,0:T(8,128)S(1)}, f32[32,128]{1,0:T(8,128)S(1)}, u32[]{:S(2)}, u32[]{:S(2)}) collective-permute-start(f32[32,128]{1,0:T(8,128)S(1)} %get-tuple-element.24), channel_id=1, source_target_pairs={{0,1},{1,0},{2,3},{3,2},{4,5},{5,4},{6,7},{7,6},{8,9},{9,8},{10,11... | collective-permute-start | bytes 49160 | tf_op jit(solution)/shard_map/ppermute | solution.py:593
  6.7 4.8 %collective-permute-start.4 = (f32[96,8,128]{2,1,0:T(8,128)S(1)}, f32[96,8,128]{2,1,0:T(8,128)S(1)}, u32[]{:S(2)}, u32[]{:S(2)}) collective-permute-start(f32[96,8,128]{2,1,0:T(8,128)S(1)} %get-tuple-element.31), channel_id=1, source_target_pairs={{0,60},{4,0},{8,4},{12,8},{16,12},{20,16},{24,20},{28,24},{32,28},... | collective-permute-start | bytes 1179656 | tf_op jit(solution)/shard_map/ppermute | solution.py:589
  11.4 0.0 collective-permute-done.from_core
  11.4 0.1 strike_faces.1
  11.5 1.4 %collective-permute-start.1 = (f32[96,8,128]{2,1,0:T(8,128)S(1)}, f32[96,8,128]{2,1,0:T(8,128)S(1)}, u32[]{:S(2)}, u32[]{:S(2)}) collective-permute-start(f32[96,8,128]{2,1,0:T(8,128)S(1)} %get-tuple-element.28), channel_id=1, source_target_pairs={{0,64},{64,128},{128,192},{192,0},{1,65},{65,129},{129,193},{193,1... | collective-permute-start | bytes 1179656 | tf_op jit(solution)/shard_map/ppermute | solution.py:589
  12.9 1.5 %collective-permute-start.2 = (f32[96,8,128]{2,1,0:T(8,128)S(1)}, f32[96,8,128]{2,1,0:T(8,128)S(1)}, u32[]{:S(2)}, u32[]{:S(2)}) collective-permute-start(f32[96,8,128]{2,1,0:T(8,128)S(1)} %get-tuple-element.29), channel_id=1, source_target_pairs={{0,192},{64,0},{128,64},{192,128},{1,193},{65,1},{129,65},{193,129... | collective-permute-start | bytes 1179656 | tf_op jit(solution)/shard_map/ppermute | solution.py:589
  14.4 3.2 %collective-permute-start.5 = (f32[40,128]{1,0:T(8,128)S(1)}, f32[40,128]{1,0:T(8,128)S(1)}, u32[]{:S(2)}, u32[]{:S(2)}) collective-permute-start(f32[40,128]{1,0:T(8,128)S(1)} %get-tuple-element.33), channel_id=1, source_target_pairs={{0,3},{1,2},{2,1},{3,0},{4,7},{5,6},{6,5},{7,4},{8,11},{9,10},{10,... | collective-permute-start | bytes 61448 | tf_op jit(solution)/shard_map/ppermute | solution.py:639
  17.6 5.1 %within.1 = (f32[3072,128]{1,0:T(8,128)S(1)}, f32[12,16,12,16,128]{4,3,2,1,0:T(8,128)S(1)}) custom-call(f32[48,128]{1,0:T(8,128)S(1)} %get-tuple-element.22.scales, f32[1536,128]{1,0:T(8,128)S(1)} %bitcast.14, f32[32,128]{1,0:T(8,128)S(1)} %collective-permute-done.from_core, bf16[12,16,12,16,128]{4,3,2,1,0:T(8,128)(2,1)} %bitcast.25), custom_call_target="tpu_custom_call" | custom-call | flops 4000000 | bytes 14000000 | tf_op jit(solution)/shard_map/within/pallas_call | solution.py:318
  22.7 4.1 %collective-permute-done.5.from_cross = f32[40,128]{1,0:T(8,128)S(1)} collective-permute-done((f32[40,128]{1,0:T(8,128)S(1)}, f32[40,128]{1,0:T(8,128)S(1)}, u32[]{:S(2)}, u32[]{:S(2)}) %collective-permute-start.5) | collective-permute-done | bytes 20512 | tf_op jit(solution)/shard_map/ppermute | solution.py:639
  26.8 0.0 collective-permute-done.4.ya
  26.9 0.0 copy-start
  26.9 0.0 copy-start.1
  26.9 0.0 copy-start.2
  26.9 0.0 copy-start.3
  26.9 6.0 %gram.1 = (f32[384,128]{1,0:T(8,128)S(1)}, f32[384,128]{1,0:T(8,128)S(1)}, f32[6144,128]{1,0:T(8,128)S(1)}, f32[8,384]{1,0:T(8,128)S(1)}) custom-call(f32[48,128]{1,0:T(8,128)S(1)} %get-tuple-element.22.scales, f32[3072,128]{1,0:T(8,128)S(1)} %get-tuple-element.25.within, f32[12,16,12,16,128]{4,3,2,1,0:T(8,128)S(1)} %get-tuple-element.26.receiver, ...), custom_call_target="tpu_custom_call" | custom-call | flops 1200000000 | bytes 8000000 | tf_op jit(solution)/shard_map/gram/pallas_call | solution.py:432
  32.9 0.3 collective-permute-start.6
  33.2 1.2 %collective-permute-done.6 = f32[384,128]{1,0:T(8,128)S(1)} collective-permute-done((f32[384,128]{1,0:T(8,128)S(1)}, f32[384,128]{1,0:T(8,128)S(1)}, u32[]{:S(2)}, u32[]{:S(2)}) %collective-permute-start.6) | collective-permute-done | bytes 196640 | tf_op jit(solution)/shard_map/ppermute | solution.py:593
  34.5 13.0 %all_to_all.15 = f32[16,24,128]{2,1,0:T(8,128)S(1)} all-to-all(f32[16,24,128]{2,1,0:T(8,128)S(1)} %bitcast.27), channel_id=1, replica_groups=mesh['y'=4,'z'=8,'xlo'=2,'xhi'=2,'core'=2] {'y','xlo','xhi'}, dimensions={0} | all-to-all | bytes 393216 | tf_op jit(solution)/shard_map/all_to_all | solution.py:597
  47.5 15.2 %all_to_all.16 = f32[8,24,128]{2,1,0:T(8,128)S(1)} all-to-all(f32[8,24,128]{2,1,0:T(8,128)S(1)} %broadcast_in_dim.6), channel_id=1, replica_groups=mesh['y'=4,'z'=8,'xlo'=2,'xhi'=2,'core'=2] {'z'}, dimensions={0} | all-to-all | bytes 196608 | tf_op jit(solution)/shard_map/all_to_all | solution.py:597
  62.8 10.1 %all_to_all.17 = f32[16,24,128]{2,1,0:T(8,128)S(1)} all-to-all(f32[16,24,128]{2,1,0:T(8,128)S(1)} %broadcast_in_dim.7), channel_id=1, replica_groups=mesh['y'=4,'z'=8,'xlo'=2,'xhi'=2,'core'=2] {'y','xlo','xhi'}, dimensions={0} | all-to-all | bytes 393216 | tf_op jit(solution)/shard_map/all_to_all | solution.py:597
  72.9 4.3 %collective-permute-start.7 = (f32[384,128]{1,0:T(8,128)S(1)}, f32[384,128]{1,0:T(8,128)S(1)}, u32[]{:S(2)}, u32[]{:S(2)}) collective-permute-start(f32[384,128]{1,0:T(8,128)S(1)} %bitcast.15), channel_id=1, source_target_pairs={{0,1},{1,0},{2,3},{3,2},{4,5},{5,4},{6,7},{7,6},{8,9},{9,8},{10,11... | collective-permute-start | bytes 589832 | tf_op jit(solution)/shard_map/ppermute | solution.py:593
  77.2 1.1 %collective-permute-done.7.other = f32[384,128]{1,0:T(8,128)S(1)} collective-permute-done((f32[384,128]{1,0:T(8,128)S(1)}, f32[384,128]{1,0:T(8,128)S(1)}, u32[]{:S(2)}, u32[]{:S(2)}) %collective-permute-start.7) | collective-permute-done | bytes 196640 | tf_op jit(solution)/shard_map/ppermute | solution.py:593
  78.3 2.9 %chain.1 = (f32[16,128]{1,0:T(8,128)}, f32[16,128]{1,0:T(8,128)}, f32[2,16,96]{2,1,0:T(8,128)}) custom-call(f32[384,128]{1,0:T(8,128)S(1)} %bitcast.16, f32[384,128]{1,0:T(8,128)S(1)} %collective-permute-done.7.other, f32[8,384]{1,0:T(8,128)S(1)} %get-tuple-element.36.stats, f32[6144,128]{1,0:T(8,128)S(1)} %get-tuple-element.37.cells, ...), custom_call_target="tpu_custom_call" | custom-call | tf_op jit(solution)/shard_map/chain/pallas_call | solution.py:574
  (13 shorter events, 0.1 us)
Async XLA Ops:
  3.3 8.1 %collective-permute-start = (f32[32,128]{1,0:T(8,128)S(1)}, f32[32,128]{1,0:T(8,128)S(1)}, u32[]{:S(2)}, u32[]{:S(2)}) collective-permute-start(f32[32,128]{1,0:T(8,128)S(1)} %get-tuple-element.24), channel_id=1, source_target_pairs={{0,1},{1,0},{2,3},{3,2},{4,5},{5,4},{6,7},{7,6},{8,9},{9,8},{10,11... | collective-permute-start | bytes 49160 | tf_op jit(solution)/shard_map/ppermute | solution.py:593
  6.7 20.2 %collective-permute-start.3 = (f32[96,8,128]{2,1,0:T(8,128)S(1)}, f32[96,8,128]{2,1,0:T(8,128)S(1)}, u32[]{:S(2)}, u32[]{:S(2)}) collective-permute-start(f32[96,8,128]{2,1,0:T(8,128)S(1)} %get-tuple-element.30), channel_id=1, source_target_pairs={{0,4},{4,8},{8,12},{12,16},{16,20},{20,24},{24,28},{28,32},{32,36}... | collective-permute-start | bytes 1179656 | tf_op jit(solution)/shard_map/ppermute | solution.py:589
  6.7 20.2 %collective-permute-start.4 = (f32[96,8,128]{2,1,0:T(8,128)S(1)}, f32[96,8,128]{2,1,0:T(8,128)S(1)}, u32[]{:S(2)}, u32[]{:S(2)}) collective-permute-start(f32[96,8,128]{2,1,0:T(8,128)S(1)} %get-tuple-element.31), channel_id=1, source_target_pairs={{0,60},{4,0},{8,4},{12,8},{16,12},{20,16},{24,20},{28,24},{32,28},... | collective-permute-start | bytes 1179656 | tf_op jit(solution)/shard_map/ppermute | solution.py:589
  11.5 15.3 %collective-permute-start.1 = (f32[96,8,128]{2,1,0:T(8,128)S(1)}, f32[96,8,128]{2,1,0:T(8,128)S(1)}, u32[]{:S(2)}, u32[]{:S(2)}) collective-permute-start(f32[96,8,128]{2,1,0:T(8,128)S(1)} %get-tuple-element.28), channel_id=1, source_target_pairs={{0,64},{64,128},{128,192},{192,0},{1,65},{65,129},{129,193},{193,1... | collective-permute-start | bytes 1179656 | tf_op jit(solution)/shard_map/ppermute | solution.py:589
  12.9 13.9 %collective-permute-start.2 = (f32[96,8,128]{2,1,0:T(8,128)S(1)}, f32[96,8,128]{2,1,0:T(8,128)S(1)}, u32[]{:S(2)}, u32[]{:S(2)}) collective-permute-start(f32[96,8,128]{2,1,0:T(8,128)S(1)} %get-tuple-element.29), channel_id=1, source_target_pairs={{0,192},{64,0},{128,64},{192,128},{1,193},{65,1},{129,65},{193,129... | collective-permute-start | bytes 1179656 | tf_op jit(solution)/shard_map/ppermute | solution.py:589
  14.4 12.4 %collective-permute-start.5 = (f32[40,128]{1,0:T(8,128)S(1)}, f32[40,128]{1,0:T(8,128)S(1)}, u32[]{:S(2)}, u32[]{:S(2)}) collective-permute-start(f32[40,128]{1,0:T(8,128)S(1)} %get-tuple-element.33), channel_id=1, source_target_pairs={{0,3},{1,2},{2,1},{3,0},{4,7},{5,6},{6,5},{7,4},{8,11},{9,10},{10,... | collective-permute-start | bytes 61448 | tf_op jit(solution)/shard_map/ppermute | solution.py:639
  26.9 51.4 %copy-start = (f32[2,96,16]{1,2,0:T(8,128)S(1)}, f32[2,96,16]{1,2,0:T(8,128)}, u32[]{:S(2)}) copy-start(f32[2,96,16]{1,2,0:T(8,128)} %param.12) | copy-start | bytes 36868
  26.9 51.4 %copy-start.1 = (s32[96,16]{0,1:T(8,128)S(1)}, s32[96,16]{0,1:T(8,128)}, u32[]{:S(2)}) copy-start(s32[96,16]{0,1:T(8,128)} %param.14) | copy-start | bytes 18436
  26.9 51.4 %copy-start.2 = (s32[96,16]{0,1:T(8,128)S(1)}, s32[96,16]{0,1:T(8,128)}, u32[]{:S(2)}) copy-start(s32[96,16]{0,1:T(8,128)} %param.15) | copy-start | bytes 18436
  26.9 51.4 %copy-start.3 = (s32[96]{0:T(128)S(1)}, s32[96]{0:T(128)}, u32[]{:S(2)}) copy-start(s32[96]{0:T(128)} %param.13) | copy-start | bytes 1156
  32.9 1.5 %collective-permute-start.6 = (f32[384,128]{1,0:T(8,128)S(1)}, f32[384,128]{1,0:T(8,128)S(1)}, u32[]{:S(2)}, u32[]{:S(2)}) collective-permute-start(f32[384,128]{1,0:T(8,128)S(1)} %get-tuple-element.35), channel_id=1, source_target_pairs={{0,1},{1,0},{2,3},{3,2},{4,5},{5,4},{6,7},{7,6},{8,9},{9,8},{10,11... | collective-permute-start | bytes 589832 | tf_op jit(solution)/shard_map/ppermute | solution.py:593
  72.9 5.4 %collective-permute-start.7 = (f32[384,128]{1,0:T(8,128)S(1)}, f32[384,128]{1,0:T(8,128)S(1)}, u32[]{:S(2)}, u32[]{:S(2)}) collective-permute-start(f32[384,128]{1,0:T(8,128)S(1)} %bitcast.15), channel_id=1, source_target_pairs={{0,1},{1,0},{2,3},{3,2},{4,5},{5,4},{6,7},{7,6},{8,9},{9,8},{10,11... | collective-permute-start | bytes 589832 | tf_op jit(solution)/shard_map/ppermute | solution.py:593

commit v11 on v10

--- a/solution.py
+++ b/solution.py
@@ -111,7 +111,7 @@
 
 def pack_kernel(
     src_in, ids_in, table_in, observed_in, tensor_in, bins_in, window_in,
-    src, y_lo, y_hi, to_core, to_cross, stats, scales,
+    src, to_side, to_pair, to_core, to_cross, stats, scales,
     ids, table, observed, tensor, bins, window, sparse, sems,
 ):
     copies = [
@@ -151,8 +151,11 @@
     high = [
         half - jnp.where(y == 2, 8.0 * pltpu.roll(half, 7, 1), 0.0) for half in (first, second)
     ]
-    y_lo[...] = jnp.where(y < 2, low[1], pltpu.roll(low[0], 2, 1))
-    y_hi[...] = jnp.where(y < 2, pltpu.roll(high[0], 6, 1), high[1])
+    lower = jnp.where(y < 2, low[1], pltpu.roll(low[0], 2, 1))
+    higher = jnp.where(y < 2, pltpu.roll(high[0], 6, 1), pltpu.roll(high[1], 4, 1))
+    odd = lax.axis_index("xlo") == 1
+    to_side[...] = jnp.where(odd, higher, lower)
+    to_pair[...] = jnp.where(odd, lower, higher)
 
     lane = lane_ids((FIELDS, LANES))
     low = jnp.zeros((FIELDS, LANES), F32)
@@ -338,7 +341,7 @@
 
 
 def gram_kernel(
-    scales, within, receiver, xb, xa, yb, ya, own, from_core, from_cross,
+    scales, within, receiver, xb, xa, from_side, from_pair, own, from_core, from_cross,
     keep, send, cells, stats, ends, sparse
 ):
     lane = lane_ids((FIELDS, LANES))
@@ -350,9 +353,10 @@
     x_before, x_after = ends_of(GX)
     y_before, y_after = ends_of(GY)
     low_y = (lax.broadcasted_iota(jnp.int32, (8, LANES), 0) & 3) < 2
-    side = jnp.where(low_y, y_before, y_after)
+    inside = jnp.where(low_y, y_before, y_after)
+    of_pair = low_y == (lax.axis_index("xlo") == 1)
     scale_x = (scales[0:8, :] * x_before, scales[8:16, :] * x_after)
-    scale_y = (scales[16:24, :] * side, scales[24:32, :] * side)
+    scale_y = (scales[16:24, :] * inside, scales[24:32, :] * inside)
     scale_z = tile(scales, 2)
 
     def body(b, carry):
@@ -360,9 +364,9 @@
             return jnp.concatenate([scale_x[0] * xb[field], scale_x[1] * xa[field]], axis=0)
 
         def from_y(field):
-            below, above = yb[field], ya[field]
-            first = jnp.where(low_y, below, above)
-            second = jnp.where(low_y, pltpu.roll(below, 6, 0), pltpu.roll(above, 2, 0))
+            side, pair = from_side[field], from_pair[field]
+            first = jnp.where(of_pair, pair, side)
+            second = pltpu.roll(jnp.where(of_pair, side, pair), 2, 0)
             return jnp.concatenate([scale_y[0] * first, scale_y[1] * second], axis=0)
 
         def from_z(field):
@@ -629,10 +633,12 @@
     values = observed.transpose(0, 2, 1)
     tensor = receiver_index.reshape(1, -1)
     bins, marks = bin_ids.T, window.T
-    src, y_lo, y_hi, to_core, to_cross, stats, scales = pack(
+    src, to_side, to_pair, to_core, to_cross, stats, scales = pack(
         src, ids, table, values, tensor, bins, marks
     )
-    yb, ya = shift(y_hi, GY, 1), shift(y_lo, GY, -1)
+    count = math.prod(SIZES[a] for a in GY)
+    ring = [(i, (i + 1 if i % 2 else i - 1) % count) for i in range(count)]
+    from_side, from_pair = lax.ppermute(to_side, GY, ring), swap(to_pair, "xlo")
     from_core = swap(to_core, "core")
     x_lo, x_hi, to_cross = strike_faces(src, to_cross, from_core)
     xb, xa = shift(x_hi, GX, 1), shift(x_lo, GX, -1)
@@ -640,7 +646,7 @@
 
     strain, receiver = within(scales, src.reshape(FIELDS * PLANES, LANES), from_core, receiver)
     sums = (stats, from_core, from_cross)
-    keep, send, cells, stats = gram(scales, strain, receiver, (xb, xa, yb, ya), sums)
+    keep, send, cells, stats = gram(scales, strain, receiver, (xb, xa, from_side, from_pair), sums)
     packed = keep + swap(send, "core")
     packed = scatter_sum(packed, PLANE)
     packed = whole_sum(packed, ("z",))

time: 81.5 us -> 81.3 us (level)
  blocking collectives: 38.4 us -> 35.5 us
  waiting for transfers between devices: 6.41 us -> 8.93 us
    ppermute x0 -> x1, starting transfers between devices: none -> 4.79 us  [per_device(): lax.ppermute(to_side, GY, ring)]
    ppermute x4 -> x2, starting transfers between devices: 7.67 us -> 2.9 us  [shift(): lax.ppermute(value, axes, [(i, (i + step) % count) for i in range(count)])]
    all_to_all x3, blocking collectives: 38.4 us -> 35.5 us  [exchange(): return lax.all_to_all(value, axes, 0, 0, tiled=True)]
    ppermute x3 -> x4, waiting for transfers between devices: 2.3 us -> 3.6 us  [swap(): return lax.ppermute(value, axis, [(0, 1), (1, 0)])]
    ppermute x1, waiting for transfers between devices: 4.1 us -> 5.33 us  [per_device(): from_cross = lax.ppermute(to_cross, GZ, [(i, 3 - i) for i in range(4)])]
    ppermute x3 -> x4, starting transfers between devices: 7.94 us -> 8.27 us  [swap(): return lax.ppermute(value, axis, [(0, 1), (1, 0)])]
  transfers between devices with their start and end apart: 8 -> 8, of which waited for: 3 -> 4; matrix products, arithmetic and copies ran while one was open for 0% -> 0% of each run, Pallas kernels for 6% -> 6%
where the time goes in v11:
time: 81.3 us; the launch traced here: 81 us
  blocking collectives  35.5 us (44%)
  starting transfers between devices  19.1 us (23%)
  Pallas kernels  16.7 us (21%)
  waiting for transfers between devices  8.93 us (11%)
    all_to_all x3, blocking collectives, exchange(): return lax.all_to_all(value, axes, 0, 0, tiled=True)  35.5 us
    ppermute x4, starting transfers between devices, swap(): return lax.ppermute(value, axis, [(0, 1), (1, 0)])  8.27 us
    pallas_call x1, Pallas kernels, gram(): pl.pallas_call(gram_kernel, out_shape=(half, half, jax.ShapeDtypeStruct((...  5.84 us
    ppermute x1, waiting for transfers between devices, per_device(): from_cross = lax.ppermute(to_cross, GZ, [(i, 3 - i) for i in range(4)])  5.33 us
    pallas_call x1, Pallas kernels, within(): pl.pallas_call(within_kernel, out_shape=(jax.ShapeDtypeStruct((BINS * 12...  5.08 us
    ppermute x1, starting transfers between devices, per_device(): lax.ppermute(to_side, GY, ring)  4.79 us
    ppermute x4, waiting for transfers between devices, swap(): return lax.ppermute(value, axis, [(0, 1), (1, 0)])  3.6 us
    ppermute x1, starting transfers between devices, per_device(): from_cross = lax.ppermute(to_cross, GZ, [(i, 3 - i) for i in range(4)])  3.11 us
  transfers between devices with their start and end apart: 8, of which 4 were waited for; matrix products, arithmetic and copies ran while one was open for 0% of the time, Pallas kernels for 6%

profile of v11, /device:TPU:1, one launch (start us, length us, event | category | flops | bytes accessed | tf_op | source)
XLA Modules:
  0.0 81.0 jit_solution(10718181146725477144)
XLA Ops:
  0.6 2.7 %pack.1 = (f32[96,16,128]{2,1,0:T(8,128)S(1)}, f32[96,8,128]{2,1,0:T(8,128)S(1)}, f32[96,8,128]{2,1,0:T(8,128)S(1)}, f32[32,128]{1,0:T(8,128)S(1)}, f32[32,128]{...) custom-call(f32[96,16,128]{2,1,0:T(8,128)} %bitcast.26, s32[16,128]{1,0:T(8,128)} %bitcast.28, ...), custom_call_target="tpu_custom_call" | custom-call | tf_op jit(solution)/shard_map/pack/pallas_call | solution.py:203
  3.4 3.3 %collective-permute-start = (f32[32,128]{1,0:T(8,128)S(1)}, f32[32,128]{1,0:T(8,128)S(1)}, u32[]{:S(2)}, u32[]{:S(2)}) collective-permute-start(f32[32,128]{1,0:T(8,128)S(1)} %get-tuple-element.24), channel_id=1, source_target_pairs={{0,1},{1,0},{2,3},{3,2},{4,5},{5,4},{6,7},{7,6},{8,9},{9,8},{10,11... | collective-permute-start | bytes 49160 | tf_op jit(solution)/shard_map/ppermute | solution.py:597
  6.7 4.8 %collective-permute-start.3 = (f32[96,8,128]{2,1,0:T(8,128)S(1)}, f32[96,8,128]{2,1,0:T(8,128)S(1)}, u32[]{:S(2)}, u32[]{:S(2)}) collective-permute-start(f32[96,8,128]{2,1,0:T(8,128)S(1)} %get-tuple-element.30), channel_id=1, source_target_pairs={{0,60},{4,8},{8,4},{12,16},{16,12},{20,24},{24,20},{28,32},{32,28}... | collective-permute-start | bytes 1179656 | tf_op jit(solution)/shard_map/ppermute | solution.py:641
  11.5 0.0 collective-permute-start.4
  11.5 0.0 collective-permute-done.from_core
  11.5 0.1 strike_faces.1
  11.6 1.4 %collective-permute-start.1 = (f32[96,8,128]{2,1,0:T(8,128)S(1)}, f32[96,8,128]{2,1,0:T(8,128)S(1)}, u32[]{:S(2)}, u32[]{:S(2)}) collective-permute-start(f32[96,8,128]{2,1,0:T(8,128)S(1)} %get-tuple-element.28), channel_id=1, source_target_pairs={{0,64},{64,128},{128,192},{192,0},{1,65},{65,129},{129,193},{193,1... | collective-permute-start | bytes 1179656 | tf_op jit(solution)/shard_map/ppermute | solution.py:593
  13.0 1.5 %collective-permute-start.2 = (f32[96,8,128]{2,1,0:T(8,128)S(1)}, f32[96,8,128]{2,1,0:T(8,128)S(1)}, u32[]{:S(2)}, u32[]{:S(2)}) collective-permute-start(f32[96,8,128]{2,1,0:T(8,128)S(1)} %get-tuple-element.29), channel_id=1, source_target_pairs={{0,192},{64,0},{128,64},{192,128},{1,193},{65,1},{129,65},{193,129... | collective-permute-start | bytes 1179656 | tf_op jit(solution)/shard_map/ppermute | solution.py:593
  14.5 3.1 %collective-permute-start.5 = (f32[40,128]{1,0:T(8,128)S(1)}, f32[40,128]{1,0:T(8,128)S(1)}, u32[]{:S(2)}, u32[]{:S(2)}) collective-permute-start(f32[40,128]{1,0:T(8,128)S(1)} %get-tuple-element.33), channel_id=1, source_target_pairs={{0,3},{1,2},{2,1},{3,0},{4,7},{5,6},{6,5},{7,4},{8,11},{9,10},{10,... | collective-permute-start | bytes 61448 | tf_op jit(solution)/shard_map/ppermute | solution.py:645
  17.6 5.1 %within.1 = (f32[3072,128]{1,0:T(8,128)S(1)}, f32[12,16,12,16,128]{4,3,2,1,0:T(8,128)S(1)}) custom-call(f32[48,128]{1,0:T(8,128)S(1)} %get-tuple-element.22.scales, f32[1536,128]{1,0:T(8,128)S(1)} %bitcast.14, f32[32,128]{1,0:T(8,128)S(1)} %collective-permute-done.from_core, bf16[12,16,12,16,128]{4,3,2,1,0:T(8,128)(2,1)} %bitcast.25), custom_call_target="tpu_custom_call" | custom-call | flops 4000000 | bytes 14000000 | tf_op jit(solution)/shard_map/within/pallas_call | solution.py:321
  22.7 5.3 %collective-permute-done.5.from_cross = f32[40,128]{1,0:T(8,128)S(1)} collective-permute-done((f32[40,128]{1,0:T(8,128)S(1)}, f32[40,128]{1,0:T(8,128)S(1)}, u32[]{:S(2)}, u32[]{:S(2)}) %collective-permute-start.5) | collective-permute-done | bytes 20512 | tf_op jit(solution)/shard_map/ppermute | solution.py:645
  28.0 1.5 %collective-permute-done.4.from_pair = f32[96,8,128]{2,1,0:T(8,128)S(1)} collective-permute-done((f32[96,8,128]{2,1,0:T(8,128)S(1)}, f32[96,8,128]{2,1,0:T(8,128)S(1)}, u32[]{:S(2)}, u32[]{:S(2)}) %collective-permute-start.4) | collective-permute-done | bytes 393248 | tf_op jit(solution)/shard_map/ppermute | solution.py:597
  29.5 0.0 copy-start.1
  29.5 0.0 copy-start.2
  29.5 0.0 copy-start.3
  29.5 5.8 %gram.1 = (f32[384,128]{1,0:T(8,128)S(1)}, f32[384,128]{1,0:T(8,128)S(1)}, f32[6144,128]{1,0:T(8,128)S(1)}, f32[8,384]{1,0:T(8,128)S(1)}) custom-call(f32[48,128]{1,0:T(8,128)S(1)} %get-tuple-element.22.scales, f32[3072,128]{1,0:T(8,128)S(1)} %get-tuple-element.25.within, f32[12,16,12,16,128]{4,3,2,1,0:T(8,128)S(1)} %get-tuple-element.26.receiver, ...), custom_call_target="tpu_custom_call" | custom-call | flops 1200000000 | bytes 8000000 | tf_op jit(solution)/shard_map/gram/pallas_call | solution.py:436
  35.4 0.6 collective-permute-start.6
  36.0 1.1 %collective-permute-done.6 = f32[384,128]{1,0:T(8,128)S(1)} collective-permute-done((f32[384,128]{1,0:T(8,128)S(1)}, f32[384,128]{1,0:T(8,128)S(1)}, u32[]{:S(2)}, u32[]{:S(2)}) %collective-permute-start.6) | collective-permute-done | bytes 196640 | tf_op jit(solution)/shard_map/ppermute | solution.py:597
  37.1 13.7 %all_to_all.15 = f32[16,24,128]{2,1,0:T(8,128)S(1)} all-to-all(f32[16,24,128]{2,1,0:T(8,128)S(1)} %bitcast.27), channel_id=1, replica_groups=mesh['y'=4,'z'=8,'xlo'=2,'xhi'=2,'core'=2] {'y','xlo','xhi'}, dimensions={0} | all-to-all | bytes 393216 | tf_op jit(solution)/shard_map/all_to_all | solution.py:601
  50.9 11.6 %all_to_all.16 = f32[8,24,128]{2,1,0:T(8,128)S(1)} all-to-all(f32[8,24,128]{2,1,0:T(8,128)S(1)} %broadcast_in_dim.6), channel_id=1, replica_groups=mesh['y'=4,'z'=8,'xlo'=2,'xhi'=2,'core'=2] {'z'}, dimensions={0} | all-to-all | bytes 196608 | tf_op jit(solution)/shard_map/all_to_all | solution.py:601
  62.6 10.1 %all_to_all.17 = f32[16,24,128]{2,1,0:T(8,128)S(1)} all-to-all(f32[16,24,128]{2,1,0:T(8,128)S(1)} %broadcast_in_dim.7), channel_id=1, replica_groups=mesh['y'=4,'z'=8,'xlo'=2,'xhi'=2,'core'=2] {'y','xlo','xhi'}, dimensions={0} | all-to-all | bytes 393216 | tf_op jit(solution)/shard_map/all_to_all | solution.py:601
  72.7 4.3 %collective-permute-start.7 = (f32[384,128]{1,0:T(8,128)S(1)}, f32[384,128]{1,0:T(8,128)S(1)}, u32[]{:S(2)}, u32[]{:S(2)}) collective-permute-start(f32[384,128]{1,0:T(8,128)S(1)} %bitcast.15), channel_id=1, source_target_pairs={{0,1},{1,0},{2,3},{3,2},{4,5},{5,4},{6,7},{7,6},{8,9},{9,8},{10,11... | collective-permute-start | bytes 589832 | tf_op jit(solution)/shard_map/ppermute | solution.py:597
  77.0 1.1 %collective-permute-done.7.other = f32[384,128]{1,0:T(8,128)S(1)} collective-permute-done((f32[384,128]{1,0:T(8,128)S(1)}, f32[384,128]{1,0:T(8,128)S(1)}, u32[]{:S(2)}, u32[]{:S(2)}) %collective-permute-start.7) | collective-permute-done | bytes 196640 | tf_op jit(solution)/shard_map/ppermute | solution.py:597
  78.1 2.9 %chain.1 = (f32[16,128]{1,0:T(8,128)}, f32[16,128]{1,0:T(8,128)}, f32[2,16,96]{2,1,0:T(8,128)}) custom-call(f32[384,128]{1,0:T(8,128)S(1)} %bitcast.16, f32[384,128]{1,0:T(8,128)S(1)} %collective-permute-done.7.other, f32[8,384]{1,0:T(8,128)S(1)} %get-tuple-element.36.stats, f32[6144,128]{1,0:T(8,128)S(1)} %get-tuple-element.37.cells, ...), custom_call_target="tpu_custom_call" | custom-call | tf_op jit(solution)/shard_map/chain/pallas_call | solution.py:578
  (13 shorter events, 0.1 us)
Async XLA Ops:
  3.4 8.1 %collective-permute-start = (f32[32,128]{1,0:T(8,128)S(1)}, f32[32,128]{1,0:T(8,128)S(1)}, u32[]{:S(2)}, u32[]{:S(2)}) collective-permute-start(f32[32,128]{1,0:T(8,128)S(1)} %get-tuple-element.24), channel_id=1, source_target_pairs={{0,1},{1,0},{2,3},{3,2},{4,5},{5,4},{6,7},{7,6},{8,9},{9,8},{10,11... | collective-permute-start | bytes 49160 | tf_op jit(solution)/shard_map/ppermute | solution.py:597
  6.7 21.3 %collective-permute-start.3 = (f32[96,8,128]{2,1,0:T(8,128)S(1)}, f32[96,8,128]{2,1,0:T(8,128)S(1)}, u32[]{:S(2)}, u32[]{:S(2)}) collective-permute-start(f32[96,8,128]{2,1,0:T(8,128)S(1)} %get-tuple-element.30), channel_id=1, source_target_pairs={{0,60},{4,8},{8,4},{12,16},{16,12},{20,24},{24,20},{28,32},{32,28}... | collective-permute-start | bytes 1179656 | tf_op jit(solution)/shard_map/ppermute | solution.py:641
  11.5 18.0 %collective-permute-start.4 = (f32[96,8,128]{2,1,0:T(8,128)S(1)}, f32[96,8,128]{2,1,0:T(8,128)S(1)}, u32[]{:S(2)}, u32[]{:S(2)}) collective-permute-start(f32[96,8,128]{2,1,0:T(8,128)S(1)} %get-tuple-element.31), channel_id=1, source_target_pairs={{0,4},{4,0},{1,5},{5,1},{2,6},{6,2},{3,7},{7,3},{8,12},{12,8},{9,1... | collective-permute-start | bytes 1179656 | tf_op jit(solution)/shard_map/ppermute | solution.py:597
  11.6 17.9 %collective-permute-start.1 = (f32[96,8,128]{2,1,0:T(8,128)S(1)}, f32[96,8,128]{2,1,0:T(8,128)S(1)}, u32[]{:S(2)}, u32[]{:S(2)}) collective-permute-start(f32[96,8,128]{2,1,0:T(8,128)S(1)} %get-tuple-element.28), channel_id=1, source_target_pairs={{0,64},{64,128},{128,192},{192,0},{1,65},{65,129},{129,193},{193,1... | collective-permute-start | bytes 1179656 | tf_op jit(solution)/shard_map/ppermute | solution.py:593
  13.0 16.5 %collective-permute-start.2 = (f32[96,8,128]{2,1,0:T(8,128)S(1)}, f32[96,8,128]{2,1,0:T(8,128)S(1)}, u32[]{:S(2)}, u32[]{:S(2)}) collective-permute-start(f32[96,8,128]{2,1,0:T(8,128)S(1)} %get-tuple-element.29), channel_id=1, source_target_pairs={{0,192},{64,0},{128,64},{192,128},{1,193},{65,1},{129,65},{193,129... | collective-permute-start | bytes 1179656 | tf_op jit(solution)/shard_map/ppermute | solution.py:593
  14.5 13.5 %collective-permute-start.5 = (f32[40,128]{1,0:T(8,128)S(1)}, f32[40,128]{1,0:T(8,128)S(1)}, u32[]{:S(2)}, u32[]{:S(2)}) collective-permute-start(f32[40,128]{1,0:T(8,128)S(1)} %get-tuple-element.33), channel_id=1, source_target_pairs={{0,3},{1,2},{2,1},{3,0},{4,7},{5,6},{6,5},{7,4},{8,11},{9,10},{10,... | collective-permute-start | bytes 61448 | tf_op jit(solution)/shard_map/ppermute | solution.py:645
  29.5 48.6 %copy-start = (f32[2,96,16]{1,2,0:T(8,128)S(1)}, f32[2,96,16]{1,2,0:T(8,128)}, u32[]{:S(2)}) copy-start(f32[2,96,16]{1,2,0:T(8,128)} %param.12) | copy-start | bytes 36868
  29.5 48.6 %copy-start.1 = (s32[96,16]{0,1:T(8,128)S(1)}, s32[96,16]{0,1:T(8,128)}, u32[]{:S(2)}) copy-start(s32[96,16]{0,1:T(8,128)} %param.14) | copy-start | bytes 18436
  29.5 48.6 %copy-start.2 = (s32[96,16]{0,1:T(8,128)S(1)}, s32[96,16]{0,1:T(8,128)}, u32[]{:S(2)}) copy-start(s32[96,16]{0,1:T(8,128)} %param.15) | copy-start | bytes 18436
  29.5 48.6 %copy-start.3 = (s32[96]{0:T(128)S(1)}, s32[96]{0:T(128)}, u32[]{:S(2)}) copy-start(s32[96]{0:T(128)} %param.13) | copy-start | bytes 1156
  35.4 1.7 %collective-permute-start.6 = (f32[384,128]{1,0:T(8,128)S(1)}, f32[384,128]{1,0:T(8,128)S(1)}, u32[]{:S(2)}, u32[]{:S(2)}) collective-permute-start(f32[384,128]{1,0:T(8,128)S(1)} %get-tuple-element.35), channel_id=1, source_target_pairs={{0,1},{1,0},{2,3},{3,2},{4,5},{5,4},{6,7},{7,6},{8,9},{9,8},{10,11... | collective-permute-start | bytes 589832 | tf_op jit(solution)/shard_map/ppermute | solution.py:597
  72.7 5.4 %collective-permute-start.7 = (f32[384,128]{1,0:T(8,128)S(1)}, f32[384,128]{1,0:T(8,128)S(1)}, u32[]{:S(2)}, u32[]{:S(2)}) collective-permute-start(f32[384,128]{1,0:T(8,128)S(1)} %bitcast.15), channel_id=1, source_target_pairs={{0,1},{1,0},{2,3},{3,2},{4,5},{5,4},{6,7},{7,6},{8,9},{9,8},{10,11... | collective-permute-start | bytes 589832 | tf_op jit(solution)/shard_map/ppermute | solution.py:597

commit v12 on v11

--- a/solution.py
+++ b/solution.py
@@ -18,7 +18,7 @@
 GX = ("y",)
 GY = ("z", "xlo")
 GZ = ("xhi", "core")
-PLANE = ("y", "xlo", "xhi")
+PLANE = ("xlo", "xhi", "y")
 VMEM_LIMIT = 16 * 1024 * 1024
 
 BINS = 16
@@ -158,15 +158,15 @@
     to_pair[...] = jnp.where(odd, lower, higher)
 
     lane = lane_ids((FIELDS, LANES))
-    low = jnp.zeros((FIELDS, LANES), F32)
-    high = jnp.zeros((FIELDS, LANES), F32)
+    ends = lane_ids((1, LANES))
+    ends = jnp.where((ends < 2) | (ends >= LANES - 2), 1.0, 0.0).astype(F32)
+    packed = jnp.zeros((FIELDS, LANES), F32)
     for plane in range(PLANES):
-        value = src[:, plane, :]
-        turned = pltpu.roll(value, 8 * plane, 1) if plane else value
-        place = (lane - 8 * plane) & (LANES - 1)
-        low = jnp.where(place < 2, turned, low)
-        high = jnp.where(place >= LANES - 2, turned, high)
+        value = src[:, plane, :] * ends
+        packed = packed + (pltpu.roll(value, 8 * plane, 1) if plane else value)
     place = lane & 7
+    low = jnp.where(place < 2, packed, 0.0)
+    high = jnp.where(place >= 6, packed, 0.0)
     low = jnp.where(place == 1, 8.0 * pltpu.roll(low, 1, 1), 0.0) - low
     high = high - jnp.where(place == 6, 8.0 * pltpu.roll(high, LANES - 1, 1), 0.0)
     high = pltpu.roll(high, 2, 1)

time: 81.3 us -> 81.1 us (level)
  no operation moved by 1% of the time
where the time goes in v12:
time: 81.1 us; the launch traced here: 80.8 us
  blocking collectives  35.4 us (44%)
  starting transfers between devices  19.1 us (24%)
  Pallas kernels  16.6 us (20%)
  waiting for transfers between devices  8.93 us (11%)
    all_to_all x3, blocking collectives, exchange(): return lax.all_to_all(value, axes, 0, 0, tiled=True)  35.4 us
    ppermute x4, starting transfers between devices, swap(): return lax.ppermute(value, axis, [(0, 1), (1, 0)])  8.27 us
    pallas_call x1, Pallas kernels, gram(): pl.pallas_call(gram_kernel, out_shape=(half, half, jax.ShapeDtypeStruct((...  5.84 us
    ppermute x1, waiting for transfers between devices, per_device(): from_cross = lax.ppermute(to_cross, GZ, [(i, 3 - i) for i in range(4)])  5.33 us
    pallas_call x1, Pallas kernels, within(): pl.pallas_call(within_kernel, out_shape=(jax.ShapeDtypeStruct((BINS * 12...  5.08 us
    ppermute x1, starting transfers between devices, per_device(): lax.ppermute(to_side, GY, ring)  4.79 us
    ppermute x4, waiting for transfers between devices, swap(): return lax.ppermute(value, axis, [(0, 1), (1, 0)])  3.6 us
    ppermute x1, starting transfers between devices, per_device(): from_cross = lax.ppermute(to_cross, GZ, [(i, 3 - i) for i in range(4)])  3.11 us
  transfers between devices with their start and end apart: 8, of which 4 were waited for; matrix products, arithmetic and copies ran while one was open for 0% of the time, Pallas kernels for 6%

profile of v12, /device:TPU:1, one launch (start us, length us, event | category | flops | bytes accessed | tf_op | source)
XLA Modules:
  0.0 80.8 jit_solution(10831012853704567497)
XLA Ops:
  0.6 2.7 %pack.1 = (f32[96,16,128]{2,1,0:T(8,128)S(1)}, f32[96,8,128]{2,1,0:T(8,128)S(1)}, f32[96,8,128]{2,1,0:T(8,128)S(1)}, f32[32,128]{1,0:T(8,128)S(1)}, f32[32,128]{...) custom-call(f32[96,16,128]{2,1,0:T(8,128)} %bitcast.26, s32[16,128]{1,0:T(8,128)} %bitcast.28, ...), custom_call_target="tpu_custom_call" | custom-call | tf_op jit(solution)/shard_map/pack/pallas_call | solution.py:203
  3.3 3.3 %collective-permute-start = (f32[32,128]{1,0:T(8,128)S(1)}, f32[32,128]{1,0:T(8,128)S(1)}, u32[]{:S(2)}, u32[]{:S(2)}) collective-permute-start(f32[32,128]{1,0:T(8,128)S(1)} %get-tuple-element.24), channel_id=1, source_target_pairs={{0,1},{1,0},{2,3},{3,2},{4,5},{5,4},{6,7},{7,6},{8,9},{9,8},{10,11... | collective-permute-start | bytes 49160 | tf_op jit(solution)/shard_map/ppermute | solution.py:597
  6.6 4.8 %collective-permute-start.3 = (f32[96,8,128]{2,1,0:T(8,128)S(1)}, f32[96,8,128]{2,1,0:T(8,128)S(1)}, u32[]{:S(2)}, u32[]{:S(2)}) collective-permute-start(f32[96,8,128]{2,1,0:T(8,128)S(1)} %get-tuple-element.30), channel_id=1, source_target_pairs={{0,60},{4,8},{8,4},{12,16},{16,12},{20,24},{24,20},{28,32},{32,28}... | collective-permute-start | bytes 1179656 | tf_op jit(solution)/shard_map/ppermute | solution.py:641
  11.4 0.0 collective-permute-start.4
  11.4 0.0 collective-permute-done.from_core
  11.4 0.1 strike_faces.1
  11.5 1.4 %collective-permute-start.1 = (f32[96,8,128]{2,1,0:T(8,128)S(1)}, f32[96,8,128]{2,1,0:T(8,128)S(1)}, u32[]{:S(2)}, u32[]{:S(2)}) collective-permute-start(f32[96,8,128]{2,1,0:T(8,128)S(1)} %get-tuple-element.28), channel_id=1, source_target_pairs={{0,64},{64,128},{128,192},{192,0},{1,65},{65,129},{129,193},{193,1... | collective-permute-start | bytes 1179656 | tf_op jit(solution)/shard_map/ppermute | solution.py:593
  12.9 1.5 %collective-permute-start.2 = (f32[96,8,128]{2,1,0:T(8,128)S(1)}, f32[96,8,128]{2,1,0:T(8,128)S(1)}, u32[]{:S(2)}, u32[]{:S(2)}) collective-permute-start(f32[96,8,128]{2,1,0:T(8,128)S(1)} %get-tuple-element.29), channel_id=1, source_target_pairs={{0,192},{64,0},{128,64},{192,128},{1,193},{65,1},{129,65},{193,129... | collective-permute-start | bytes 1179656 | tf_op jit(solution)/shard_map/ppermute | solution.py:593
  14.4 3.1 %collective-permute-start.5 = (f32[40,128]{1,0:T(8,128)S(1)}, f32[40,128]{1,0:T(8,128)S(1)}, u32[]{:S(2)}, u32[]{:S(2)}) collective-permute-start(f32[40,128]{1,0:T(8,128)S(1)} %get-tuple-element.33), channel_id=1, source_target_pairs={{0,3},{1,2},{2,1},{3,0},{4,7},{5,6},{6,5},{7,4},{8,11},{9,10},{10,... | collective-permute-start | bytes 61448 | tf_op jit(solution)/shard_map/ppermute | solution.py:645
  17.6 5.1 %within.1 = (f32[3072,128]{1,0:T(8,128)S(1)}, f32[12,16,12,16,128]{4,3,2,1,0:T(8,128)S(1)}) custom-call(f32[48,128]{1,0:T(8,128)S(1)} %get-tuple-element.22.scales, f32[1536,128]{1,0:T(8,128)S(1)} %bitcast.14, f32[32,128]{1,0:T(8,128)S(1)} %collective-permute-done.from_core, bf16[12,16,12,16,128]{4,3,2,1,0:T(8,128)(2,1)} %bitcast.25), custom_call_target="tpu_custom_call" | custom-call | flops 4000000 | bytes 14000000 | tf_op jit(solution)/shard_map/within/pallas_call | solution.py:321
  22.6 5.3 %collective-permute-done.5.from_cross = f32[40,128]{1,0:T(8,128)S(1)} collective-permute-done((f32[40,128]{1,0:T(8,128)S(1)}, f32[40,128]{1,0:T(8,128)S(1)}, u32[]{:S(2)}, u32[]{:S(2)}) %collective-permute-start.5) | collective-permute-done | bytes 20512 | tf_op jit(solution)/shard_map/ppermute | solution.py:645
  28.0 1.5 %collective-permute-done.4.from_pair = f32[96,8,128]{2,1,0:T(8,128)S(1)} collective-permute-done((f32[96,8,128]{2,1,0:T(8,128)S(1)}, f32[96,8,128]{2,1,0:T(8,128)S(1)}, u32[]{:S(2)}, u32[]{:S(2)}) %collective-permute-start.4) | collective-permute-done | bytes 393248 | tf_op jit(solution)/shard_map/ppermute | solution.py:597
  29.4 0.0 copy-start.1
  29.5 0.0 copy-start.2
  29.5 0.0 copy-start.3
  29.5 5.8 %gram.1 = (f32[384,128]{1,0:T(8,128)S(1)}, f32[384,128]{1,0:T(8,128)S(1)}, f32[6144,128]{1,0:T(8,128)S(1)}, f32[8,384]{1,0:T(8,128)S(1)}) custom-call(f32[48,128]{1,0:T(8,128)S(1)} %get-tuple-element.22.scales, f32[3072,128]{1,0:T(8,128)S(1)} %get-tuple-element.25.within, f32[12,16,12,16,128]{4,3,2,1,0:T(8,128)S(1)} %get-tuple-element.26.receiver, ...), custom_call_target="tpu_custom_call" | custom-call | flops 1200000000 | bytes 8000000 | tf_op jit(solution)/shard_map/gram/pallas_call | solution.py:436
  35.3 0.6 collective-permute-start.6
  36.0 1.1 %collective-permute-done.6 = f32[384,128]{1,0:T(8,128)S(1)} collective-permute-done((f32[384,128]{1,0:T(8,128)S(1)}, f32[384,128]{1,0:T(8,128)S(1)}, u32[]{:S(2)}, u32[]{:S(2)}) %collective-permute-start.6) | collective-permute-done | bytes 196640 | tf_op jit(solution)/shard_map/ppermute | solution.py:597
  37.1 13.6 %all_to_all.15 = f32[16,24,128]{2,1,0:T(8,128)S(1)} all-to-all(f32[16,24,128]{2,1,0:T(8,128)S(1)} %bitcast.27), channel_id=1, replica_groups=mesh['y'=4,'z'=8,'xlo'=2,'xhi'=2,'core'=2] {'xlo','xhi','y'}, dimensions={0} | all-to-all | bytes 393216 | tf_op jit(solution)/shard_map/all_to_all | solution.py:601
  50.7 11.6 %all_to_all.16 = f32[8,24,128]{2,1,0:T(8,128)S(1)} all-to-all(f32[8,24,128]{2,1,0:T(8,128)S(1)} %broadcast_in_dim.6), channel_id=1, replica_groups=mesh['y'=4,'z'=8,'xlo'=2,'xhi'=2,'core'=2] {'z'}, dimensions={0} | all-to-all | bytes 196608 | tf_op jit(solution)/shard_map/all_to_all | solution.py:601
  62.3 10.1 %all_to_all.17 = f32[16,24,128]{2,1,0:T(8,128)S(1)} all-to-all(f32[16,24,128]{2,1,0:T(8,128)S(1)} %broadcast_in_dim.7), channel_id=1, replica_groups=mesh['y'=4,'z'=8,'xlo'=2,'xhi'=2,'core'=2] {'xlo','xhi','y'}, dimensions={0} | all-to-all | bytes 393216 | tf_op jit(solution)/shard_map/all_to_all | solution.py:601
  72.5 4.3 %collective-permute-start.7 = (f32[384,128]{1,0:T(8,128)S(1)}, f32[384,128]{1,0:T(8,128)S(1)}, u32[]{:S(2)}, u32[]{:S(2)}) collective-permute-start(f32[384,128]{1,0:T(8,128)S(1)} %bitcast.15), channel_id=1, source_target_pairs={{0,1},{1,0},{2,3},{3,2},{4,5},{5,4},{6,7},{7,6},{8,9},{9,8},{10,11... | collective-permute-start | bytes 589832 | tf_op jit(solution)/shard_map/ppermute | solution.py:597
  76.8 1.1 %collective-permute-done.7.other = f32[384,128]{1,0:T(8,128)S(1)} collective-permute-done((f32[384,128]{1,0:T(8,128)S(1)}, f32[384,128]{1,0:T(8,128)S(1)}, u32[]{:S(2)}, u32[]{:S(2)}) %collective-permute-start.7) | collective-permute-done | bytes 196640 | tf_op jit(solution)/shard_map/ppermute | solution.py:597
  77.9 2.9 %chain.1 = (f32[16,128]{1,0:T(8,128)}, f32[16,128]{1,0:T(8,128)}, f32[2,16,96]{2,1,0:T(8,128)}) custom-call(f32[384,128]{1,0:T(8,128)S(1)} %bitcast.16, f32[384,128]{1,0:T(8,128)S(1)} %collective-permute-done.7.other, f32[8,384]{1,0:T(8,128)S(1)} %get-tuple-element.36.stats, f32[6144,128]{1,0:T(8,128)S(1)} %get-tuple-element.37.cells, ...), custom_call_target="tpu_custom_call" | custom-call | tf_op jit(solution)/shard_map/chain/pallas_call | solution.py:578
  (13 shorter events, 0.1 us)
Async XLA Ops:
  3.3 8.1 %collective-permute-start = (f32[32,128]{1,0:T(8,128)S(1)}, f32[32,128]{1,0:T(8,128)S(1)}, u32[]{:S(2)}, u32[]{:S(2)}) collective-permute-start(f32[32,128]{1,0:T(8,128)S(1)} %get-tuple-element.24), channel_id=1, source_target_pairs={{0,1},{1,0},{2,3},{3,2},{4,5},{5,4},{6,7},{7,6},{8,9},{9,8},{10,11... | collective-permute-start | bytes 49160 | tf_op jit(solution)/shard_map/ppermute | solution.py:597
  6.6 21.3 %collective-permute-start.3 = (f32[96,8,128]{2,1,0:T(8,128)S(1)}, f32[96,8,128]{2,1,0:T(8,128)S(1)}, u32[]{:S(2)}, u32[]{:S(2)}) collective-permute-start(f32[96,8,128]{2,1,0:T(8,128)S(1)} %get-tuple-element.30), channel_id=1, source_target_pairs={{0,60},{4,8},{8,4},{12,16},{16,12},{20,24},{24,20},{28,32},{32,28}... | collective-permute-start | bytes 1179656 | tf_op jit(solution)/shard_map/ppermute | solution.py:641
  11.4 18.0 %collective-permute-start.4 = (f32[96,8,128]{2,1,0:T(8,128)S(1)}, f32[96,8,128]{2,1,0:T(8,128)S(1)}, u32[]{:S(2)}, u32[]{:S(2)}) collective-permute-start(f32[96,8,128]{2,1,0:T(8,128)S(1)} %get-tuple-element.31), channel_id=1, source_target_pairs={{0,4},{4,0},{1,5},{5,1},{2,6},{6,2},{3,7},{7,3},{8,12},{12,8},{9,1... | collective-permute-start | bytes 1179656 | tf_op jit(solution)/shard_map/ppermute | solution.py:597
  11.5 17.9 %collective-permute-start.1 = (f32[96,8,128]{2,1,0:T(8,128)S(1)}, f32[96,8,128]{2,1,0:T(8,128)S(1)}, u32[]{:S(2)}, u32[]{:S(2)}) collective-permute-start(f32[96,8,128]{2,1,0:T(8,128)S(1)} %get-tuple-element.28), channel_id=1, source_target_pairs={{0,64},{64,128},{128,192},{192,0},{1,65},{65,129},{129,193},{193,1... | collective-permute-start | bytes 1179656 | tf_op jit(solution)/shard_map/ppermute | solution.py:593
  12.9 16.5 %collective-permute-start.2 = (f32[96,8,128]{2,1,0:T(8,128)S(1)}, f32[96,8,128]{2,1,0:T(8,128)S(1)}, u32[]{:S(2)}, u32[]{:S(2)}) collective-permute-start(f32[96,8,128]{2,1,0:T(8,128)S(1)} %get-tuple-element.29), channel_id=1, source_target_pairs={{0,192},{64,0},{128,64},{192,128},{1,193},{65,1},{129,65},{193,129... | collective-permute-start | bytes 1179656 | tf_op jit(solution)/shard_map/ppermute | solution.py:593
  14.4 13.5 %collective-permute-start.5 = (f32[40,128]{1,0:T(8,128)S(1)}, f32[40,128]{1,0:T(8,128)S(1)}, u32[]{:S(2)}, u32[]{:S(2)}) collective-permute-start(f32[40,128]{1,0:T(8,128)S(1)} %get-tuple-element.33), channel_id=1, source_target_pairs={{0,3},{1,2},{2,1},{3,0},{4,7},{5,6},{6,5},{7,4},{8,11},{9,10},{10,... | collective-permute-start | bytes 61448 | tf_op jit(solution)/shard_map/ppermute | solution.py:645
  29.4 48.4 %copy-start = (f32[2,96,16]{1,2,0:T(8,128)S(1)}, f32[2,96,16]{1,2,0:T(8,128)}, u32[]{:S(2)}) copy-start(f32[2,96,16]{1,2,0:T(8,128)} %param.12) | copy-start | bytes 36868
  29.4 48.4 %copy-start.1 = (s32[96,16]{0,1:T(8,128)S(1)}, s32[96,16]{0,1:T(8,128)}, u32[]{:S(2)}) copy-start(s32[96,16]{0,1:T(8,128)} %param.14) | copy-start | bytes 18436
  29.5 48.4 %copy-start.2 = (s32[96,16]{0,1:T(8,128)S(1)}, s32[96,16]{0,1:T(8,128)}, u32[]{:S(2)}) copy-start(s32[96,16]{0,1:T(8,128)} %param.15) | copy-start | bytes 18436
  29.5 48.4 %copy-start.3 = (s32[96]{0:T(128)S(1)}, s32[96]{0:T(128)}, u32[]{:S(2)}) copy-start(s32[96]{0:T(128)} %param.13) | copy-start | bytes 1156
  35.3 1.7 %collective-permute-start.6 = (f32[384,128]{1,0:T(8,128)S(1)}, f32[384,128]{1,0:T(8,128)S(1)}, u32[]{:S(2)}, u32[]{:S(2)}) collective-permute-start(f32[384,128]{1,0:T(8,128)S(1)} %get-tuple-element.35), channel_id=1, source_target_pairs={{0,1},{1,0},{2,3},{3,2},{4,5},{5,4},{6,7},{7,6},{8,9},{9,8},{10,11... | collective-permute-start | bytes 589832 | tf_op jit(solution)/shard_map/ppermute | solution.py:597
  72.5 5.4 %collective-permute-start.7 = (f32[384,128]{1,0:T(8,128)S(1)}, f32[384,128]{1,0:T(8,128)S(1)}, u32[]{:S(2)}, u32[]{:S(2)}) collective-permute-start(f32[384,128]{1,0:T(8,128)S(1)} %bitcast.15), channel_id=1, source_target_pairs={{0,1},{1,0},{2,3},{3,2},{4,5},{5,4},{6,7},{7,6},{8,9},{9,8},{10,11... | collective-permute-start | bytes 589832 | tf_op jit(solution)/shard_map/ppermute | solution.py:597
